TPU v7x, 32 devices: a whole 2x2x4 slice. The times are simulated.
32 devices in a mesh: section: 2 (over core), dp: 8 (over z, x), tensor: 2 (over y).
Axes of the slice: x: 2, y: 2, z: 4, core: 2. Of those that a mesh axis runs over, the one named last changes fastest.
Arguments:
- boundary: bfloat16 [2, 2, 1024, 2048], P('section', None, ('dp', 'tensor')), may hold values from -6 to 6
- doc_lengths: int32 [2, 1, 8], replicated, may hold values from 1 to 960, as said below
- qkv_weight: bfloat16 [2, 2048, 3, 2048], P('section', 'dp', None, 'tensor'), may hold values from -0.125 to 0.125
- qv_bias: bfloat16 [2, 2, 16, 128], P('section', None, 'tensor', 'dp'), may hold values from -3 to 3
- out_weight: bfloat16 [2, 2048, 2048], P('section', 'tensor', 'dp'), may hold values from -1.5 to 1.5
- up_weight: bfloat16 [2, 2048, 8192], P('section', 'dp', 'tensor'), may hold values from -0.125 to 0.125
- up_bias: bfloat16 [2, 64, 128], P('section', 'tensor', 'dp'), may hold values from -3 to 3
- down_weight: bfloat16 [2, 8192, 2048], P('section', 'tensor', 'dp'), may hold values from -0.0625 to 0.0625
- norm_gains: bfloat16 [2, 2, 2048], P('section', None, ('dp', 'tensor')), may hold values from 0.5 to 1.5
- norm_biases: bfloat16 [2, 4, 2048], P('section', None, ('dp', 'tensor')), may hold values from -2 to 2
Outputs:
- acts: bfloat16 [2, 2, 1024, 2048], P('section', None, ('dp', 'tensor'))
- input_grads: float32 [2, 2, 1024, 2048], P('section', None, ('dp', 'tensor'))
- qkv_weight_grad: float32 [2, 2048, 3, 2048], P('section', 'dp', None, 'tensor')
- qv_bias_grad: float32 [2, 2, 16, 128], P('section', None, 'tensor', 'dp')
- out_weight_grad: float32 [2, 2048, 2048], P('section', 'tensor', 'dp')
- up_weight_grad: float32 [2, 2048, 8192], P('section', 'dp', 'tensor')
- up_bias_grad: float32 [2, 64, 128], P('section', 'tensor', 'dp')
- down_weight_grad: float32 [2, 8192, 2048], P('section', 'tensor', 'dp')
- norm_gains_grad: float32 [2, 2, 2048], P('section', None, ('dp', 'tensor'))
- norm_biases_grad: float32 [2, 4, 2048], P('section', None, ('dp', 'tensor'))
Inputs may be any that keep to these rules, and one draw needn't show every extreme that they name: `doc_lengths`: each row lists the 8 documents of a packed sequence in order; one has exactly 960 tokens, the others together 32 to 63 tokens; the tokens after the last document are padding.
All inputs are finite; a program needn't handle non-finite values.
Results may differ from a plain program's by a relative error of at most 0.025.
Values may be sent and summed in bfloat16 or wider, within the bound.
A program may use at most 384 MiB of HBM per device.

v0:
```python
from functools import partial
import math

import jax
import jax.numpy as jnp
from jax import lax
from jax.sharding import PartitionSpec as P

HD = 128


EPSILON = 1e-05
NEG_FILL = -1e30


def from_behind(value, axis, steps):
    count = lax.axis_size(axis)
    first, last = (max(0, -steps), min(count, count - steps))
    return lax.ppermute(value, axis, [(source, source + steps) for source in range(first, last)])


def layer_norm(hidden, gain, shift):
    average = jnp.mean(hidden, axis=-1, keepdims=True)
    centred = hidden - average
    variance = jnp.mean(centred * centred, axis=-1, keepdims=True)
    inverse = lax.rsqrt(variance + EPSILON)
    normed = centred * inverse
    return (normed * gain + shift, normed, inverse)


def norm_back(grad_out, normed, inverse, gain):
    scaled = grad_out * gain
    return inverse * (
        scaled
        - jnp.mean(scaled, axis=-1, keepdims=True)
        - normed * jnp.mean(scaled * normed, axis=-1, keepdims=True)
    )


def visibility(lengths, dp_index, rows_dp, seq_len):
    per_seq = seq_len // lengths.shape[0]
    docs = lengths.shape[1]
    key_pos = jnp.arange(seq_len, dtype=jnp.int32)
    seq_of = key_pos // per_seq
    local = key_pos - seq_of * per_seq
    doc_ends = jnp.cumsum(lengths, axis=1)
    ends_row = jnp.take(doc_ends, seq_of, axis=0)
    key_seg = seq_of * (docs + 1) + jnp.sum((local[:, None] >= ends_row).astype(jnp.int32), axis=1)
    key_live = local < ends_row[:, docs - 1]
    start_row = dp_index * rows_dp
    query_pos = start_row + jnp.arange(rows_dp, dtype=jnp.int32)
    query_seg = lax.dynamic_slice_in_dim(key_seg, start_row, rows_dp)
    query_live = lax.dynamic_slice_in_dim(key_live, start_row, rows_dp)
    return (query_pos, query_seg, query_live, key_pos, key_seg, key_live)


def widen(rows_low):
    return lax.all_gather(rows_low, "tensor", axis=0, tiled=True)


def narrow(partial_rows):
    return lax.psum_scatter(
        partial_rows.astype(jnp.bfloat16), "tensor", scatter_dimension=0, tiled=True
    ).astype(jnp.float32)


def fetch_weights(
    qkv_weight, qv_bias, out_weight, up_weight, up_bias, down_weight, norm_gains, norm_biases
):
    w_qkv, b_qv, w_out, w_up, b_up, w_down = (
        lax.all_gather(qkv_weight[0], "dp", axis=0, tiled=True),
        lax.all_gather(qv_bias[0], "dp", axis=2, tiled=True),
        lax.all_gather(out_weight[0], "dp", axis=1, tiled=True),
        lax.all_gather(up_weight[0], "dp", axis=0, tiled=True),
        lax.all_gather(up_bias[0], "dp", axis=1, tiled=True),
        lax.all_gather(down_weight[0], "dp", axis=1, tiled=True),
    )
    gain_rows, bias_rows = (
        lax.all_gather(norm_gains[0], ("dp", "tensor"), axis=1, tiled=True),
        lax.all_gather(norm_biases[0], ("dp", "tensor"), axis=1, tiled=True),
    )
    return (
        w_qkv,
        b_qv.reshape(2, -1).astype(jnp.float32),
        w_out,
        w_up,
        b_up.reshape(-1).astype(jnp.float32),
        w_down,
        gain_rows.astype(jnp.float32),
        bias_rows.astype(jnp.float32),
    )


def block_scores(q_heads, key_block, kpos_block, kseg_block, sight):
    scores = jnp.einsum(
        "qhd,khd->hqk", q_heads, key_block, preferred_element_type=jnp.float32
    ) * HD ** (-0.5)
    allowed = (
        (sight[1][:, None] == kseg_block[None, :])
        & (kpos_block[None, :] <= sight[0][:, None])
        & sight[2][:, None]
    )
    return (jnp.where(allowed[None], scores, NEG_FILL), allowed)


def key_blocks(keys, values, sight):
    seq_len = keys.shape[0]
    block_rows = math.gcd(seq_len, 512)
    blocks = seq_len // block_rows
    heads = keys.shape[1] // HD
    return (
        keys.reshape(blocks, block_rows, heads, HD),
        values.reshape(blocks, block_rows, heads, HD),
        sight[3].reshape(blocks, block_rows),
        sight[4].reshape(blocks, block_rows),
    )


def attend(queries, keys, values, sight):
    rows = queries.shape[0]
    heads = queries.shape[1] // HD
    q_heads = queries.reshape(rows, heads, HD)
    stacked = key_blocks(keys, values, sight)

    def find_scale(carry, pieces):
        top, total = carry
        scores, allowed = block_scores(q_heads, pieces[0], pieces[2], pieces[3], sight)
        new_top = jnp.maximum(top, jnp.max(scores, axis=-1))
        total = total * jnp.exp(top - new_top) + jnp.sum(
            jnp.exp(scores - new_top[..., None]), axis=-1
        )
        return ((new_top, total), None)

    start = (jnp.full((heads, rows), -jnp.inf, jnp.float32), jnp.zeros((heads, rows), jnp.float32))
    (top, total), ignored = lax.scan(find_scale, start, stacked)
    log_total = top + jnp.log(total)

    def weigh(carry, pieces):
        scores, allowed = block_scores(q_heads, pieces[0], pieces[2], pieces[3], sight)
        probs = jnp.exp(scores - log_total[..., None]).astype(jnp.bfloat16)
        return (
            carry
            + jnp.einsum("hqk,khd->qhd", probs, pieces[1], preferred_element_type=jnp.float32),
            None,
        )

    heads_out, ignored = lax.scan(weigh, jnp.zeros((rows, heads, HD), jnp.float32), stacked)
    return (heads_out, log_total, q_heads)


def attend_back(q_heads, keys, values, sight, log_total, grad_heads, delta):
    seq_len = keys.shape[0]
    stacked = key_blocks(keys, values, sight)
    scaling = HD ** (-0.5)

    def one_step(grad_q, pieces):
        scores, allowed = block_scores(q_heads, pieces[0], pieces[2], pieces[3], sight)
        probs = jnp.exp(scores - log_total[..., None])
        grad_p = jnp.einsum(
            "qhd,khd->hqk", grad_heads, pieces[1], preferred_element_type=jnp.float32
        )
        grad_s = jnp.where(allowed[None], probs * (grad_p - delta[..., None]), 0.0).astype(
            jnp.bfloat16
        )
        grad_q = (
            grad_q
            + jnp.einsum("hqk,khd->qhd", grad_s, pieces[0], preferred_element_type=jnp.float32)
            * scaling
        )
        grad_v = jnp.einsum(
            "hqk,qhd->khd",
            probs.astype(jnp.bfloat16),
            grad_heads,
            preferred_element_type=jnp.float32,
        )
        grad_k = (
            jnp.einsum("hqk,qhd->khd", grad_s, q_heads, preferred_element_type=jnp.float32)
            * scaling
        )
        return (grad_q, (grad_k, grad_v))

    grad_q, outputs = lax.scan(one_step, jnp.zeros(q_heads.shape, jnp.float32), stacked)
    return (grad_q, outputs[0].reshape(seq_len, -1), outputs[1].reshape(seq_len, -1))


def forward(entering, weights, sight):
    w_qkv, b_qv, w_out, w_up, b_up, w_down, gain_rows, bias_rows = weights
    hidden = entering.astype(jnp.float32)
    normed_a, unit_a, inverse_a = layer_norm(hidden, gain_rows[0], bias_rows[0])
    rows_a = widen(normed_a.astype(jnp.bfloat16))
    projected = jnp.einsum("rd,djh->rjh", rows_a, w_qkv, preferred_element_type=jnp.float32)
    queries = (projected[:, 0] + b_qv[0]).astype(jnp.bfloat16)
    keys_own = projected[:, 1].astype(jnp.bfloat16)
    values_own = (projected[:, 2] + b_qv[1]).astype(jnp.bfloat16)
    keys, values = (
        lax.all_gather(keys_own, "dp", axis=0, tiled=True),
        lax.all_gather(values_own, "dp", axis=0, tiled=True),
    )
    heads_out, log_total, q_heads = attend(queries, keys, values, sight)
    live_rows = sight[2].astype(jnp.float32)
    mixed_low = (heads_out.reshape(heads_out.shape[0], -1) * live_rows[:, None]).astype(
        jnp.bfloat16
    )
    middle = (
        hidden
        + narrow(jnp.dot(mixed_low, w_out, preferred_element_type=jnp.float32))
        + bias_rows[1]
    )
    normed_b, unit_b, inverse_b = layer_norm(middle, gain_rows[1], bias_rows[2])
    rows_b = widen(normed_b.astype(jnp.bfloat16))
    preact = jnp.dot(rows_b, w_up, preferred_element_type=jnp.float32) + b_up
    activated = jax.nn.gelu(preact, approximate=False).astype(jnp.bfloat16)
    result = (
        middle
        + narrow(jnp.dot(activated, w_down, preferred_element_type=jnp.float32))
        + bias_rows[3]
    )
    saved = (
        unit_a,
        inverse_a,
        rows_a,
        q_heads,
        keys,
        values,
        heads_out,
        log_total,
        mixed_low,
        unit_b,
        inverse_b,
        rows_b,
        preact,
        activated,
    )
    return (result, saved)


def backward(saved, grad_out, weights, sight):
    w_qkv, b_qv, w_out, w_up, b_up, w_down, gain_rows, bias_rows = weights
    (
        unit_a,
        inverse_a,
        rows_a,
        q_heads,
        keys,
        values,
        heads_out,
        log_total,
        mixed_low,
        unit_b,
        inverse_b,
        rows_b,
        preact,
        activated,
    ) = saved
    rows = rows_a.shape[0]
    grad_branch = grad_out.astype(jnp.bfloat16)
    down_bias_grad = jnp.sum(grad_branch.astype(jnp.float32), axis=0)
    wide_branch = widen(grad_branch)
    grad_act = jnp.einsum("rd,fd->rf", wide_branch, w_down, preferred_element_type=jnp.float32)
    ignored, gelu_pull = jax.vjp(partial(jax.nn.gelu, approximate=False), preact)
    grad_pre = gelu_pull(grad_act)[0].astype(jnp.bfloat16)
    up_bias_grad = jnp.sum(grad_pre.astype(jnp.float32), axis=0)
    grad_normed_b = narrow(
        jnp.einsum("rf,df->rd", grad_pre, w_up, preferred_element_type=jnp.float32)
    )
    gain_b_grad = jnp.sum(grad_normed_b * unit_b, axis=0)
    shift_b_grad = jnp.sum(grad_normed_b, axis=0)
    grad_middle = grad_out + norm_back(grad_normed_b, unit_b, inverse_b, gain_rows[1])
    grad_attn = grad_middle.astype(jnp.bfloat16)
    out_bias_grad = jnp.sum(grad_attn.astype(jnp.float32), axis=0)
    wide_attn = widen(grad_attn)
    live_rows = sight[2].astype(jnp.bfloat16)
    grad_flat = (
        jnp.einsum("rd,ed->re", wide_attn, w_out, preferred_element_type=jnp.float32).astype(
            jnp.bfloat16
        )
        * live_rows[:, None]
    )
    grad_heads = grad_flat.reshape(heads_out.shape)
    delta = jnp.einsum("qhd,qhd->hq", grad_heads.astype(jnp.float32), heads_out)
    grad_q, grad_k_all, grad_v_all = attend_back(
        q_heads, keys, values, sight, log_total, grad_heads, delta
    )
    grad_k, grad_v = (
        lax.psum_scatter(
            grad_k_all.astype(jnp.bfloat16), "dp", scatter_dimension=0, tiled=True
        ).astype(jnp.float32),
        lax.psum_scatter(
            grad_v_all.astype(jnp.bfloat16), "dp", scatter_dimension=0, tiled=True
        ).astype(jnp.float32),
    )
    grad_proj = jnp.stack((grad_q.reshape(rows, -1), grad_k, grad_v), axis=1).astype(jnp.bfloat16)
    proj_sums = jnp.sum(grad_proj.astype(jnp.float32), axis=0)
    qv_grad = jnp.stack((proj_sums[0], proj_sums[2]))
    grad_normed_a = narrow(
        jnp.einsum("rjh,djh->rd", grad_proj, w_qkv, preferred_element_type=jnp.float32)
    )
    gain_a_grad = jnp.sum(grad_normed_a * unit_a, axis=0)
    shift_a_grad = jnp.sum(grad_normed_a, axis=0)
    grad_in = grad_middle + norm_back(grad_normed_a, unit_a, inverse_a, gain_rows[0])
    gains_grad = jnp.stack((gain_a_grad, gain_b_grad))
    biases_grad = jnp.stack((shift_a_grad, out_bias_grad, shift_b_grad, down_bias_grad))
    factors = (rows_b, grad_pre, activated, wide_branch, mixed_low, wide_attn, rows_a, grad_proj)
    vectors = (qv_grad, up_bias_grad, gains_grad, biases_grad)
    return (grad_in, factors, vectors)


def weight_products(factors):
    rows_b, grad_pre, activated, wide_branch, mixed_low, wide_attn, rows_a, grad_proj = factors
    down_grad = jnp.einsum("rf,rd->fd", activated, wide_branch, preferred_element_type=jnp.float32)
    up_grad = jnp.einsum("rd,rf->df", rows_b, grad_pre, preferred_element_type=jnp.float32)
    out_grad = jnp.einsum("re,rd->ed", mixed_low, wide_attn, preferred_element_type=jnp.float32)
    qkv_grad = jnp.einsum("rd,rjh->djh", rows_a, grad_proj, preferred_element_type=jnp.float32)
    return (qkv_grad, out_grad, up_grad, down_grad)


def assemble(products, vectors):
    qkv_grad, out_grad, up_grad, down_grad = products
    qv_grad, up_bias_grad, gains_grad, biases_grad = vectors
    return (qkv_grad, qv_grad, out_grad, up_grad, up_bias_grad, down_grad, gains_grad, biases_grad)


def reduce_grads(local_grads):
    qkv_grad, qv_grad, out_grad, up_grad, up_bias_grad, down_grad, gains_grad, biases_grad = (
        local_grads
    )
    heads = qv_grad.shape[1] // HD
    shards = (
        lax.psum_scatter(
            qkv_grad[None].astype(jnp.bfloat16), "dp", scatter_dimension=1, tiled=True
        ).astype(jnp.float32),
        lax.psum_scatter(
            qv_grad.reshape(1, 2, heads, HD).astype(jnp.bfloat16),
            "dp",
            scatter_dimension=3,
            tiled=True,
        ).astype(jnp.float32),
        lax.psum_scatter(
            out_grad[None].astype(jnp.bfloat16), "dp", scatter_dimension=2, tiled=True
        ).astype(jnp.float32),
        lax.psum_scatter(
            up_grad[None].astype(jnp.bfloat16), "dp", scatter_dimension=1, tiled=True
        ).astype(jnp.float32),
        lax.psum_scatter(
            up_bias_grad.reshape(1, -1, HD).astype(jnp.bfloat16),
            "dp",
            scatter_dimension=2,
            tiled=True,
        ).astype(jnp.float32),
        lax.psum_scatter(
            down_grad[None].astype(jnp.bfloat16), "dp", scatter_dimension=2, tiled=True
        ).astype(jnp.float32),
    )
    vectors = (
        lax.psum_scatter(gains_grad[None], ("dp", "tensor"), scatter_dimension=2, tiled=True),
        lax.psum_scatter(biases_grad[None], ("dp", "tensor"), scatter_dimension=2, tiled=True),
    )
    return tuple(shards) + tuple(vectors)


def body(
    boundary,
    doc_lengths,
    qkv_weight,
    qv_bias,
    out_weight,
    up_weight,
    up_bias,
    down_weight,
    norm_gains,
    norm_biases,
):
    section_index = lax.axis_index("section")
    on_first = section_index == 0
    own_part = boundary[0]
    batches = own_part.shape[0]
    rows_dp = own_part.shape[1] * lax.axis_size("tensor")
    seq_len = rows_dp * lax.axis_size("dp")
    dp_index = lax.axis_index("dp")
    sources = (
        qkv_weight,
        qv_bias,
        out_weight,
        up_weight,
        up_bias,
        down_weight,
        norm_gains,
        norm_biases,
    )
    fixed_weights = fetch_weights(*sources)

    def current():
        return fixed_weights

    def sight_for(batch_at):
        lengths = lax.dynamic_index_in_dim(doc_lengths, batch_at, 0, keepdims=False)
        return visibility(lengths, dp_index, rows_dp, seq_len)

    def pick(first_value, second_value):
        return jnp.where(on_first, first_value, second_value)

    received = jnp.zeros_like(own_part[0])
    kept_ticks, exits = ([], [])
    for tick_index in range(batches + 1):
        entering = jnp.where(on_first, own_part[min(tick_index, batches - 1)], received)
        batch_at = jnp.clip(tick_index - section_index, 0, batches - 1)
        result, saved = forward(entering, current(), sight_for(batch_at))
        leaving = result.astype(jnp.bfloat16)
        kept_ticks.append(saved)
        exits.append(leaving)
        if tick_index < batches:
            received = from_behind(leaving, "section", 1)
    acts = jnp.stack(
        [jnp.where(on_first, exits[number], exits[number + 1]) for number in range(batches)]
    )[None]
    returned = jnp.zeros_like(own_part[0])
    summed = None
    vector_sum = None
    factor_ticks = []
    leaving_grads = []
    for tick_index in range(batches + 1):
        own_grad = own_part[min(tick_index, batches - 1)].astype(jnp.float32)
        if tick_index == batches:
            own_grad = jnp.zeros_like(own_grad)
        grad_out = jnp.where(on_first, returned.astype(jnp.float32), own_grad)
        saved = jax.tree.map(
            pick, kept_ticks[max(tick_index - 1, 0)], kept_ticks[min(tick_index + 1, batches)]
        )
        batch_at = jnp.where(on_first, max(tick_index - 1, 0), min(tick_index, batches - 1))
        grad_in, factors, vectors = backward(saved, grad_out, current(), sight_for(batch_at))
        leaving_grads.append(grad_in)
        if tick_index < batches:
            returned = from_behind(grad_in.astype(jnp.bfloat16), "section", -1)
        factor_ticks.append(factors)
        vector_sum = (
            vectors
            if vector_sum is None
            else tuple((former + latter for former, latter in zip(vector_sum, vectors)))
        )
    joined = tuple(
        (
            jnp.concatenate([entry[number] for entry in factor_ticks], axis=0)
            for number in range(len(factor_ticks[0]))
        )
    )
    summed = reduce_grads(assemble(weight_products(joined), vector_sum))
    input_grads = jnp.stack(
        [
            jnp.where(on_first, leaving_grads[number + 1], leaving_grads[number])
            for number in range(batches)
        ]
    )[None]
    return (acts, input_grads) + tuple(summed)


def solution(mesh):
    placed = (
        P("section", None, ("dp", "tensor"), None),
        P(),
        P("section", "dp", None, "tensor"),
        P("section", None, "tensor", "dp"),
        P("section", "tensor", "dp"),
        P("section", "dp", "tensor"),
        P("section", "tensor", "dp"),
        P("section", "tensor", "dp"),
        P("section", None, ("dp", "tensor")),
        P("section", None, ("dp", "tensor")),
    )
    return jax.shard_map(
        body,
        mesh=mesh,
        in_specs=placed,
        out_specs=(
            P("section", None, ("dp", "tensor"), None),
            P("section", None, ("dp", "tensor"), None),
            P("section", "dp", None, "tensor"),
            P("section", None, "tensor", "dp"),
            P("section", "tensor", "dp"),
            P("section", "dp", "tensor"),
            P("section", "tensor", "dp"),
            P("section", "tensor", "dp"),
            P("section", None, ("dp", "tensor")),
            P("section", None, ("dp", "tensor")),
        ),
        check_vma=False,
    )
```

profile of v0, /device:TPU:0, one launch (start us, length us, event | category | flops | bytes accessed | tf_op | source)
XLA Modules:
  0.0 3173.6 jit_solution(18051411576785191474)
XLA Ops:
  41.6 41.0 %all-gather = bf16[1,2,2048]{2,1,0:T(2,128)(2,1)S(1)} all-gather(bf16[1,2,128]{2,1,0:T(2,128)(2,1)} %param.38), channel_id=2, replica_groups=mesh['section'=2,'dp'=8,'tensor'=2] {'dp','tensor'}, dimensions={2}, use_global_device_ids=true | all-gather | bytes 8704 | tf_op jit(solution)/shard_map/all_gather | solution.py:79
  82.5 36.3 %all-gather.1 = bf16[1,4,2048]{2,1,0:T(4,128)(2,1)S(1)} all-gather(bf16[1,4,128]{2,1,0:T(4,128)(2,1)} %param.39), channel_id=3, replica_groups=mesh['section'=2,'dp'=8,'tensor'=2] {'dp','tensor'}, dimensions={2}, use_global_device_ids=true | all-gather | bytes 17408 | tf_op jit(solution)/shard_map/all_gather | solution.py:80
  127.5 62.2 %all-gather.28.cloned.1.call-done = bf16[1,2048,3,1024]{3,1,2,0:T(8,128)(2,1)} async-done(((bf16[1,256,3,1024]{3,1,2,0:T(8,128)(2,1)}), bf16[1,2048,3,1024]{3,1,2,0:T(8,128)(2,1)}) %all-gather.28.cloned.1.call-update) | async-done | bytes 12582928 | tf_op jit(solution)/shard_map/all_gather | solution.py:71
  202.2 42.5 %all-gather.22.cloned.1.call-done = bf16[1024,1024]{1,0:T(8,128)(2,1)} async-done(((bf16[128,1024]{1,0:T(8,128)(2,1)}), bf16[1024,1024]{1,0:T(8,128)(2,1)}) %all-gather.22.cloned.1.call-update) | async-done | bytes 2097168 | tf_op jit(solution)/shard_map/all_gather | solution.py:197
  248.2 47.0 %all-gather.30.cloned.1.call-done = bf16[1024,1,1024]{2,0,1:T(8,128)(2,1)} async-done(((bf16[128,1,1024]{2,0,1:T(8,128)(2,1)}), bf16[1024,1,1024]{2,0,1:T(8,128)(2,1)}) %all-gather.30.cloned.1.call-update) | async-done | bytes 2097168 | tf_op jit(solution)/shard_map/all_gather | solution.py:196
  315.7 54.9 %all-gather.32.cloned.1.call-done = bf16[1,1024,2048]{2,1,0:T(8,128)(2,1)} async-done(((bf16[1,1024,256]{2,1,0:T(8,128)(2,1)}), bf16[1,1024,2048]{2,1,0:T(8,128)(2,1)}) %all-gather.32.cloned.1.call-update) | async-done | bytes 4194320 | tf_op jit(solution)/shard_map/all_gather | solution.py:73
  418.4 198.7 %all-gather.34.cloned.1.call-done = bf16[1,2048,4096]{2,1,0:T(8,128)(2,1)} async-done(((bf16[1,256,4096]{2,1,0:T(8,128)(2,1)}), bf16[1,2048,4096]{2,1,0:T(8,128)(2,1)}) %all-gather.34.cloned.1.call-update) | async-done | bytes 16777232 | tf_op jit(solution)/shard_map/all_gather | solution.py:74
  628.6 216.8 %all-gather.36.cloned.1.call-done = bf16[1,4096,2048]{2,1,0:T(8,128)(2,1)} async-done(((bf16[1,4096,256]{2,1,0:T(8,128)(2,1)}), bf16[1,4096,2048]{2,1,0:T(8,128)(2,1)}) %all-gather.36.cloned.1.call-update) | async-done | bytes 16777232 | tf_op jit(solution)/shard_map/all_gather | solution.py:76
  894.2 44.4 %all-gather.24.cloned.1.call-done = bf16[1024,1024]{1,0:T(8,128)(2,1)} async-done(((bf16[128,1024]{1,0:T(8,128)(2,1)}), bf16[1024,1024]{1,0:T(8,128)(2,1)}) %all-gather.24.cloned.1.call-update) | async-done | bytes 2097168 | tf_op jit(solution)/shard_map/all_gather | solution.py:197
  942.2 46.8 %all-gather.38.cloned.1.call-done = bf16[1024,1,1024]{2,0,1:T(8,128)(2,1)} async-done(((bf16[128,1,1024]{2,0,1:T(8,128)(2,1)}), bf16[1024,1,1024]{2,0,1:T(8,128)(2,1)}) %all-gather.38.cloned.1.call-update) | async-done | bytes 2097168 | tf_op jit(solution)/shard_map/all_gather | solution.py:196
  1178.6 46.5 %all-gather.40.cloned.1.call-done = bf16[1024,1,1024]{2,0,1:T(8,128)(2,1)} async-done(((bf16[128,1,1024]{2,0,1:T(8,128)(2,1)}), bf16[1024,1,1024]{2,0,1:T(8,128)(2,1)}) %all-gather.40.cloned.1.call-update) | async-done | bytes 2097168 | tf_op jit(solution)/shard_map/all_gather | solution.py:196
  1301.3 58.9 %reduce-scatter.51.cloned.1.call-done = bf16[128,1024]{1,0:T(8,128)(2,1)} async-done(((bf16[1024,1024]{1,0:T(8,128)(2,1)}), bf16[128,1024]{1,0:T(8,128)(2,1)}) %reduce-scatter.51.cloned.1.call-update) | async-done | bytes 262160 | tf_op jit(solution)/shard_map/reduce_scatter | solution.py:288
  1360.2 70.8 %reduce-scatter.49.cloned.1.call-done = bf16[128,1024]{1,0:T(8,128)(2,1)} async-done(((bf16[1024,1024]{1,0:T(8,128)(2,1)}), bf16[128,1024]{1,0:T(8,128)(2,1)}) %reduce-scatter.49.cloned.1.call-update) | async-done | bytes 262160 | tf_op jit(solution)/shard_map/reduce_scatter | solution.py:285
  1577.4 61.6 %reduce-scatter.59.cloned.1.call-done = bf16[128,1024]{1,0:T(8,128)(2,1)} async-done(((bf16[1024,1024]{1,0:T(8,128)(2,1)}), bf16[128,1024]{1,0:T(8,128)(2,1)}) %reduce-scatter.59.cloned.1.call-update) | async-done | bytes 262160 | tf_op jit(solution)/shard_map/reduce_scatter | solution.py:288
  1639.0 70.8 %reduce-scatter.57.cloned.1.call-done = bf16[128,1024]{1,0:T(8,128)(2,1)} async-done(((bf16[1024,1024]{1,0:T(8,128)(2,1)}), bf16[128,1024]{1,0:T(8,128)(2,1)}) %reduce-scatter.57.cloned.1.call-update) | async-done | bytes 262160 | tf_op jit(solution)/shard_map/reduce_scatter | solution.py:285
  1848.3 61.8 %reduce-scatter.67.cloned.1.call-done = bf16[128,1024]{1,0:T(8,128)(2,1)} async-done(((bf16[1024,1024]{1,0:T(8,128)(2,1)}), bf16[128,1024]{1,0:T(8,128)(2,1)}) %reduce-scatter.67.cloned.1.call-update) | async-done | bytes 262160 | tf_op jit(solution)/shard_map/reduce_scatter | solution.py:288
  1910.1 70.8 %reduce-scatter.65.cloned.1.call-done = bf16[128,1024]{1,0:T(8,128)(2,1)} async-done(((bf16[1024,1024]{1,0:T(8,128)(2,1)}), bf16[128,1024]{1,0:T(8,128)(2,1)}) %reduce-scatter.65.cloned.1.call-update) | async-done | bytes 262160 | tf_op jit(solution)/shard_map/reduce_scatter | solution.py:285
  2080.1 54.1 %reduce-scatter.79.cloned.1.call-done = bf16[16,16]{1,0:T(8,128)(2,1)} async-done(((bf16[128,16]{1,0:T(8,128)(2,1)}), bf16[16,16]{1,0:T(8,128)(2,1)}) %reduce-scatter.79.cloned.1.call-update) | async-done | bytes 528
  2138.3 75.6 %reduce-scatter.83.cloned.1.call-done = f32[128,2]{1,0:T(8,128)} async-done(((f32[2048,2]{1,0:T(8,128)}), f32[128,2]{1,0:T(8,128)}) %reduce-scatter.83.cloned.1.call-update) | async-done | bytes 1040
  2215.4 75.6 %reduce-scatter.85.cloned.1.call-done = f32[128,4]{1,0:T(8,128)} async-done(((f32[2048,4]{1,0:T(8,128)}), f32[128,4]{1,0:T(8,128)}) %reduce-scatter.85.cloned.1.call-update) | async-done | bytes 2064
  2292.4 87.4 %reduce-scatter.73.cloned.1.call-done = bf16[1,1024,256]{2,1,0:T(8,128)(2,1)} async-done(((bf16[1,1024,2048]{2,1,0:T(8,128)(2,1)}), bf16[1,1024,256]{2,1,0:T(8,128)(2,1)}) %reduce-scatter.73.cloned.1.call-update) | async-done | bytes 524304 | tf_op jit(solution)/shard_map/reduce_scatter | solution.py:338
  2381.9 209.5 %reduce-scatter.71.cloned.1.call-done = bf16[1,256,3,1024]{3,1,2,0:T(8,128)(2,1)} async-done(((bf16[1,2048,3,1024]{3,1,2,0:T(8,128)(2,1)}), bf16[1,256,3,1024]{3,1,2,0:T(8,128)(2,1)}) %reduce-scatter.71.cloned.1.call-update) | async-done | bytes 1572880 | tf_op jit(solution)/shard_map/reduce_scatter | solution.py:329
  2594.8 282.6 %reduce-scatter.75.cloned.1.call-done = bf16[1,256,4096]{2,1,0:T(8,128)(2,1)} async-done(((bf16[1,2048,4096]{2,1,0:T(8,128)(2,1)}), bf16[1,256,4096]{2,1,0:T(8,128)(2,1)}) %reduce-scatter.75.cloned.1.call-update) | async-done | bytes 2097168 | tf_op jit(solution)/shard_map/reduce_scatter | solution.py:341
  2881.5 281.4 %reduce-scatter.77.cloned.1.call-done = bf16[1,4096,256]{2,1,0:T(8,128)(2,1)} async-done(((bf16[1,4096,2048]{2,1,0:T(8,128)(2,1)}), bf16[1,4096,256]{2,1,0:T(8,128)(2,1)}) %reduce-scatter.77.cloned.1.call-update) | async-done | bytes 2097168 | tf_op jit(solution)/shard_map/reduce_scatter | solution.py:350
  (1043 shorter events, 971.1 us)
Async XLA Ops:
  7.2 182.5 %all-gather.28.cloned.1.call-start = ((), (), s32[]{:S(2)}) async-start(), calls=%async_computation.51 | async-start | bytes 14155776 | tf_op jit(solution)/shard_map/all_gather | solution.py:71
  7.9 236.7 %all-gather.22.cloned.1.call-start = ((), (), s32[]{:S(2)}) async-start(), calls=%async_computation.26 | async-start | bytes 2359296 | tf_op jit(solution)/shard_map/all_gather | solution.py:197
  197.7 172.9 %all-gather.32.cloned.1.call-start = ((), (), s32[]{:S(2)}) async-start(), calls=%async_computation.53 | async-start | bytes 4718592 | tf_op jit(solution)/shard_map/all_gather | solution.py:73
  198.3 208.1 %reduce-scatter.35.cloned.1.call-start = ((), (), s32[]{:S(2)}) async-start(), calls=%async_computation.27 | async-start | bytes 786432 | tf_op jit(solution)/shard_map/reduce_scatter | solution.py:62
  374.4 242.8 %all-gather.34.cloned.1.call-start = ((), (), s32[]{:S(2)}) async-start(), calls=%async_computation.54 | async-start | bytes 18874368 | tf_op jit(solution)/shard_map/all_gather | solution.py:74
  374.9 470.4 %all-gather.36.cloned.1.call-start = ((), (), s32[]{:S(2)}) async-start(), calls=%async_computation.55 | async-start | bytes 18874368 | tf_op jit(solution)/shard_map/all_gather | solution.py:76
  375.7 491.6 %reduce-scatter.37.cloned.1.call-start = ((), (), s32[]{:S(2)}) async-start(), calls=%async_computation.28 | async-start | bytes 786432 | tf_op jit(solution)/shard_map/reduce_scatter | solution.py:62
  890.0 143.0 %reduce-scatter.39.cloned.1.call-start = ((), (), s32[]{:S(2)}) async-start(), calls=%async_computation.30 | async-start | bytes 786432 | tf_op jit(solution)/shard_map/reduce_scatter | solution.py:62
  1126.5 173.6 %reduce-scatter.43.cloned.1.call-start = ((), (), s32[]{:S(2)}) async-start(), calls=%async_computation.33 | async-start | bytes 786432 | tf_op jit(solution)/shard_map/reduce_scatter | solution.py:62
  1293.8 137.1 %reduce-scatter.49.cloned.1.call-start = ((), (), s32[]{:S(2)}) async-start(), calls=%async_computation.36 | async-start | bytes 2359296 | tf_op jit(solution)/shard_map/reduce_scatter | solution.py:285
  1298.7 156.4 %reduce-scatter.53.cloned.1.call-start = ((), (), s32[]{:S(2)}) async-start(), calls=%async_computation.38 | async-start | bytes 786432 | tf_op jit(solution)/shard_map/reduce_scatter | solution.py:62
  1510.8 128.3 %reduce-scatter.59.cloned.1.call-start = ((), (), s32[]{:S(2)}) async-start(), calls=%async_computation.41 | async-start | bytes 2359296 | tf_op jit(solution)/shard_map/reduce_scatter | solution.py:288
  1571.3 138.5 %reduce-scatter.57.cloned.1.call-start = ((), (), s32[]{:S(2)}) async-start(), calls=%async_computation.40 | async-start | bytes 2359296 | tf_op jit(solution)/shard_map/reduce_scatter | solution.py:285
  1576.2 157.3 %reduce-scatter.61.cloned.1.call-start = ((), (), s32[]{:S(2)}) async-start(), calls=%async_computation.42 | async-start | bytes 786432 | tf_op jit(solution)/shard_map/reduce_scatter | solution.py:62
  1778.4 131.7 %reduce-scatter.67.cloned.1.call-start = ((), (), s32[]{:S(2)}) async-start(), calls=%async_computation.45 | async-start | bytes 2359296 | tf_op jit(solution)/shard_map/reduce_scatter | solution.py:288
  1842.2 138.8 %reduce-scatter.65.cloned.1.call-start = ((), (), s32[]{:S(2)}) async-start(), calls=%async_computation.44 | async-start | bytes 2359296 | tf_op jit(solution)/shard_map/reduce_scatter | solution.py:285
  1847.1 158.5 %reduce-scatter.69.cloned.1.call-start = ((), (), s32[]{:S(2)}) async-start(), calls=%async_computation.46 | async-start | bytes 786432 | tf_op jit(solution)/shard_map/reduce_scatter | solution.py:62
  2003.4 130.8 %reduce-scatter.79.cloned.1.call-start = ((), (), s32[]{:S(2)}) async-start(), calls=%async_computation.58 | async-start | bytes 36864
  2005.5 208.4 %reduce-scatter.83.cloned.1.call-start = ((), (), s32[]{:S(2)}) async-start(), calls=%async_computation.60 | async-start | bytes 1114112
  2009.2 281.7 %reduce-scatter.85.cloned.1.call-start = ((), (), s32[]{:S(2)}) async-start(), calls=%async_computation.61 | async-start | bytes 1114112
  2012.1 367.7 %reduce-scatter.73.cloned.1.call-start = ((), (), s32[]{:S(2)}) async-start(), calls=%async_computation.48 | async-start | bytes 4718592 | tf_op jit(solution)/shard_map/reduce_scatter | solution.py:338
  2017.7 573.7 %reduce-scatter.71.cloned.1.call-start = ((), (), s32[]{:S(2)}) async-start(), calls=%async_computation.47 | async-start | bytes 14155776 | tf_op jit(solution)/shard_map/reduce_scatter | solution.py:329
  2030.3 847.1 %reduce-scatter.75.cloned.1.call-start = ((), (), s32[]{:S(2)}) async-start(), calls=%async_computation.49 | async-start | bytes 18874368 | tf_op jit(solution)/shard_map/reduce_scatter | solution.py:341
  2046.1 1116.9 %reduce-scatter.77.cloned.1.call-start = ((), (), s32[]{:S(2)}) async-start(), calls=%async_computation.50 | async-start | bytes 18874368 | tf_op jit(solution)/shard_map/reduce_scatter | solution.py:350
  (274 other events, 7593.5 us)
Sparse Core Ops, SparseCore 0:
  10.2 179.4 all-gather.27
  197.0 47.5 all-gather.21
  247.4 47.7 all-gather.29
  297.1 73.4 all-gather.31
  389.4 227.6 all-gather.33
  619.4 225.9 all-gather.35
  889.3 49.2 all-gather.23
  941.2 47.7 all-gather.37
  1125.8 49.2 all-gather.25
  1177.3 47.7 all-gather.39
  1294.0 66.1 reduce-scatter.50
  1364.2 66.7 reduce-scatter.48
  1571.4 67.5 reduce-scatter.58
  1643.1 66.6 reduce-scatter.56
  1842.3 67.7 reduce-scatter.66
  1914.1 66.8 reduce-scatter.64
  2025.1 53.4 reduce-scatter.80
  2081.6 52.5 reduce-scatter.78
  2137.0 76.8 reduce-scatter.82
  2216.8 74.0 reduce-scatter.84
  2295.0 84.7 reduce-scatter.72
  2383.8 207.4 reduce-scatter.70
  2595.6 281.7 reduce-scatter.74
  2881.0 281.8 reduce-scatter.76
  (12 shorter events, 163.8 us)
where the time goes:
time: 3180 us; the launch traced here: 3170 us
  waiting for transfers between devices  2330 us (73%)
  matrix products  314 us (10%)
  blocking collectives  246 us (8%)
  local copies, waits for them, and re-layouts  157 us (5%)
  other arithmetic  96 us (3%)
    reduce_scatter x1, waiting for transfers between devices, reduce_grads(): lax.psum_scatter(up_grad[None].astype(jnp.bfloat16), 'dp', scatter_dimens...  283 us
    reduce_scatter x1, waiting for transfers between devices, reduce_grads(): lax.psum_scatter(down_grad[None].astype(jnp.bfloat16), 'dp', scatter_dime...  281 us
    unnamed x40, waiting for transfers between devices  221 us
    all_gather x1, waiting for transfers between devices, fetch_weights(): lax.all_gather(down_weight[0], 'dp', axis=1, tiled=True)  217 us
    reduce_scatter x3, waiting for transfers between devices, backward(): lax.psum_scatter(grad_k_all.astype(jnp.bfloat16), 'dp', scatter_dimension...  212 us
    reduce_scatter x1, waiting for transfers between devices, reduce_grads(): lax.psum_scatter(qkv_grad[None].astype(jnp.bfloat16), 'dp', scatter_dimen...  209 us
    all_gather x1, waiting for transfers between devices, fetch_weights(): lax.all_gather(up_weight[0], 'dp', axis=0, tiled=True)  199 us
    reduce_scatter x3, waiting for transfers between devices, backward(): lax.psum_scatter(grad_v_all.astype(jnp.bfloat16), 'dp', scatter_dimension...  182 us
  transfers between devices with their start and end apart: 40, of which 33 were waited for; matrix products, arithmetic and copies ran while one was open for 8% of the time, Pallas kernels for 0%

commit v1 on v0

--- a/solution.py
+++ b/solution.py
@@ -4,6 +4,8 @@
 import jax
 import jax.numpy as jnp
 from jax import lax
+from jax.experimental import pallas as pl
+from jax.experimental.pallas import tpu as pltpu
 from jax.sharding import PartitionSpec as P
 
 HD = 128
@@ -11,6 +13,7 @@
 
 EPSILON = 1e-05
 NEG_FILL = -1e30
+MESH = pl.DeviceIdType.MESH
 
 
 def from_behind(value, axis, steps):
@@ -453,6 +456,782 @@
     return (acts, input_grads) + tuple(summed)
 
 
+def place():
+    dp = lax.axis_index("dp")
+    return (lax.axis_index("section"), dp // 2, lax.rem(dp, 2), lax.axis_index("tensor"))
+
+
+def device(core, z, x, y):
+    return (core, z * 2 + x, y)
+
+
+def greet(partners):
+    barrier = pltpu.get_barrier_semaphore()
+    expected = 0
+    for present, partner in partners:
+        if present is True:
+            pl.semaphore_signal(barrier, inc=1, device_id=partner, device_id_type=MESH)
+            expected = expected + 1
+        else:
+
+            @pl.when(present)
+            def _(partner=partner):
+                pl.semaphore_signal(barrier, inc=1, device_id=partner, device_id_type=MESH)
+
+            expected = expected + present.astype(jnp.int32)
+    pl.semaphore_wait(barrier, expected)
+
+
+def guarded(present, act):
+    if present is True:
+        act()
+    else:
+        pl.when(present)(act)
+
+
+class Sends:
+    def __init__(self, sems):
+        self.sems = sems
+        self.pending = []
+
+    def start(self, present, source, target, arrived, partner):
+        copy = pltpu.make_async_remote_copy(
+            src_ref=source,
+            dst_ref=target,
+            send_sem=self.sems.at[len(self.pending)],
+            recv_sem=arrived,
+            device_id=partner,
+            device_id_type=MESH,
+        )
+        guarded(present, copy.start)
+        self.pending.append((present, copy))
+
+    def finish(self):
+        for present, copy in self.pending:
+            guarded(present, copy.wait_send)
+
+
+def await_block(block, arrived, partner):
+    pltpu.make_async_remote_copy(
+        src_ref=block,
+        dst_ref=block,
+        send_sem=arrived,
+        recv_sem=arrived,
+        device_id=partner,
+        device_id_type=MESH,
+    ).wait_recv()
+
+
+def plane_neighbours(levels):
+    core, z, x, y = place()
+    return (
+        device(1 - core, z, x, y),
+        device(core, z, x, 1 - y),
+        device(core, jnp.maximum(z - 1, 0), x, y),
+        device(core, jnp.minimum(z + 1, levels - 1), x, y),
+    )
+
+
+def gather_kernel(levels, own_ref, all_ref, send_sems, recv_sems, local_sem):
+    core, z, x, y = place()
+    sibling, across, left, right = plane_neighbours(levels)
+    has_left, has_right = (z > 0, z < levels - 1)
+    greet([(True, sibling), (True, across), (has_left, left), (has_right, right)])
+    rows = own_ref.shape[0]
+
+    def block(zz, cc, yy):
+        number = zz * 4 + cc * 2 + yy
+        return (
+            all_ref.at[pl.ds(pl.multiple_of(number * rows, rows), rows)],
+            recv_sems.at[number],
+        )
+
+    sends = Sends(send_sems)
+    home, home_sem = block(z, core, y)
+    keep = pltpu.make_async_copy(own_ref, home, local_sem)
+    for present, partner in (
+        (True, across),
+        (has_left, left),
+        (has_right, right),
+        (True, sibling),
+    ):
+        sends.start(present, own_ref, home, home_sem, partner)
+    keep.start()
+
+    def take_across(distance):
+        for zz in (z,) if distance == 0 else (z - distance, z + distance):
+            present = True if distance == 0 else (zz >= 0) & (zz < levels)
+            held, arrived = block(jnp.clip(zz, 0, levels - 1), core, 1 - y)
+            guarded(present, partial(await_block, held, arrived, across))
+            sends.start(present, held, held, arrived, sibling)
+
+    for distance in range(1, levels):
+        for zz, onward, can_go, source in (
+            (z - distance, right, has_right, left),
+            (z + distance, left, has_left, right),
+        ):
+            present = (zz >= 0) & (zz < levels)
+            held, arrived = block(jnp.clip(zz, 0, levels - 1), core, y)
+            guarded(present, partial(await_block, held, arrived, source))
+            sends.start(present, held, held, arrived, across)
+            sends.start(present & can_go, held, held, arrived, onward)
+            sends.start(present, held, held, arrived, sibling)
+        take_across(distance - 1)
+    take_across(levels - 1)
+    for zz in range(levels):
+        for yy in (0, 1):
+            held, arrived = block(zz, 1 - core, yy)
+            await_block(held, arrived, sibling)
+    keep.wait()
+    sends.finish()
+
+
+def gather_rows(own):
+    levels = lax.axis_size("dp") // 2
+    rows, width = own.shape
+    blocks = levels * 4
+    return pl.pallas_call(
+        partial(gather_kernel, levels),
+        out_shape=jax.ShapeDtypeStruct((blocks * rows, width), own.dtype),
+        in_specs=[pl.BlockSpec(memory_space=pl.ANY)],
+        out_specs=pl.BlockSpec(memory_space=pl.ANY),
+        scratch_shapes=[
+            pltpu.SemaphoreType.DMA((4 + 6 * (levels - 1) + 2 * levels - 1,)),
+            pltpu.SemaphoreType.DMA((blocks,)),
+            pltpu.SemaphoreType.DMA,
+        ],
+        compiler_params=pltpu.CompilerParams(collective_id=0, has_side_effects=True),
+        name="gather_rows",
+    )(own)
+
+
+def scatter_kernel(
+    levels,
+    part_ref,
+    sum_ref,
+    from_sibling,
+    from_across,
+    from_left,
+    from_right,
+    to_across,
+    to_left,
+    to_right,
+    send_sems,
+    sibling_sems,
+    across_sems,
+    left_sems,
+    right_sems,
+):
+    core, z, x, y = place()
+    sibling, across, left, right = plane_neighbours(levels)
+    has_left, has_right = (z > 0, z < levels - 1)
+    greet([(True, sibling), (True, across), (has_left, left), (has_right, right)])
+    rows = sum_ref.shape[0]
+
+    def part(zz, cc, yy):
+        number = zz * 4 + cc * 2 + yy
+        return part_ref.at[pl.ds(pl.multiple_of(number * rows, rows), rows)]
+
+    def wide(ref):
+        return ref[...].astype(jnp.float32)
+
+    sends = Sends(send_sems)
+    order = []
+    for distance in range(levels - 1, -1, -1):
+        for zz in (z,) if distance == 0 else (z + distance, z - distance):
+            present = True if distance == 0 else (zz >= 0) & (zz < levels)
+            order.append((distance, present, jnp.clip(zz, 0, levels - 1)))
+    for yy in (1 - y, y):
+        for distance, present, zz in order:
+            slot = zz * 2 + yy
+            sends.start(
+                present,
+                part(zz, 1 - core, yy),
+                from_sibling.at[slot],
+                sibling_sems.at[slot],
+                sibling,
+            )
+
+    def pair(zz, yy):
+        slot = zz * 2 + yy
+        await_block(from_sibling.at[slot], sibling_sems.at[slot], sibling)
+        return wide(part(zz, core, yy)) + wide(from_sibling.at[slot])
+
+    for distance, present, zz in order:
+
+        def stage(zz=zz):
+            to_across[zz] = pair(zz, 1 - y).astype(to_across.dtype)
+
+        guarded(present, stage)
+        sends.start(present, to_across.at[zz], from_across.at[zz], across_sems.at[zz], across)
+
+    def plane_sum(zz):
+        total = pair(zz, y)
+        await_block(from_across.at[zz], across_sems.at[zz], across)
+        return total + wide(from_across.at[zz])
+
+    for distance in range(levels - 1, 0, -1):
+        for zz, staging, landing, sems, onward, behind, has_behind, came, came_sems in (
+            (z + distance, to_right, from_left, left_sems, right, left, has_left, from_left, left_sems),
+            (z - distance, to_left, from_right, right_sems, left, right, has_right, from_right, right_sems),
+        ):
+            present = (zz >= 0) & (zz < levels)
+            zz = jnp.clip(zz, 0, levels - 1)
+
+            def stage(zz=zz, staging=staging, behind=behind, has_behind=has_behind, came=came, came_sems=came_sems):
+                total = plane_sum(zz)
+
+                @pl.when(has_behind)
+                def _():
+                    await_block(came.at[zz], came_sems.at[zz], behind)
+                    staging[zz] = (total + wide(came.at[zz])).astype(staging.dtype)
+
+                @pl.when(jnp.logical_not(has_behind))
+                def _():
+                    staging[zz] = total.astype(staging.dtype)
+
+            guarded(present, stage)
+            sends.start(present, staging.at[zz], landing.at[zz], sems.at[zz], onward)
+    sum_ref[...] = plane_sum(z)
+    for present, came, came_sems, behind in (
+        (has_left, from_left, left_sems, left),
+        (has_right, from_right, right_sems, right),
+    ):
+
+        def take(came=came, came_sems=came_sems, behind=behind):
+            await_block(came.at[z], came_sems.at[z], behind)
+            sum_ref[...] += wide(came.at[z])
+
+        guarded(present, take)
+    sends.finish()
+
+
+def scatter_sum(part):
+    levels = lax.axis_size("dp") // 2
+    blocks = levels * 4
+    rows, width = (part.shape[0] // blocks, part.shape[1])
+
+    def held(count):
+        return pltpu.VMEM((count, rows, width), part.dtype)
+
+    return pl.pallas_call(
+        partial(scatter_kernel, levels),
+        out_shape=jax.ShapeDtypeStruct((rows, width), jnp.float32),
+        in_specs=[pl.BlockSpec(memory_space=pltpu.VMEM)],
+        out_specs=pl.BlockSpec(memory_space=pltpu.VMEM),
+        scratch_shapes=[
+            held(2 * levels),
+            held(levels),
+            held(levels),
+            held(levels),
+            held(levels),
+            held(levels),
+            held(levels),
+            pltpu.SemaphoreType.DMA((3 * (2 * levels - 1) + 2 * (levels - 1),)),
+            pltpu.SemaphoreType.DMA((2 * levels,)),
+            pltpu.SemaphoreType.DMA((levels,)),
+            pltpu.SemaphoreType.DMA((levels,)),
+            pltpu.SemaphoreType.DMA((levels,)),
+        ],
+        compiler_params=pltpu.CompilerParams(
+            collective_id=1, has_side_effects=True, vmem_limit_bytes=32 << 20
+        ),
+        name="scatter_sum",
+    )(part)
+
+
+def piece_of_shard(which, ref, member, depth):
+    if which in (1, 3):
+        return ref.at[pl.ds(pl.multiple_of(member * depth, depth), depth)]
+    return ref.at[:, pl.ds(pl.multiple_of(member * depth, depth), depth)]
+
+
+def piece_of_slice(which, ref, layer, shard, depth):
+    if which in (1, 3):
+        return ref.at[layer, :, pl.ds(pl.multiple_of(shard * depth, depth), depth)]
+    return ref.at[layer, pl.ds(pl.multiple_of(shard * depth, depth), depth)]
+
+
+def everyone_in_column(levels):
+    core, z, x, y = place()
+    partners = []
+    for step in range(levels):
+        zz = lax.rem(z + step, levels)
+        for other in (0, 1):
+            if step or other:
+                partners.append((True, device(1 - core if other else core, zz, x, y)))
+    return partners
+
+
+def fetch_kernel(levels, *refs):
+    shards, slices = (refs[:4], refs[4:8])
+    send_sems, column_sems, cross_sems, local_sems = refs[8:]
+    core, z, x, y = place()
+    over = device(core, z, 1 - x, y)
+    greet(everyone_in_column(levels) + [(True, over)])
+    own_shard = z * 2 + x
+    members = 2 * levels
+    sends = Sends(send_sems)
+    keeps = []
+
+    def spread(which):
+        shard_ref, slice_ref = (shards[which], slices[which])
+        member_depth = shard_ref.shape[0 if which in (1, 3) else 1] // members
+        slice_depth = slice_ref.shape[2 if which in (1, 3) else 1] // members
+        target = piece_of_slice(which, slice_ref, core, own_shard, slice_depth)
+        for step in range(levels):
+            zz = lax.rem(z + step, levels)
+            for other in (0, 1):
+                cc = 1 - core if other else core
+                source = piece_of_shard(which, shard_ref, zz * 2 + cc, member_depth)
+                if step or other:
+                    sends.start(
+                        True, source, target, column_sems.at[which, core, z], device(cc, zz, x, y)
+                    )
+                else:
+                    keep = pltpu.make_async_copy(source, target, local_sems.at[which])
+                    keep.start()
+                    keeps.append(keep)
+                    sends.start(True, source, target, cross_sems.at[which, core, z], over)
+
+    def hand_over(which):
+        slice_ref = slices[which]
+        slice_depth = slice_ref.shape[2 if which in (1, 3) else 1] // members
+        for step in range(levels):
+            zz = lax.rem(z - step + levels, levels)
+            for other in (0, 1):
+                if step or other:
+                    layer = 1 - core if other else core
+                    held = piece_of_slice(which, slice_ref, layer, zz * 2 + x, slice_depth)
+                    await_block(held, column_sems.at[which, layer, zz], over)
+                    sends.start(True, held, held, cross_sems.at[which, layer, zz], over)
+
+    for which in range(4):
+        spread(which)
+    for which in range(4):
+        hand_over(which)
+    for which in range(4):
+        slice_ref = slices[which]
+        slice_depth = slice_ref.shape[2 if which in (1, 3) else 1] // members
+        for zz in range(levels):
+            for layer in (0, 1):
+                held = piece_of_slice(which, slice_ref, layer, zz * 2 + 1 - x, slice_depth)
+                await_block(held, cross_sems.at[which, layer, zz], over)
+    for keep in keeps:
+        keep.wait()
+    sends.finish()
+
+
+def fetch_slices(shards):
+    levels = lax.axis_size("dp") // 2
+    members = 2 * levels
+    shapes = [
+        (2, shard.shape[0] // members, shard.shape[1] * members)
+        if which in (1, 3)
+        else (2, shard.shape[0] * members, shard.shape[1] // members)
+        for which, shard in enumerate(shards)
+    ]
+    anywhere = pl.BlockSpec(memory_space=pl.ANY)
+    return pl.pallas_call(
+        partial(fetch_kernel, levels),
+        out_shape=[jax.ShapeDtypeStruct(shape, jnp.bfloat16) for shape in shapes],
+        in_specs=[anywhere] * 4,
+        out_specs=[anywhere] * 4,
+        scratch_shapes=[
+            pltpu.SemaphoreType.DMA((4 * 4 * levels,)),
+            pltpu.SemaphoreType.DMA((4, 2, levels)),
+            pltpu.SemaphoreType.DMA((4, 2, levels)),
+            pltpu.SemaphoreType.DMA((4,)),
+        ],
+        compiler_params=pltpu.CompilerParams(collective_id=2, has_side_effects=True),
+        name="fetch_slices",
+    )(*shards)
+
+
+def return_kernel(levels, *refs):
+    slices, shards, landed = (refs[:4], refs[4:8], refs[8:12])
+    send_sems, column_sems, cross_sems, local_sems = refs[12:]
+    core, z, x, y = place()
+    over = device(core, z, 1 - x, y)
+    greet(everyone_in_column(levels) + [(True, over)])
+    members = 2 * levels
+    sends = Sends(send_sems)
+    keeps = []
+    order = [
+        (lax.rem(z + step, levels), 1 - core if other else core, bool(step or other))
+        for step in range(levels - 1, -1, -1)
+        for other in (1, 0)
+    ]
+
+    def depth_of(which):
+        return slices[which].shape[2 if which in (1, 3) else 1] // members
+
+    for which in (3, 2, 1, 0):
+        for zz, layer, away in order:
+            sends.start(
+                True,
+                piece_of_slice(which, slices[which], layer, zz * 2 + 1 - x, depth_of(which)),
+                landed[which].at[layer, zz],
+                cross_sems.at[which, layer, zz],
+                over,
+            )
+    for which in (3, 2, 1, 0):
+        member_depth = shards[which].shape[0 if which in (1, 3) else 1] // members
+        target = piece_of_shard(which, shards[which], z * 2 + core, member_depth)
+        for zz, layer, away in order:
+            held = landed[which].at[layer, zz]
+            await_block(held, cross_sems.at[which, layer, zz], over)
+            own = piece_of_slice(which, slices[which], layer, zz * 2 + x, depth_of(which))
+            held[...] = (held[...].astype(jnp.float32) + own[...].astype(jnp.float32)).astype(
+                held.dtype
+            )
+            if away:
+                sends.start(
+                    True, held, target, column_sems.at[which, core, z], device(layer, zz, x, y)
+                )
+            else:
+                keep = pltpu.make_async_copy(held, target, local_sems.at[which])
+                keep.start()
+                keeps.append(keep)
+    for which in (3, 2, 1, 0):
+        member_depth = shards[which].shape[0 if which in (1, 3) else 1] // members
+        for step in range(levels):
+            zz = lax.rem(z + step, levels)
+            for other in (0, 1):
+                if step or other:
+                    cc = 1 - core if other else core
+                    held = piece_of_shard(which, shards[which], zz * 2 + cc, member_depth)
+                    await_block(held, column_sems.at[which, cc, zz], over)
+    for keep in keeps:
+        keep.wait()
+    sends.finish()
+
+
+def return_slices(slices):
+    levels = lax.axis_size("dp") // 2
+    members = 2 * levels
+    shapes, landing = ([], [])
+    for which, held in enumerate(slices):
+        if which in (1, 3):
+            shapes.append((held.shape[1] * members, held.shape[2] // members))
+            landing.append((2, levels, held.shape[1], held.shape[2] // members))
+        else:
+            shapes.append((held.shape[1] // members, held.shape[2] * members))
+            landing.append((2, levels, held.shape[1] // members, held.shape[2]))
+    return pl.pallas_call(
+        partial(return_kernel, levels),
+        out_shape=[jax.ShapeDtypeStruct(shape, jnp.bfloat16) for shape in shapes],
+        in_specs=[pl.BlockSpec(memory_space=pltpu.VMEM)] * 4,
+        out_specs=[pl.BlockSpec(memory_space=pl.ANY)] * 4,
+        scratch_shapes=[pltpu.VMEM(shape, jnp.bfloat16) for shape in landing]
+        + [
+            pltpu.SemaphoreType.DMA((4 * 4 * levels,)),
+            pltpu.SemaphoreType.DMA((4, 2, levels)),
+            pltpu.SemaphoreType.DMA((4, 2, levels)),
+            pltpu.SemaphoreType.DMA((4,)),
+        ],
+        compiler_params=pltpu.CompilerParams(
+            collective_id=3, has_side_effects=True, vmem_limit_bytes=48 << 20
+        ),
+        name="return_slices",
+    )(*slices)
+
+
+def regroup_kernel(levels, inward, *refs):
+    count = len(refs) // 2 - 1
+    sources, targets = (refs[:count], refs[count : 2 * count])
+    send_sems, recv_sems = refs[2 * count :]
+    core, z, x, y = place()
+    sibling, over, corner = (
+        device(1 - core, z, x, y),
+        device(core, z, 1 - x, y),
+        device(1 - core, z, 1 - x, y),
+    )
+    greet([(True, sibling), (True, over), (True, corner)])
+    waits = []
+    for number, (source, target) in enumerate(zip(sources, targets)):
+        for slot in (0, 1):
+            to_core, to_x, to_slot = (x, slot, core) if inward else (slot, core, x)
+            arrived = recv_sems.at[number, to_slot]
+            sent = send_sems.at[number, slot]
+            for is_here, is_over, partner in (
+                (True, False, over),
+                (False, True, corner),
+                (True, True, sibling),
+            ):
+                chosen = (to_core == core) if not (is_here and is_over) else (to_core != core)
+                same_x = to_x == x
+                if partner is over:
+                    chosen = (to_core == core) & jnp.logical_not(same_x)
+                elif partner is corner:
+                    chosen = (to_core != core) & jnp.logical_not(same_x)
+                else:
+                    chosen = (to_core != core) & same_x
+                copy = pltpu.make_async_remote_copy(
+                    src_ref=source.at[slot],
+                    dst_ref=target.at[to_slot],
+                    send_sem=sent,
+                    recv_sem=arrived,
+                    device_id=partner,
+                    device_id_type=MESH,
+                )
+                pl.when(chosen)(copy.start)
+                waits.append((chosen, copy.wait_send))
+            here = (to_core == core) & (to_x == x)
+            keep = pltpu.make_async_copy(source.at[slot], target.at[to_slot], sent)
+            pl.when(here)(keep.start)
+            waits.append((here, keep.wait))
+    for number, target in enumerate(targets):
+        for slot in (0, 1):
+            from_core, from_x = (slot, core) if inward else (x, slot)
+            away = jnp.logical_not((from_core == core) & (from_x == x))
+            pl.when(away)(
+                partial(await_block, target.at[slot], recv_sems.at[number, slot], over)
+            )
+    for present, wait in waits:
+        pl.when(present)(wait)
+
+
+def regroup(inward, arrays):
+    levels = lax.axis_size("dp") // 2
+    anywhere = pl.BlockSpec(memory_space=pl.ANY)
+    return pl.pallas_call(
+        partial(regroup_kernel, levels, inward),
+        out_shape=[jax.ShapeDtypeStruct(array.shape, array.dtype) for array in arrays],
+        in_specs=[anywhere] * len(arrays),
+        out_specs=[anywhere] * len(arrays),
+        scratch_shapes=[
+            pltpu.SemaphoreType.DMA((len(arrays), 2)),
+            pltpu.SemaphoreType.DMA((len(arrays), 2)),
+        ],
+        compiler_params=pltpu.CompilerParams(
+            collective_id=4 if inward else 5, has_side_effects=True
+        ),
+        name="regroup_in" if inward else "regroup_out",
+    )(*arrays)
+
+
+def attention_weights(queries, keys, allowed):
+    scores = lax.dot_general(
+        queries, keys, (((1,), (1,)), ((), ())), preferred_element_type=jnp.float32
+    ) * HD ** (-0.5)
+    scores = jnp.where(allowed, scores, NEG_FILL)
+    top = jnp.max(scores, axis=-1, keepdims=True)
+    raised = jnp.exp(scores - top)
+    return raised / jnp.sum(raised, axis=-1, keepdims=True)
+
+
+def plane_body(
+    boundary,
+    doc_lengths,
+    qkv_weight,
+    qv_bias,
+    out_weight,
+    up_weight,
+    up_bias,
+    down_weight,
+    norm_gains,
+    norm_biases,
+):
+    core, z, x, y = place()
+    levels = lax.axis_size("dp") // 2
+    members = 2 * levels
+    member = z * 2 + core
+    width = boundary.shape[3]
+    heads_shard = qv_bias.shape[2]
+    head_cut = qv_bias.shape[3]
+    block_shard = up_bias.shape[1]
+    own_blocks = block_shard // members
+    f32, bf16 = (jnp.float32, jnp.bfloat16)
+
+    pieces = (qv_bias[0], up_bias[0], norm_gains[0], norm_biases[0])
+    packed = jnp.concatenate([piece.reshape(-1) for piece in pieces])
+    shared = lax.all_gather(packed, ("section", "dp", "tensor"), axis=0, tiled=False)
+    shared = shared.reshape(2, members, 2, -1)
+    cuts = [0]
+    for piece in pieces:
+        cuts.append(cuts[-1] + piece.size)
+    plane_part = lax.dynamic_index_in_dim(shared, y, 2, keepdims=False)
+    qv = plane_part[:, :, cuts[0] : cuts[1]].reshape(2, members, 2, heads_shard, head_cut)
+    qv = lax.dynamic_index_in_dim(qv, member, 3, keepdims=False)
+    b_qv = qv.transpose(0, 2, 1, 3).reshape(2, 2, HD).astype(f32)
+    ub = plane_part[:, :, cuts[1] : cuts[2]].reshape(2, members, block_shard, head_cut)
+    ub = lax.dynamic_slice_in_dim(ub, member * own_blocks, own_blocks, axis=2)
+    b_up = ub.transpose(0, 2, 1, 3).reshape(2, own_blocks * HD).astype(f32)
+    gain_rows = (
+        shared[..., cuts[2] : cuts[3]].reshape(2, members * 2, 2, -1).transpose(0, 2, 1, 3)
+    ).reshape(2, 2, width).astype(f32)
+    bias_rows = (
+        shared[..., cuts[3] : cuts[4]].reshape(2, members * 2, 4, -1).transpose(0, 2, 1, 3)
+    ).reshape(2, 4, width).astype(f32)
+
+    (planes,) = regroup(True, (boundary[0],))
+    depth = qkv_weight.shape[1]
+    by_head = (
+        qkv_weight[0]
+        .reshape(depth, 3, members, HD)
+        .transpose(0, 2, 1, 3)
+        .reshape(depth, members * 3 * HD)
+    )
+    w_qkv, w_out, w_up, w_down = fetch_slices(
+        (by_head, out_weight[0], up_weight[0], down_weight[0])
+    )
+
+    lengths = lax.dynamic_index_in_dim(doc_lengths, x, 0, keepdims=False)
+    tokens = boundary.shape[2] * 4 * levels
+    position, segment, live, _, _, _ = visibility(lengths, 0, tokens, tokens)
+    allowed = (
+        (segment[:, None] == segment[None, :])
+        & (position[None, :] <= position[:, None])
+        & live[:, None]
+    )
+    live_column = live.astype(f32)[:, None]
+    scaling = HD ** (-0.5)
+
+    def dot(left, right):
+        return jnp.dot(left, right, preferred_element_type=f32)
+
+    def dot_back(left, right):
+        return lax.dot_general(left, right, (((1,), (1,)), ((), ())), preferred_element_type=f32)
+
+    def dot_rows(left, right):
+        return lax.dot_general(left, right, (((0,), (0,)), ((), ())), preferred_element_type=f32)
+
+    entering = planes[0]
+    saved, acts = ([], [])
+    for layer in (0, 1):
+        gains, biases = (gain_rows[layer], bias_rows[layer])
+        hidden = entering.astype(f32)
+        normed, unit_a, inverse_a = layer_norm(hidden, gains[0], biases[0])
+        rows_a = gather_rows(normed.astype(bf16))
+        projected = dot(rows_a, w_qkv[layer])
+        queries = (projected[:, :HD] + b_qv[layer, 0]).astype(bf16)
+        keys = projected[:, HD : 2 * HD].astype(bf16)
+        values = (projected[:, 2 * HD :] + b_qv[layer, 1]).astype(bf16)
+        probs = attention_weights(queries, keys, allowed)
+        mixed = (dot(probs.astype(bf16), values) * live_column).astype(bf16)
+        middle = hidden + scatter_sum(dot(mixed, w_out[layer]).astype(bf16)) + biases[1]
+        normed, unit_b, inverse_b = layer_norm(middle, gains[1], biases[2])
+        rows_b = gather_rows(normed.astype(bf16))
+        preact = dot(rows_b, w_up[layer]) + b_up[layer]
+        activated = jax.nn.gelu(preact, approximate=False).astype(bf16)
+        result = middle + scatter_sum(dot(activated, w_down[layer]).astype(bf16)) + biases[3]
+        entering = result.astype(bf16)
+        acts.append(entering)
+        saved.append(
+            (unit_a, inverse_a, rows_a, queries, keys, values, probs, mixed)
+            + (unit_b, inverse_b, rows_b, preact, activated)
+        )
+
+    grad_out = planes[1].astype(f32)
+    slices, vectors, input_grads = ([None, None], [None, None], [None, None])
+    for layer in (1, 0):
+        gains = gain_rows[layer]
+        unit_a, inverse_a, rows_a, queries, keys, values, probs, mixed = saved[layer][:8]
+        unit_b, inverse_b, rows_b, preact, activated = saved[layer][8:]
+        low_branch = grad_out.astype(bf16)
+        down_bias_grad = jnp.sum(low_branch.astype(f32), axis=0)
+        wide_branch = gather_rows(low_branch)
+        grad_act = dot_back(wide_branch, w_down[layer])
+        _, pull = jax.vjp(partial(jax.nn.gelu, approximate=False), preact)
+        grad_pre = pull(grad_act)[0].astype(bf16)
+        up_bias_grad = jnp.sum(grad_pre.astype(f32), axis=0)
+        grad_b = scatter_sum(dot_back(grad_pre, w_up[layer]).astype(bf16))
+        down_grad = dot_rows(activated, wide_branch).astype(bf16)
+        up_grad = dot_rows(rows_b, grad_pre).astype(bf16)
+        grad_middle = grad_out + norm_back(grad_b, unit_b, inverse_b, gains[1])
+        low_middle = grad_middle.astype(bf16)
+        wide_middle = gather_rows(low_middle)
+        out_grad = dot_rows(mixed, wide_middle).astype(bf16)
+        grad_mixed = dot_back(wide_middle, w_out[layer]).astype(bf16) * live_column.astype(bf16)
+        grad_probs = dot_back(grad_mixed, values)
+        delta = jnp.sum(probs * grad_probs, axis=-1, keepdims=True)
+        grad_scores = jnp.where(allowed, probs * (grad_probs - delta), 0.0).astype(bf16)
+        grad_q = dot(grad_scores, keys) * scaling
+        grad_k = dot_rows(grad_scores, queries) * scaling
+        grad_v = dot_rows(probs.astype(bf16), grad_mixed)
+        grad_proj = jnp.concatenate((grad_q, grad_k, grad_v), axis=1).astype(bf16)
+        proj_sums = jnp.sum(grad_proj.astype(f32), axis=0)
+        grad_a = scatter_sum(dot_back(grad_proj, w_qkv[layer]).astype(bf16))
+        qkv_grad = dot_rows(rows_a, grad_proj).astype(bf16)
+        grad_in = grad_middle + norm_back(grad_a, unit_a, inverse_a, gains[0])
+        input_grads[layer] = grad_in
+        grad_out = grad_in.astype(bf16).astype(f32)
+        slices[layer] = (qkv_grad, out_grad, up_grad, down_grad)
+        vectors[layer] = (
+            jnp.stack((proj_sums[:HD], proj_sums[2 * HD :])),
+            up_bias_grad,
+            jnp.stack((jnp.sum(grad_a * unit_a, axis=0), jnp.sum(grad_b * unit_b, axis=0))),
+            jnp.stack(
+                (
+                    jnp.sum(grad_a, axis=0),
+                    jnp.sum(low_middle.astype(f32), axis=0),
+                    jnp.sum(grad_b, axis=0),
+                    down_bias_grad,
+                )
+            ),
+        )
+
+    shards = return_slices([jnp.stack(pair) for pair in zip(*slices)])
+    qkv_shard = (
+        shards[0]
+        .reshape(depth, members, 3, HD)
+        .transpose(0, 2, 1, 3)
+        .reshape(depth, 3, members * HD)
+        .astype(f32)
+    )
+    outward = []
+    for layer in (0, 1):
+        qv_grad, up_bias_grad, gains_grad, biases_grad = vectors[layer]
+        qv_all = jnp.zeros((2, 2, heads_shard, HD), f32)
+        qv_all = lax.dynamic_update_slice(qv_all, qv_grad[None, :, None], (y, 0, member, 0))
+        up_all = jnp.zeros((2, block_shard, HD), f32)
+        up_all = lax.dynamic_update_slice(
+            up_all, up_bias_grad.reshape(1, own_blocks, HD), (y, member * own_blocks, 0)
+        )
+        outward.append(
+            jnp.concatenate(
+                (
+                    qv_all.reshape(2, 2, heads_shard, members, head_cut)
+                    .transpose(3, 0, 1, 2, 4)
+                    .reshape(members * 2, -1),
+                    up_all.reshape(2, block_shard, members, head_cut)
+                    .transpose(2, 0, 1, 3)
+                    .reshape(members * 2, -1),
+                    gains_grad.reshape(2, members * 2, -1).transpose(1, 0, 2).reshape(members * 2, -1),
+                    biases_grad.reshape(4, members * 2, -1).transpose(1, 0, 2).reshape(members * 2, -1),
+                ),
+                axis=1,
+            )
+        )
+    own_vector = lax.psum_scatter(
+        jnp.stack(outward).reshape(4 * members, -1),
+        ("section", "dp", "tensor"),
+        scatter_dimension=0,
+        tiled=True,
+    ).reshape(-1)
+    small = [
+        own_vector[cuts[at] : cuts[at + 1]].reshape((1,) + pieces[at].shape) for at in range(4)
+    ]
+    acts_out, grads_out = regroup(False, (jnp.stack(acts), jnp.stack(input_grads)))
+    return (
+        acts_out[None],
+        grads_out[None],
+        qkv_shard[None],
+        small[0],
+        shards[1].astype(f32)[None],
+        shards[2].astype(f32)[None],
+        small[1],
+        shards[3].astype(f32)[None],
+        small[2],
+        small[3],
+    )
+
+
+def fits_plane(mesh):
+    return mesh.shape["dp"] == 8 and mesh.shape["tensor"] == 2 and mesh.shape["section"] == 2
+
+
 def solution(mesh):
     placed = (
         P("section", None, ("dp", "tensor"), None),
@@ -467,7 +1246,7 @@
         P("section", None, ("dp", "tensor")),
     )
     return jax.shard_map(
-        body,
+        plane_body if fits_plane(mesh) else body,
         mesh=mesh,
         in_specs=placed,
         out_specs=(

time: 3180 us -> 1140 us (0.36)
  waiting for transfers between devices: 2330 us -> 0.02 us
  Pallas kernels: 0 us -> 869 us
  matrix products: 314 us -> 98.9 us
  blocking collectives: 246 us -> 71.1 us
  local copies, waits for them, and re-layouts: 157 us -> 37.9 us
  other arithmetic: 96 us -> 38 us
    reduce_scatter x22 -> x0, waiting for transfers between devices: 1320 us -> none  [the longest x1 283 us: reduce_grads(): lax.psum_scatter(up_grad[None].astype(jnp.bfloat16), 'dp', scatter_dimens...]
    pallas_call x0 -> x20, Pallas kernels: none -> 860 us  [the longest x8 261 us: scatter_sum(): pl.pallas_call(partial(scatter_kernel, levels), out_shape=jax.ShapeDtypeS...]
    all_gather x10 -> x0, waiting for transfers between devices: 791 us -> none  [the longest x1 217 us: fetch_weights(): lax.all_gather(down_weight[0], 'dp', axis=1, tiled=True)]
    unnamed x40 -> x2, waiting for transfers between devices: 221 us -> 0.02 us
    dot_general x70 -> x34, matrix products: 314 us -> 98.9 us  [the longest x10 40.7 us: dot(): return jnp.dot(left, right, preferred_element_type=f32)]
    all_gather x16 -> x1, blocking collectives: 246 us -> 71.1 us  [plane_body(): lax.all_gather(packed, ('section', 'dp', 'tensor'), axis=0, tiled=False)]
    unnamed x451 -> x132, local copies, waits for them, and re-layouts: 86.9 us -> 19.7 us
  transfers between devices with their start and end apart: 40 -> 1, of which waited for: 33 -> 0; matrix products, arithmetic and copies ran while one was open for 8% -> 4% of each run, Pallas kernels for 0% -> 16%
where the time goes in v1:
time: 1140 us; the launch traced here: 1130 us
  Pallas kernels  869 us (76%)
  matrix products  98.9 us (9%)
  blocking collectives  71.1 us (6%)
  other arithmetic  38 us (3%)
  local copies, waits for them, and re-layouts  37.9 us (3%)
  between operations  15.9 us (1%)
    pallas_call x8, Pallas kernels, scatter_sum(): pl.pallas_call(partial(scatter_kernel, levels), out_shape=jax.ShapeDtypeS...  261 us
    pallas_call x8, Pallas kernels, gather_rows(): pl.pallas_call(partial(gather_kernel, levels), out_shape=jax.ShapeDtypeSt...  241 us
    pallas_call x1, Pallas kernels, fetch_slices(): pl.pallas_call(partial(fetch_kernel, levels), out_shape=[jax.ShapeDtypeSt...  168 us
    pallas_call x1, Pallas kernels, return_slices(): pl.pallas_call(partial(return_kernel, levels), out_shape=[jax.ShapeDtypeS...  151 us
    all_gather x1, blocking collectives, plane_body(): lax.all_gather(packed, ('section', 'dp', 'tensor'), axis=0, tiled=False)  71.1 us
    dot_general x10, matrix products, dot(): return jnp.dot(left, right, preferred_element_type=f32)  40.7 us
    pallas_call x2, Pallas kernels, regroup(): pl.pallas_call(partial(regroup_kernel, levels, inward), out_shape=[jax.Sh...  38.2 us
    dot_general x10, matrix products, dot_back(): lax.dot_general(left, right, (((1,), (1,)), ((), ())), preferred_element_...  31.5 us
  transfers between devices with their start and end apart: 1, of which 0 were waited for; matrix products, arithmetic and copies ran while one was open for 4% of the time, Pallas kernels for 16%

profile of v1, /device:TPU:0, one launch (start us, length us, event | category | flops | bytes accessed | tf_op | source)
XLA Modules:
  0.0 1130.4 jit_solution(5621391974640674951)
XLA Ops:
  9.6 71.1 %all-gather.1 = bf16[32,1,1536]{2,1,0:T(2,128)(2,1)S(1)} all-gather(bf16[1,1,1536]{2,1,0:T(2,128)(2,1)S(1)} %reshape.404), channel_id=2, replica_groups=mesh['section'=2,'dp'=8,'tensor'=2] {'section','dp','tensor'}, dimensions={0}, use_global_device_ids=true | all-gather | bytes 101376 | tf_op jit(solution)/shard_map/all_gather | solution.py:1049
  81.5 9.5 regroup_in.1
  101.1 28.6 %gather_rows.12 = bf16[1024,2048]{1,0:T(8,128)(2,1)} custom-call(bf16[64,2048]{1,0:T(8,128)(2,1)} %slice_bitcast_fusion.own_ref), custom_call_target="tpu_custom_call" | custom-call | tf_op jit(solution)/shard_map/gather_rows/pallas_call | solution.py:593
  130.6 34.0 %gather_rows.8 = bf16[1024,2048]{1,0:T(8,128)(2,1)} custom-call(bf16[64,2048]{1,0:T(8,128)(2,1)} %fusion.106.own_ref), custom_call_target="tpu_custom_call" | custom-call | tf_op jit(solution)/shard_map/gather_rows/pallas_call | solution.py:593
  164.6 167.7 %fetch_slices.1 = (bf16[2,2048,384]{2,1,0:T(8,128)(2,1)}, bf16[2,128,2048]{2,1,0:T(8,128)(2,1)}, bf16[2,2048,512]{2,1,0:T(8,128)(2,1)}, bf16[2,512,2048]{2,1,0:T(8,128)(2,1)}) custom-call(bf16[256,3072]{1,0:T(8,128)(2,1)} %copy.73.refs_0_, bf16[1024,256]{1,0:T(8,128)(2,1)} %bitcast.327, bf16[256,4096]{1,0:T(8,128)(2,1)} %bitcast.322, bf16[4096,256]{1,0:T(8,128)(2,1)} %bitcast.323), custom_call_target="tpu_custom_call" | custom-call | tf_op jit(solution)/shard_map/fetch_slices/pallas_call | solution.py:835
  348.4 42.6 %scatter_sum.8 = f32[64,2048]{1,0:T(8,128)S(1)} custom-call(bf16[1024,2048]{1,0:T(8,128)(2,1)S(1)} %convolution_convert_fusion.7.part_ref), custom_call_target="tpu_custom_call" | custom-call | tf_op jit(solution)/shard_map/scatter_sum/pallas_call | solution.py:717
  392.4 30.4 %gather_rows.9 = bf16[1024,2048]{1,0:T(8,128)(2,1)} custom-call(bf16[64,2048]{1,0:T(8,128)(2,1)} %add_convert_fusion.4.own_ref), custom_call_target="tpu_custom_call" | custom-call | tf_op jit(solution)/shard_map/gather_rows/pallas_call | solution.py:593
  422.8 10.6 multiply_convert_fusion.1
  435.7 30.5 %scatter_sum.9 = f32[64,2048]{1,0:T(8,128)S(1)} custom-call(bf16[1024,2048]{1,0:T(8,128)(2,1)S(1)} %convolution_convert_fusion.5.part_ref), custom_call_target="tpu_custom_call" | custom-call | tf_op jit(solution)/shard_map/scatter_sum/pallas_call | solution.py:717
  467.5 27.4 %gather_rows.10 = bf16[1024,2048]{1,0:T(8,128)(2,1)} custom-call(bf16[64,2048]{1,0:T(8,128)(2,1)} %fusion.98.own_ref), custom_call_target="tpu_custom_call" | custom-call | tf_op jit(solution)/shard_map/gather_rows/pallas_call | solution.py:593
  511.8 32.1 %scatter_sum.10 = f32[64,2048]{1,0:T(8,128)S(1)} custom-call(bf16[1024,2048]{1,0:T(8,128)(2,1)S(1)} %convolution_convert_fusion.6.part_ref), custom_call_target="tpu_custom_call" | custom-call | tf_op jit(solution)/shard_map/scatter_sum/pallas_call | solution.py:717
  545.2 30.5 %gather_rows.11 = bf16[1024,2048]{1,0:T(8,128)(2,1)} custom-call(bf16[64,2048]{1,0:T(8,128)(2,1)} %add_convert_fusion.2.own_ref), custom_call_target="tpu_custom_call" | custom-call | tf_op jit(solution)/shard_map/gather_rows/pallas_call | solution.py:593
  575.7 9.2 multiply_convert_fusion
  588.2 30.7 %scatter_sum.11 = f32[64,2048]{1,0:T(8,128)S(1)} custom-call(bf16[1024,2048]{1,0:T(8,128)(2,1)S(1)} %convolution_convert_fusion.4.part_ref), custom_call_target="tpu_custom_call" | custom-call | tf_op jit(solution)/shard_map/scatter_sum/pallas_call | solution.py:717
  625.4 32.1 %scatter_sum.12 = f32[64,2048]{1,0:T(8,128)S(1)} custom-call(bf16[1024,2048]{1,0:T(8,128)(2,1)S(1)} %convolution_convert_fusion.3.part_ref), custom_call_target="tpu_custom_call" | custom-call | tf_op jit(solution)/shard_map/scatter_sum/pallas_call | solution.py:717
  658.8 32.6 %gather_rows.13 = bf16[1024,2048]{1,0:T(8,128)(2,1)} custom-call(bf16[64,2048]{1,0:T(8,128)(2,1)} %get-tuple-element.84.own_ref), custom_call_target="tpu_custom_call" | custom-call | tf_op jit(solution)/shard_map/gather_rows/pallas_call | solution.py:593
  705.8 30.5 %scatter_sum.13 = f32[64,2048]{1,0:T(8,128)S(1)} custom-call(bf16[1024,2048]{1,0:T(8,128)(2,1)S(1)} %convolution_convert_fusion.1.part_ref), custom_call_target="tpu_custom_call" | custom-call | tf_op jit(solution)/shard_map/scatter_sum/pallas_call | solution.py:717
  737.5 27.2 %gather_rows.14 = bf16[1024,2048]{1,0:T(8,128)(2,1)} custom-call(bf16[64,2048]{1,0:T(8,128)(2,1)} %get-tuple-element.81.own_ref), custom_call_target="tpu_custom_call" | custom-call | tf_op jit(solution)/shard_map/gather_rows/pallas_call | solution.py:593
  764.7 7.2 convert_reduce_fusion.1
  774.4 32.2 %scatter_sum.14 = f32[64,2048]{1,0:T(8,128)S(1)} custom-call(bf16[1024,2048]{1,0:T(8,128)(2,1)S(1)} %convolution_convert_fusion.2.part_ref), custom_call_target="tpu_custom_call" | custom-call | tf_op jit(solution)/shard_map/scatter_sum/pallas_call | solution.py:717
  808.1 30.5 %gather_rows.15 = bf16[1024,2048]{1,0:T(8,128)(2,1)} custom-call(bf16[64,2048]{1,0:T(8,128)(2,1)} %get-tuple-element.78.own_ref), custom_call_target="tpu_custom_call" | custom-call | tf_op jit(solution)/shard_map/gather_rows/pallas_call | solution.py:593
  858.5 30.5 %scatter_sum.15 = f32[64,2048]{1,0:T(8,128)S(1)} custom-call(bf16[1024,2048]{1,0:T(8,128)(2,1)S(1)} %copy-done.2), custom_call_target="tpu_custom_call" | custom-call | tf_op jit(solution)/shard_map/scatter_sum/pallas_call | solution.py:717
  919.6 151.3 %return_slices.1 = (bf16[256,3072]{1,0:T(8,128)(2,1)S(1)}, bf16[1024,256]{1,0:T(8,128)(2,1)S(1)}, bf16[256,4096]{1,0:T(8,128)(2,1)S(1)}, bf16[4096,256]{1,0:T(8,128)(2,1)}) custom-call(bf16[2,2048,384]{2,1,0:T(8,128)(2,1)} %pad_maximum_fusion.2.refs_0_, bf16[2,128,2048]{2,1,0:T(8,128)(2,1)S(1)} %pad_maximum_fusion.4.refs_1_, ...), custom_call_target="tpu_custom_call" | custom-call | tf_op jit(solution)/shard_map/return_slices/pallas_call | solution.py:921
  1078.9 28.7 %regroup_out.1 = (bf16[2,64,2048]{2,1,0:T(8,128)(2,1)}, f32[2,64,2048]{2,1,0:T(8,128)}) custom-call(bf16[2,64,2048]{2,1,0:T(8,128)(2,1)} %pad_maximum_fusion.7.refs_0_, f32[2,64,2048]{2,1,0:T(8,128)} %pad_maximum_fusion.3.refs_1_), custom_call_target="tpu_custom_call" | custom-call | tf_op jit(solution)/shard_map/regroup_out/pallas_call | solution.py:998
  (294 shorter events, 157.0 us)
Async XLA Ops:
  7.2 86.6 %copy-start = (s32[2,1,8]{2,1,0:T(1,128)S(1)}, s32[2,1,8]{2,1,0:T(1,128)}, u32[]{:S(2)}) copy-start(s32[2,1,8]{2,1,0:T(1,128)} %param.11) | copy-start | bytes 196
  7.2 1110.0 %all-reduce.3.cloned.1.call-start = ((), (), s32[]{:S(2)}) async-start(), calls=%async_computation | async-start | bytes 393216
  80.7 15.5 %copy-start.23 = (bf16[1,256,3,1024]{3,1,2,0:T(8,128)(2,1)S(1)}, bf16[1,256,3,1024]{3,1,2,0:T(8,128)(2,1)}, u32[]{:S(2)}) copy-start(bf16[1,256,3,1024]{3,1,2,0:T(8,128)(2,1)} %param.12) | copy-start | bytes 4718596
  94.3 35.4 %copy-start.41 = (f32[1,1,2048]{2,1,0:T(1,128)}, f32[1,1,2048]{2,1,0:T(1,128)S(1)}, u32[]{:S(2)}) copy-start(f32[1,1,2048]{2,1,0:T(1,128)S(1)} %get-tuple-element.116) | copy-start | bytes 24580
  95.0 34.7 %copy-start.43 = (f32[64]{0:T(128)}, f32[64]{0:T(128)S(1)}, u32[]{:S(2)}) copy-start(f32[64]{0:T(128)S(1)} %broadcast_multiply_fusion.11) | copy-start | bytes 772
  96.2 33.5 %copy-start.45 = (f32[64]{0:T(128)}, f32[64]{0:T(128)S(1)}, u32[]{:S(2)}) copy-start(f32[64]{0:T(128)S(1)} %add_rsqrt_fusion.3) | copy-start | bytes 772
  101.1 28.6 %copy-start.9 = (bf16[2,64,2048]{2,1,0:T(8,128)(2,1)S(1)}, bf16[2,64,2048]{2,1,0:T(8,128)(2,1)}, u32[]{:S(2)}) copy-start(bf16[2,64,2048]{2,1,0:T(8,128)(2,1)} %regroup_in.1) | copy-start | bytes 1572868
  422.8 10.6 copy-start.49
  575.7 10.2 copy-start.50
  588.2 30.7 %copy-start.13 = (bf16[1024,2048]{1,0:T(8,128)(2,1)S(1)}, bf16[1024,2048]{1,0:T(8,128)(2,1)}, u32[]{:S(2)}) copy-start(bf16[1024,2048]{1,0:T(8,128)(2,1)} %gather_rows.12) | copy-start | bytes 12582916
  696.2 5.2 copy-start.33
  764.7 7.3 copy-start.48
  774.4 32.6 %copy-start.18 = (bf16[64,2048]{1,0:T(8,128)(2,1)S(1)}, bf16[64,2048]{1,0:T(8,128)(2,1)}, u32[]{:S(2)}) copy-start(bf16[64,2048]{1,0:T(8,128)(2,1)} %get-tuple-element.81.own_ref) | copy-start | bytes 786436
  808.1 30.5 %copy-start.25 = (bf16[2,128,2048]{2,1,0:T(8,128)(2,1)S(1)}, bf16[2,128,2048]{2,1,0:T(8,128)(2,1)}, u32[]{:S(2)}) copy-start(bf16[2,128,2048]{2,1,0:T(8,128)(2,1)} %get-tuple-element.21) | copy-start | bytes 3145732
  843.4 5.2 copy-start.37
  847.5 6.4 copy-start.39
  858.5 30.5 %copy-start.42 = (f32[1,1,2048]{2,1,0:T(1,128)S(1)}, f32[1,1,2048]{2,1,0:T(1,128)}, u32[]{:S(2)}) copy-start(f32[1,1,2048]{2,1,0:T(1,128)} %copy-done.41) | copy-start | bytes 24580
  858.5 30.6 %copy-start.44 = (f32[64]{0:T(128)S(1)}, f32[64]{0:T(128)}, u32[]{:S(2)}) copy-start(f32[64]{0:T(128)} %copy-done.43) | copy-start | bytes 772
  858.5 30.6 %copy-start.46 = (f32[64]{0:T(128)S(1)}, f32[64]{0:T(128)}, u32[]{:S(2)}) copy-start(f32[64]{0:T(128)} %copy-done.45) | copy-start | bytes 772
  890.2 5.1 copy-start.16
  890.2 5.1 copy-start.57
  1113.5 7.9 copy-start.32
  1113.5 8.7 copy-start.26
  1113.5 9.6 copy-start.1
  (37 other events, 91.0 us)
Sparse Core Ops, SparseCore 0:
  890.3 182.1 all-reduce.2

commit v2 on v0

--- a/solution.py
+++ b/solution.py
@@ -1,9 +1,12 @@
 from functools import partial
 import math
+from types import SimpleNamespace
 
 import jax
 import jax.numpy as jnp
 from jax import lax
+from jax.experimental import pallas as pl
+from jax.experimental.pallas import tpu as pltpu
 from jax.sharding import PartitionSpec as P
 
 HD = 128
@@ -11,6 +14,7 @@
 
 EPSILON = 1e-05
 NEG_FILL = -1e30
+MESH = pl.DeviceIdType.MESH
 
 
 def from_behind(value, axis, steps):
@@ -453,6 +457,1359 @@
     return (acts, input_grads) + tuple(summed)
 
 
+LOW, WIDE = (jnp.bfloat16, jnp.float32)
+HBM, VMEM = (pl.ANY, pltpu.VMEM)
+
+
+def dot(left, right):
+    return jnp.dot(left, right, preferred_element_type=WIDE)
+
+
+def dot_back(left, right):
+    return lax.dot_general(left, right, (((1,), (1,)), ((), ())), preferred_element_type=WIDE)
+
+
+def dot_rows(left, right):
+    return lax.dot_general(left, right, (((0,), (0,)), ((), ())), preferred_element_type=WIDE)
+
+
+def device(core, z, x, y):
+    return (core, z * 2 + x, y)
+
+
+class Plane:
+    def __init__(self):
+        dp = lax.axis_index("dp")
+        self.levels = lax.axis_size("dp") // 2
+        self.core, self.y = (lax.axis_index("section"), lax.axis_index("tensor"))
+        self.z, self.x = (dp // 2, lax.rem(dp, 2))
+        self.sibling = device(1 - self.core, self.z, self.x, self.y)
+        self.across = device(self.core, self.z, self.x, 1 - self.y)
+        self.over = device(self.core, self.z, 1 - self.x, self.y)
+        self.corner = device(1 - self.core, self.z, 1 - self.x, self.y)
+        self.member = self.z * 2 + self.core
+        self.block = self.z * 4 + self.core * 2 + self.y
+
+    def along(self, z):
+        return device(self.core, jnp.clip(z, 0, self.levels - 1), self.x, self.y)
+
+    def neighbours(self):
+        return [
+            (True, self.sibling),
+            (True, self.across),
+            (self.z > 0, self.along(self.z - 1)),
+            (self.z < self.levels - 1, self.along(self.z + 1)),
+        ]
+
+    def column(self):
+        partners = []
+        for step in range(self.levels):
+            zz = lax.rem(self.z + step, self.levels)
+            for other in (0, 1):
+                if step or other:
+                    core = 1 - self.core if other else self.core
+                    partners.append((True, device(core, zz, self.x, self.y)))
+        return partners
+
+    def nearest(self):
+        tables = []
+        for z in range(self.levels):
+            tables.append(sorted(range(self.levels), key=lambda zz: (abs(zz - z), zz)))
+        found = []
+        for place in range(self.levels):
+            number = jnp.int32(tables[0][place])
+            for z in range(1, self.levels):
+                number = jnp.where(self.z == z, tables[z][place], number)
+            found.append(number)
+        return found
+
+
+def guarded(present, act):
+    if present is True:
+        act()
+    else:
+        pl.when(present)(act)
+
+
+class Greeting:
+    def __init__(self, partners):
+        self.barrier = pltpu.get_barrier_semaphore()
+        self.expected = 0
+        for present, partner in partners:
+            guarded(present, partial(self.tell, partner))
+            self.expected = self.expected + (1 if present is True else present.astype(jnp.int32))
+
+    def tell(self, partner):
+        pl.semaphore_signal(self.barrier, inc=1, device_id=partner, device_id_type=MESH)
+
+    def wait(self):
+        pl.semaphore_wait(self.barrier, self.expected)
+
+
+class Sends:
+    def __init__(self, sems):
+        self.sems = sems
+        self.pending = []
+
+    def start(self, present, source, target, arrived, partner):
+        copy = pltpu.make_async_remote_copy(
+            src_ref=source,
+            dst_ref=target,
+            send_sem=self.sems.at[len(self.pending)],
+            recv_sem=arrived,
+            device_id=partner,
+            device_id_type=MESH,
+        )
+        guarded(present, copy.start)
+        self.pending.append((present, copy))
+
+    def finish(self):
+        for present, copy in self.pending:
+            guarded(present, copy.wait_send)
+
+
+class Copies:
+    def __init__(self, sems):
+        self.sems = sems
+        self.pending = []
+
+    def start(self, source, target, present=True):
+        copy = pltpu.make_async_copy(source, target, self.sems.at[len(self.pending)])
+        guarded(present, copy.start)
+        self.pending.append([present, copy, False])
+        return len(self.pending) - 1
+
+    def wait(self, number):
+        present, copy, done = self.pending[number]
+        if not done:
+            guarded(present, copy.wait)
+            self.pending[number][2] = True
+
+    def finish(self):
+        for number in range(len(self.pending)):
+            self.wait(number)
+
+
+def await_block(block, arrived, partner):
+    pltpu.make_async_remote_copy(
+        src_ref=block,
+        dst_ref=block,
+        send_sem=arrived,
+        recv_sem=arrived,
+        device_id=partner,
+        device_id_type=MESH,
+    ).wait_recv()
+
+
+def span(start, size):
+    return pl.ds(pl.multiple_of(start * size, size), size)
+
+
+class Gather:
+    def __init__(self, plane, sends, rows, sems):
+        self.plane, self.sends, self.rows, self.sems = (plane, sends, rows, sems)
+        self.chunks = sems.shape[1]
+        self.size = rows.shape[0] // (sems.shape[0] * self.chunks)
+
+    def spot(self, zz, core, y, chunk):
+        number = zz * 4 + core * 2 + y
+        return (
+            self.rows.at[span(number * self.chunks + chunk, self.size)],
+            self.sems.at[number, chunk],
+        )
+
+    def open(self):
+        plane = self.plane
+        for chunk in range(self.chunks):
+            held, arrived = self.spot(plane.z, plane.core, plane.y, chunk)
+            for present, partner in (
+                (True, plane.across),
+                (plane.z > 0, plane.along(plane.z - 1)),
+                (plane.z < plane.levels - 1, plane.along(plane.z + 1)),
+                (True, plane.sibling),
+            ):
+                self.sends.start(present, held, held, arrived, partner)
+
+    def run(self, on_group, tick):
+        plane = self.plane
+        order = plane.nearest()
+
+        def complete(step):
+            zz = order[step]
+            for chunk in range(self.chunks):
+                held, arrived = self.spot(zz, plane.core, 1 - plane.y, chunk)
+                await_block(held, arrived, plane.across)
+                self.sends.start(True, held, held, arrived, plane.sibling)
+            for yy in (plane.y, 1 - plane.y):
+                for chunk in range(self.chunks):
+                    held, arrived = self.spot(zz, 1 - plane.core, yy, chunk)
+                    await_block(held, arrived, plane.sibling)
+            on_group(step, zz)
+
+        for step in range(1, plane.levels):
+            zz = order[step]
+            onward = jnp.where(zz < plane.z, plane.z + 1, plane.z - 1)
+            can_go = (onward >= 0) & (onward < plane.levels)
+            for chunk in range(self.chunks):
+                held, arrived = self.spot(zz, plane.core, plane.y, chunk)
+                await_block(held, arrived, plane.across)
+                self.sends.start(can_go, held, held, arrived, plane.along(onward))
+                self.sends.start(True, held, held, arrived, plane.across)
+                self.sends.start(True, held, held, arrived, plane.sibling)
+            complete(step - 1)
+            tick()
+        complete(plane.levels - 1)
+        tick()
+
+    @staticmethod
+    def count(levels, chunks):
+        return chunks * (4 + 3 * (levels - 1) + levels)
+
+
+def gather_scratch(rows, width, levels, chunks, dtype=LOW):
+    return {
+        "rows": pltpu.VMEM((rows * 4 * levels, width), dtype),
+        "gather_sems": pltpu.SemaphoreType.DMA((4 * levels, chunks)),
+    }
+
+
+class Scatter:
+    def __init__(self, plane, sends, refs, result):
+        self.plane, self.sends, self.refs, self.result = (plane, sends, refs, result)
+        self.size = result.shape[0]
+
+    def part(self, zz, core, y):
+        return self.refs.part.at[span(zz * 4 + core * 2 + y, self.size)]
+
+    def pair(self, zz, y):
+        refs, slot = (self.refs, zz * 2 + y)
+        came = refs.from_sibling.at[slot]
+        await_block(came, refs.sibling_sems.at[slot], self.plane.sibling)
+        return self.part(zz, self.plane.core, y)[...].astype(WIDE) + came[...].astype(WIDE)
+
+    def give_sibling(self, zz):
+        plane, refs = (self.plane, self.refs)
+        for yy in (1 - plane.y, plane.y):
+            slot = zz * 2 + yy
+            self.sends.start(
+                True,
+                self.part(zz, 1 - plane.core, yy),
+                refs.from_sibling.at[slot],
+                refs.sibling_sems.at[slot],
+                plane.sibling,
+            )
+
+    def give_across(self, zz):
+        plane, refs = (self.plane, self.refs)
+        refs.to_across[zz] = self.pair(zz, 1 - plane.y).astype(refs.to_across.dtype)
+        self.sends.start(
+            True, refs.to_across.at[zz], refs.from_across.at[zz], refs.across_sems.at[zz], plane.across
+        )
+
+    def plane_sum(self, zz):
+        refs = self.refs
+        total = self.pair(zz, self.plane.y)
+        came = refs.from_across.at[zz]
+        await_block(came, refs.across_sems.at[zz], self.plane.across)
+        return total + came[...].astype(WIDE)
+
+    def come(self, slot):
+        came = self.refs.from_behind.at[slot]
+        await_block(came, self.refs.behind_sems.at[slot], self.plane.across)
+        return came[...].astype(WIDE)
+
+    def give_onward(self, zz):
+        plane, refs = (self.plane, self.refs)
+        onward = jnp.where(zz > plane.z, plane.z + 1, plane.z - 1)
+        behind = plane.z * 2 - onward
+        refs.total[...] = self.plane_sum(zz)
+
+        @pl.when((behind >= 0) & (behind < plane.levels))
+        def _():
+            refs.total[...] += self.come(zz)
+
+        refs.to_onward[zz] = refs.total[...].astype(refs.to_onward.dtype)
+        slot = jnp.where((onward == zz) & (zz < plane.z), plane.levels, zz)
+        self.sends.start(
+            True,
+            refs.to_onward.at[zz],
+            refs.from_behind.at[slot],
+            refs.behind_sems.at[slot],
+            plane.along(onward),
+        )
+
+    def conclude(self):
+        plane = self.plane
+        self.result[...] = self.plane_sum(plane.z)
+
+        @pl.when(plane.z > 0)
+        def _():
+            self.result[...] += self.come(plane.z)
+
+        @pl.when(plane.z < plane.levels - 1)
+        def _():
+            self.result[...] += self.come(plane.levels)
+
+    @staticmethod
+    def count(levels):
+        return 4 * levels - 1
+
+    def run(self, make, tick, fill=None):
+        levels = self.plane.levels
+        order = self.plane.nearest()[::-1]
+        for step in range(levels + 3):
+            if step < levels:
+                make(step, order[step])
+                self.give_sibling(order[step])
+            if 0 < step <= levels:
+                self.give_across(order[step - 1])
+            if step >= levels - 1:
+                tick()
+                if fill is not None:
+                    fill(step - levels + 1)
+            if 3 <= step < levels + 2:
+                self.give_onward(order[step - 3])
+        self.conclude()
+
+
+def scatter_scratch(rows, width, levels, dtype=LOW):
+    return {
+        "part": pltpu.VMEM((rows * 4 * levels, width), dtype),
+        "from_sibling": pltpu.VMEM((2 * levels, rows, width), dtype),
+        "from_across": pltpu.VMEM((levels, rows, width), dtype),
+        "from_behind": pltpu.VMEM((levels + 1, rows, width), dtype),
+        "to_across": pltpu.VMEM((levels, rows, width), dtype),
+        "to_onward": pltpu.VMEM((levels, rows, width), dtype),
+        "total": pltpu.VMEM((rows, width), WIDE),
+        "sum": pltpu.VMEM((rows, width), WIDE),
+        "sibling_sems": pltpu.SemaphoreType.DMA((2 * levels,)),
+        "across_sems": pltpu.SemaphoreType.DMA((levels,)),
+        "behind_sems": pltpu.SemaphoreType.DMA((levels + 1,)),
+    }
+
+
+def by_rows(which):
+    return which in (1, 3)
+
+
+def piece_of_shard(which, ref, member, members):
+    if by_rows(which):
+        return ref.at[span(member, ref.shape[0] // members)]
+    return ref.at[:, span(member, ref.shape[1] // members)]
+
+
+def piece_of_slice(which, ref, shard, shards):
+    if by_rows(which):
+        return ref.at[:, span(shard, ref.shape[1] // shards)]
+    return ref.at[span(shard, ref.shape[0] // shards)]
+
+
+def slice_shape(which, shape, shards):
+    rows, columns = shape
+    if by_rows(which):
+        return (rows // shards, columns * shards)
+    return (rows * shards, columns // shards)
+
+
+def shard_shape(which, shape, shards):
+    rows, columns = shape
+    if by_rows(which):
+        return (rows * shards, columns // shards)
+    return (rows // shards, columns * shards)
+
+
+class Paced:
+    def __init__(self):
+        self.steps = []
+
+    def declare(self, inputs, outputs, scratch):
+        return (0, 0)
+
+    def partners(self, plane):
+        return plane.column() + [(True, plane.over), (True, plane.corner)]
+
+    def begin(self, plane, refs, sends, copies):
+        pass
+
+    def tick(self):
+        if self.steps:
+            self.steps.pop(0)()
+
+    def drain(self):
+        while self.steps:
+            self.tick()
+
+    def finish(self):
+        pass
+
+
+class Nothing(Paced):
+    def partners(self, plane):
+        return []
+
+
+class Fetch(Paced):
+    def __init__(self, layer, weights, together=1, lag=2):
+        super().__init__()
+        self.layer, self.weights, self.together, self.lag = (layer, weights, together, lag)
+
+    def declare(self, inputs, outputs, scratch):
+        levels = lax.axis_size("dp") // 2
+        for which, shard in self.weights.items():
+            inputs[f"shard{which}"] = (shard, HBM)
+            outputs[f"slice{which}"] = (slice_shape(which, shard.shape, 2 * levels), LOW, HBM)
+        count = len(self.weights)
+        scratch["column_sems"] = pltpu.SemaphoreType.DMA((count, levels))
+        scratch["cross_sems"] = pltpu.SemaphoreType.DMA((count, levels))
+        return (count * 3 * levels, count)
+
+    def begin(self, plane, refs, sends, copies):
+        self.plane, self.refs, self.sends, self.copies = (plane, refs, sends, copies)
+        spreads, hands = ([], [])
+        for number, which in enumerate(self.weights):
+            for step in range(plane.levels - 1, -1, -1):
+                spreads.append(partial(self.spread, number, which, step))
+                hands.append(partial(self.hand_over, number, which, step))
+        moments = [[] for _ in range(len(spreads) + self.lag)]
+        for at, (spread, hand) in enumerate(zip(spreads, hands)):
+            moments[at].append(spread)
+            moments[at + self.lag].append(hand)
+        for at in range(0, len(moments), self.together):
+            acts = [act for moment in moments[at : at + self.together] for act in moment]
+            self.steps.append(lambda acts=acts: [act() for act in acts])
+        self.tick()
+
+    def ends(self, which):
+        return getattr(self.refs, f"shard{which}"), getattr(self.refs, f"slice{which}")
+
+    def spread(self, number, which, step):
+        plane, refs = (self.plane, self.refs)
+        shard, part = self.ends(which)
+        members = 2 * plane.levels
+        owner = plane.core == self.layer
+        target = piece_of_slice(which, part, plane.z * 2 + plane.x, members)
+        zz = lax.rem(plane.z + step, plane.levels)
+        for other in (0, 1):
+            core = 1 - plane.core if other else plane.core
+            source = piece_of_shard(which, shard, zz * 2 + core, members)
+            if step or other:
+                self.sends.start(
+                    owner,
+                    source,
+                    target,
+                    refs.column_sems.at[number, plane.z],
+                    device(core, zz, plane.x, plane.y),
+                )
+            else:
+                self.copies.start(source, target, owner)
+
+    def hand_over(self, number, which, step):
+        plane, refs = (self.plane, self.refs)
+        shard, part = self.ends(which)
+        members = 2 * plane.levels
+        zz = lax.rem(plane.z - step + plane.levels, plane.levels)
+        held = piece_of_slice(which, part, zz * 2 + plane.x, members)
+        arrived = refs.column_sems.at[number, zz]
+        cross = refs.cross_sems.at[number, zz]
+        if step:
+            await_block(held, arrived, plane.over)
+            self.sends.start(True, held, held, cross, plane.over)
+        else:
+            owner = plane.core == self.layer
+            source = piece_of_shard(which, shard, plane.member, members)
+            guarded(jnp.logical_not(owner), partial(await_block, held, arrived, plane.over))
+            self.sends.start(jnp.logical_not(owner), held, held, cross, plane.over)
+            self.sends.start(owner, source, held, cross, plane.over)
+
+    def finish(self):
+        self.drain()
+        plane, refs = (self.plane, self.refs)
+        members = 2 * plane.levels
+        for number, which in enumerate(self.weights):
+            part = self.ends(which)[1]
+            for zz in range(plane.levels):
+                held = piece_of_slice(which, part, zz * 2 + 1 - plane.x, members)
+                await_block(held, refs.cross_sems.at[number, zz], plane.over)
+
+
+class Return(Paced):
+    def __init__(self, layer, weights, lag=1):
+        super().__init__()
+        self.layer, self.weights, self.lag = (layer, weights, lag)
+
+    def declare(self, inputs, outputs, scratch):
+        levels = lax.axis_size("dp") // 2
+        for which, part in self.weights.items():
+            inputs[f"slice{which}"] = (part, VMEM)
+            shape = shard_shape(which, part.shape, 2 * levels)
+            outputs[f"shard{which}"] = (shape, LOW, HBM)
+            piece = (
+                (part.shape[0], part.shape[1] // (2 * levels))
+                if by_rows(which)
+                else (part.shape[0] // (2 * levels), part.shape[1])
+            )
+            scratch[f"landed{which}"] = pltpu.VMEM((levels,) + piece, LOW)
+        count = len(self.weights)
+        scratch["column_sems"] = pltpu.SemaphoreType.DMA((count, 2, levels))
+        scratch["cross_sems"] = pltpu.SemaphoreType.DMA((count, levels))
+        return (count * 2 * levels, count)
+
+    def ends(self, which):
+        refs = self.refs
+        return (
+            getattr(refs, f"slice{which}"),
+            getattr(refs, f"landed{which}"),
+            getattr(refs, f"shard{which}"),
+        )
+
+    def begin(self, plane, refs, sends, copies):
+        self.plane, self.refs, self.sends, self.copies = (plane, refs, sends, copies)
+        members = 2 * plane.levels
+        self.steps.extend([lambda: None] * self.lag)
+        for number, which in enumerate(self.weights):
+            part, landed, _ = self.ends(which)
+            for step in range(plane.levels - 1, -1, -1):
+                zz = lax.rem(plane.z + step, plane.levels)
+                self.sends.start(
+                    True,
+                    piece_of_slice(which, part, zz * 2 + 1 - plane.x, members),
+                    landed.at[zz],
+                    refs.cross_sems.at[number, zz],
+                    plane.over,
+                )
+                self.steps.append(partial(self.add, number, which, step))
+
+    def add(self, number, which, step):
+        plane, refs = (self.plane, self.refs)
+        part, landed, shard = self.ends(which)
+        members = 2 * plane.levels
+        here = plane.core == self.layer
+        target = piece_of_shard(which, shard, plane.member, members)
+        zz = lax.rem(plane.z + step, plane.levels)
+        held = landed.at[zz]
+        await_block(held, refs.cross_sems.at[number, zz], plane.over)
+        own = piece_of_slice(which, part, zz * 2 + plane.x, members)
+        held[...] = (held[...].astype(WIDE) + own[...].astype(WIDE)).astype(LOW)
+        self.sends.start(
+            True if step else jnp.logical_not(here),
+            held,
+            target,
+            refs.column_sems.at[number, plane.core, plane.z],
+            device(self.layer, zz, plane.x, plane.y),
+        )
+        if step == 0:
+            self.copies.start(held, target, here)
+
+    def finish(self):
+        self.drain()
+        plane, refs = (self.plane, self.refs)
+        members = 2 * plane.levels
+        here = plane.core == self.layer
+        for number, which in enumerate(self.weights):
+            shard = self.ends(which)[2]
+            for core in (0, 1):
+                for step in range(plane.levels):
+                    zz = lax.rem(plane.z + step, plane.levels)
+                    present = here if step else here & (plane.core != core)
+                    held = piece_of_shard(which, shard, zz * 2 + core, members)
+                    guarded(
+                        present,
+                        partial(
+                            await_block, held, refs.column_sems.at[number, core, zz], plane.over
+                        ),
+                    )
+
+
+class Outward(Paced):
+    def __init__(self, layers):
+        super().__init__()
+        self.layers = layers
+
+    def declare(self, inputs, outputs, scratch):
+        for layer, rows in self.layers.items():
+            inputs[f"leaving_rows{layer}"] = (rows, HBM)
+            outputs["owned_rows"] = ((2,) + rows.shape, rows.dtype, HBM)
+        scratch["outward_sems"] = pltpu.SemaphoreType.DMA((2,))
+        return (3 * len(self.layers), len(self.layers))
+
+    def begin(self, plane, refs, sends, copies):
+        self.plane, self.refs = (plane, refs)
+        for layer in self.layers:
+            source = getattr(refs, f"leaving_rows{layer}")
+            target = refs.owned_rows.at[plane.x]
+            same_core, same_x = (plane.core == layer, plane.core == plane.x)
+            other_core, other_x = (plane.core != layer, plane.core != plane.x)
+            for present, partner in (
+                (same_core & other_x, plane.over),
+                (other_core & same_x, plane.sibling),
+                (other_core & other_x, plane.corner),
+            ):
+                sends.start(present, source, target, refs.outward_sems.at[plane.x], partner)
+            copies.start(source, target, same_core & same_x)
+
+    def finish(self):
+        plane, refs = (self.plane, self.refs)
+        owner = False
+        for layer in self.layers:
+            owner = owner | (plane.core == layer)
+        for slot in (0, 1):
+            away = jnp.logical_not((plane.core == plane.x) & (plane.x == slot))
+            guarded(
+                owner & away,
+                partial(await_block, refs.owned_rows.at[slot], refs.outward_sems.at[slot], plane.over),
+            )
+
+
+class Together(Paced):
+    def __init__(self, *parts):
+        self.parts = parts
+
+    def declare(self, inputs, outputs, scratch):
+        counts = [part.declare(inputs, outputs, scratch) for part in self.parts]
+        return tuple(map(sum, zip(*counts)))
+
+    def begin(self, plane, refs, sends, copies):
+        for part in self.parts:
+            part.begin(plane, refs, sends, copies)
+
+    def tick(self):
+        for part in self.parts:
+            part.tick()
+
+    def drain(self):
+        for part in self.parts:
+            part.drain()
+
+    def finish(self):
+        for part in self.parts:
+            part.finish()
+
+
+def launch(name, ident, kernel, beside, counts, inputs, outputs, scratch):
+    inputs, outputs, scratch = (dict(inputs), dict(outputs), dict(scratch))
+    more = beside.declare(inputs, outputs, scratch)
+    scratch["send_sems"] = pltpu.SemaphoreType.DMA((counts[0] + more[0],))
+    scratch["copy_sems"] = pltpu.SemaphoreType.DMA((max(1, counts[1] + more[1]),))
+    names = list(inputs) + list(outputs) + list(scratch)
+
+    def body(*refs):
+        held = SimpleNamespace(**dict(zip(names, refs)))
+        plane = Plane()
+        partners = plane.neighbours()
+        if not isinstance(beside, Nothing):
+            partners = [(True, plane.across)] + beside.partners(plane)
+        greeting = Greeting(partners)
+        sends, copies = (Sends(held.send_sems), Copies(held.copy_sems))
+        kernel(held, plane, greeting, sends, copies)
+        beside.finish()
+        copies.finish()
+        sends.finish()
+        assert len(sends.pending) == counts[0] + more[0], len(sends.pending)
+        assert len(copies.pending) == counts[1] + more[1], len(copies.pending)
+
+    results = pl.pallas_call(
+        body,
+        out_shape=[jax.ShapeDtypeStruct(shape, dtype) for shape, dtype, _ in outputs.values()],
+        in_specs=[pl.BlockSpec(memory_space=space) for _, space in inputs.values()],
+        out_specs=[pl.BlockSpec(memory_space=space) for _, _, space in outputs.values()],
+        scratch_shapes=list(scratch.values()),
+        compiler_params=pltpu.CompilerParams(
+            collective_id=ident, has_side_effects=True, vmem_limit_bytes=56 << 20
+        ),
+        name=name,
+    )(*[array for array, _ in inputs.values()])
+    return SimpleNamespace(**dict(zip(outputs, results)))
+
+
+def sizes():
+    levels = lax.axis_size("dp") // 2
+    return levels, 4 * levels
+
+
+CHUNKS = 2
+
+
+def opening(ident, boundary, packed, beside):
+    levels, blocks = sizes()
+    rows, width = boundary.shape[1:]
+    lines, lanes = packed.shape
+
+    def kernel(refs, plane, greeting, sends, copies):
+        core, x = (plane.core, plane.x)
+        block = plane.block * 2 + x
+        refs.small[span(block, lines)] = refs.packed[...]
+        greeting.wait()
+        own_small = refs.small.at[span(block, lines)]
+        sends.start(True, own_small, own_small, refs.pair_sem.at[0], plane.over)
+        for slot in (0, 1):
+            source, target = (refs.boundary.at[slot], refs.landed_planes.at[core])
+            arrived = refs.inward_sems.at[core]
+            for present, partner in (
+                ((x == core) & (slot != x), plane.over),
+                ((x != core) & (slot == x), plane.sibling),
+                ((x != core) & (slot != x), plane.corner),
+            ):
+                sends.start(present, source, target, arrived, partner)
+            copies.start(source, target, (x == core) & (slot == x))
+        beside.begin(plane, refs, sends, copies)
+        other_small = refs.small.at[span(plane.block * 2 + 1 - x, lines)]
+        await_block(other_small, refs.pair_sem.at[0], plane.over)
+        small = Gather(plane, sends, refs.small, refs.small_sems)
+        small.open()
+        small.run(lambda step, zz: None, lambda: None)
+        refs.vectors[...] = refs.small[...]
+        for slot in (0, 1):
+            here = (core == x) & (core == slot)
+            guarded(
+                jnp.logical_not(here),
+                partial(await_block, refs.landed_planes.at[slot], refs.inward_sems.at[slot], plane.over),
+            )
+        copies.wait(0)
+        copies.wait(1)
+        refs.planes[...] = refs.landed_planes[...]
+        refs.rows[span(plane.block, rows)] = refs.landed_planes[1]
+        gather = Gather(plane, sends, refs.rows, refs.gather_sems)
+        gather.open()
+
+        def keep(step, zz):
+            group = span(zz, 4 * rows)
+            copies.start(refs.rows.at[group], refs.gathered.at[group])
+
+        gather.run(keep, beside.tick)
+
+    return launch(
+        "opening",
+        ident,
+        kernel,
+        beside,
+        (7 + Gather.count(levels, 1) + Gather.count(levels, CHUNKS), 2 + levels),
+        {"boundary": (boundary, HBM), "packed": (packed, VMEM)},
+        {
+            "planes": ((2, rows, width), LOW, VMEM),
+            "gathered": ((blocks * rows, width), LOW, HBM),
+            "vectors": ((2 * blocks * lines, lanes), LOW, VMEM),
+        },
+        gather_scratch(rows, width, levels, CHUNKS)
+        | {
+            "small": pltpu.VMEM((2 * blocks * lines, lanes), LOW),
+            "small_sems": pltpu.SemaphoreType.DMA((blocks, 1)),
+            "pair_sem": pltpu.SemaphoreType.DMA((1,)),
+            "inward_sems": pltpu.SemaphoreType.DMA((2,)),
+            "landed_planes": pltpu.VMEM((2, rows, width), LOW),
+        },
+    )
+
+
+def visible(refs, group, size, tokens):
+    segment = refs.query_segment[group]
+    place = group.start + lax.broadcasted_iota(jnp.int32, (size, tokens), 0)
+    keys = lax.broadcasted_iota(jnp.int32, (size, tokens), 1)
+    return (segment == refs.key_segment[...]) & (keys <= place)
+
+
+def attention_forward(ident, beside, entering, gains, biases, b_qv, segments, w_qkv, w_out):
+    levels, blocks = sizes()
+    rows, width = entering.shape
+    tokens, size = (blocks * rows, 4 * rows)
+    scaling = HD ** (-0.5)
+
+    def kernel(refs, plane, greeting, sends, copies):
+        first = copies.start(refs.w_qkv, refs.own_qkv)
+        second = copies.start(refs.w_out, refs.own_out)
+        hidden = refs.entering[...].astype(WIDE)
+        normed, _, _ = layer_norm(hidden, refs.gains[0:1], refs.biases[0:1])
+        refs.rows[span(plane.block, rows)] = normed.astype(LOW)
+        greeting.wait()
+        gather = Gather(plane, sends, refs.rows, refs.gather_sems)
+        gather.open()
+        beside.begin(plane, refs, sends, copies)
+        copies.wait(first)
+
+        def project(step, zz):
+            group = span(zz, size)
+            projected = dot(refs.rows[group], refs.own_qkv[...])
+            refs.queries[group] = (projected[:, :HD] + refs.b_qv[0:1]).astype(LOW)
+            refs.keys[group] = projected[:, HD : 2 * HD].astype(LOW)
+            refs.values[group] = (projected[:, 2 * HD :] + refs.b_qv[1:2]).astype(LOW)
+            copies.start(refs.rows.at[group], refs.rows_a.at[group])
+
+        gather.run(project, beside.tick)
+        copies.wait(second)
+
+        def make(step, zz):
+            group = span(zz, size)
+            allowed = visible(refs, group, size, tokens)
+            scores = dot_back(refs.queries[group], refs.keys[...]) * scaling
+            scores = jnp.where(allowed, scores, NEG_FILL)
+            top = jnp.max(scores, axis=-1, keepdims=True)
+            raised = jnp.exp(scores - top)
+            total = jnp.sum(raised, axis=-1, keepdims=True)
+            refs.log_total[group] = top + jnp.log(total)
+            probs = (raised / total).astype(LOW)
+            live = (refs.query_segment[group] >= 0).astype(WIDE)
+            mixed = (dot(probs, refs.values[...]) * live).astype(LOW)
+            refs.mixed[group] = mixed
+            for cut in range(0, width, 512):
+                refs.part[group, cut : cut + 512] = dot(
+                    mixed, refs.own_out[:, cut : cut + 512]
+                ).astype(LOW)
+
+        Scatter(plane, sends, refs, refs.sum).run(make, beside.tick)
+        refs.middle[...] = refs.entering[...].astype(WIDE) + refs.sum[...] + refs.biases[1:2]
+
+    head = ((tokens, HD), LOW, VMEM)
+    return launch(
+        f"attention_forward{ident}",
+        ident,
+        kernel,
+        beside,
+        (Gather.count(levels, CHUNKS) + Scatter.count(levels), 2 + levels),
+        {
+            "entering": (entering, VMEM),
+            "gains": (gains, VMEM),
+            "biases": (biases, VMEM),
+            "b_qv": (b_qv, VMEM),
+            "query_segment": (segments[0], VMEM),
+            "key_segment": (segments[1], VMEM),
+            "w_qkv": (w_qkv, HBM),
+            "w_out": (w_out, HBM),
+        },
+        {
+            "middle": ((rows, width), WIDE, VMEM),
+            "rows_a": ((tokens, width), LOW, HBM),
+            "queries": head,
+            "keys": head,
+            "values": head,
+            "mixed": head,
+            "log_total": ((tokens, 1), WIDE, VMEM),
+        },
+        gather_scratch(rows, width, levels, CHUNKS)
+        | scatter_scratch(rows, width, levels)
+        | {"own_qkv": pltpu.VMEM(w_qkv.shape, LOW), "own_out": pltpu.VMEM(w_out.shape, LOW)},
+    )
+
+
+def feed_forward(ident, beside, middle, gains, biases, b_up, w_up, w_down):
+    levels, blocks = sizes()
+    rows, width = middle.shape
+    tokens, size = (blocks * rows, 4 * rows)
+    units = w_up.shape[1]
+
+    def kernel(refs, plane, greeting, sends, copies):
+        first = copies.start(refs.w_up, refs.own_up)
+        second = copies.start(refs.w_down, refs.own_down)
+        normed, _, _ = layer_norm(refs.middle[...], refs.gains[1:2], refs.biases[2:3])
+        refs.rows[span(plane.block, rows)] = normed.astype(LOW)
+        greeting.wait()
+        gather = Gather(plane, sends, refs.rows, refs.gather_sems)
+        gather.open()
+        beside.begin(plane, refs, sends, copies)
+        copies.wait(first)
+
+        def expand(step, zz):
+            group = span(zz, size)
+            preact = dot(refs.rows[group], refs.own_up[...]) + refs.b_up[...]
+            refs.preact[group] = preact
+            refs.activated[group] = (
+                0.5 * preact * (1.0 + lax.erf(preact * math.sqrt(0.5)))
+            ).astype(LOW)
+            copies.start(refs.rows.at[group], refs.rows_b.at[group])
+
+        gather.run(expand, beside.tick)
+        copies.wait(second)
+
+        def make(step, zz):
+            group = span(zz, size)
+            for cut in range(0, width, 512):
+                refs.part[group, cut : cut + 512] = dot(
+                    refs.activated[group], refs.own_down[:, cut : cut + 512]
+                ).astype(LOW)
+
+        Scatter(plane, sends, refs, refs.sum).run(make, beside.tick)
+        result = refs.middle[...] + refs.sum[...] + refs.biases[3:4]
+        refs.leaving[...] = result.astype(LOW)
+
+    return launch(
+        f"feed_forward{ident}",
+        ident,
+        kernel,
+        beside,
+        (Gather.count(levels, CHUNKS) + Scatter.count(levels), 2 + levels),
+        {
+            "middle": (middle, VMEM),
+            "gains": (gains, VMEM),
+            "biases": (biases, VMEM),
+            "b_up": (b_up, VMEM),
+            "w_up": (w_up, HBM),
+            "w_down": (w_down, HBM),
+        },
+        {
+            "leaving": ((rows, width), LOW, VMEM),
+            "rows_b": ((tokens, width), LOW, HBM),
+            "preact": ((tokens, units), WIDE, VMEM),
+            "activated": ((tokens, units), LOW, VMEM),
+        },
+        gather_scratch(rows, width, levels, CHUNKS)
+        | scatter_scratch(rows, width, levels)
+        | {"own_up": pltpu.VMEM(w_up.shape, LOW), "own_down": pltpu.VMEM(w_down.shape, LOW)},
+    )
+
+
+def feed_backward(ident, beside, grad, gathered, middle, gains, w_up, w_down, rows_b, preact, activated):
+    levels, blocks = sizes()
+    rows, width = middle.shape
+    tokens, size = (blocks * rows, 4 * rows)
+    units = w_up.shape[1]
+
+    def kernel(refs, plane, greeting, sends, copies):
+        loads = [copies.start(refs.w_down, refs.own_down), copies.start(refs.preact, refs.own_preact)]
+        if gathered is not None:
+            loads.append(copies.start(refs.gathered, refs.rows))
+        late = [copies.start(refs.w_up, refs.own_up)]
+        last = [
+            copies.start(refs.activated, refs.own_activated),
+            copies.start(refs.rows_b, refs.own_rows_b),
+        ]
+        low = refs.grad[...].astype(LOW)
+        if gathered is None:
+            refs.rows[span(plane.block, rows)] = low
+        refs.down_bias[...] = jnp.sum(low.astype(WIDE), axis=0, keepdims=True)
+        refs.up_bias[...] = jnp.zeros_like(refs.up_bias)
+        greeting.wait()
+        if gathered is None:
+            gather = Gather(plane, sends, refs.rows, refs.gather_sems)
+            gather.open()
+        beside.begin(plane, refs, sends, copies)
+        for number in loads:
+            copies.wait(number)
+
+        def shrink(step, zz):
+            group = span(zz, size)
+            grad_act = dot_back(refs.rows[group], refs.own_down[...])
+            value = refs.own_preact[group]
+            slope = 0.5 * (1.0 + lax.erf(value * math.sqrt(0.5))) + value * jnp.exp(
+                -0.5 * value * value
+            ) * (1.0 / math.sqrt(2.0 * math.pi))
+            grad_pre = (grad_act * slope).astype(LOW)
+            refs.grad_pre[group] = grad_pre
+            refs.up_bias[...] += jnp.sum(grad_pre.astype(WIDE), axis=0, keepdims=True)
+
+        if gathered is None:
+            gather.run(shrink, beside.tick)
+        for number in late:
+            copies.wait(number)
+
+        def make(step, zz):
+            group = span(zz, size)
+            if gathered is not None:
+                shrink(step, zz)
+            for cut in range(0, width, 512):
+                refs.part[group, cut : cut + 512] = dot_back(
+                    refs.grad_pre[group], refs.own_up[cut : cut + 512]
+                ).astype(LOW)
+
+        def down_product(at, carry):
+            cut = span(at, 128)
+            refs.down_grad[cut] = dot_rows(refs.own_activated[:, cut], refs.rows[...]).astype(LOW)
+            return carry
+
+        def up_product(at, carry):
+            cut = span(at, 256)
+            refs.up_grad[cut] = dot_rows(refs.own_rows_b[:, cut], refs.grad_pre[...]).astype(LOW)
+            return carry
+
+        def fill(at):
+            if at == 0:
+                for number in last:
+                    copies.wait(number)
+            if at == 1:
+                lax.fori_loop(0, units // 128, down_product, 0)
+            if at == 2:
+                lax.fori_loop(0, width // 512, up_product, 0)
+            if at == 3:
+                lax.fori_loop(width // 512, width // 256, up_product, 0)
+
+        Scatter(plane, sends, refs, refs.sum).run(make, beside.tick, fill)
+        _, unit, inverse = layer_norm(refs.middle[...], refs.gains[1:2], refs.gains[1:2])
+        refs.gain_grad[...] = jnp.sum(refs.sum[...] * unit, axis=0, keepdims=True)
+        refs.shift_grad[...] = jnp.sum(refs.sum[...], axis=0, keepdims=True)
+        refs.grad_middle[...] = refs.grad[...].astype(WIDE) + norm_back(
+            refs.sum[...], unit, inverse, refs.gains[1:2]
+        )
+
+    line = ((1, width), WIDE, VMEM)
+    inputs = {
+        "grad": (grad, VMEM),
+        "middle": (middle, VMEM),
+        "gains": (gains, VMEM),
+        "w_up": (w_up, HBM),
+        "w_down": (w_down, HBM),
+        "rows_b": (rows_b, HBM),
+        "preact": (preact, HBM),
+        "activated": (activated, HBM),
+    }
+    if gathered is not None:
+        inputs["gathered"] = (gathered, HBM)
+    return launch(
+        f"feed_backward{ident}",
+        ident,
+        kernel,
+        beside,
+        ((0 if gathered is not None else Gather.count(levels, CHUNKS)) + Scatter.count(levels), 5 + (gathered is not None)),
+        inputs,
+        {
+            "grad_middle": ((rows, width), WIDE, VMEM),
+            "up_grad": (w_up.shape, LOW, VMEM),
+            "down_grad": (w_down.shape, LOW, VMEM),
+            "up_bias": ((1, units), WIDE, VMEM),
+            "gain_grad": line,
+            "shift_grad": line,
+            "down_bias": line,
+        },
+        gather_scratch(rows, width, levels, CHUNKS)
+        | scatter_scratch(rows, width, levels)
+        | {
+            "own_up": pltpu.VMEM(w_up.shape, LOW),
+            "own_down": pltpu.VMEM(w_down.shape, LOW),
+            "own_preact": pltpu.VMEM((tokens, units), WIDE),
+            "own_activated": pltpu.VMEM((tokens, units), LOW),
+            "own_rows_b": pltpu.VMEM((tokens, width), LOW),
+            "grad_pre": pltpu.VMEM((tokens, units), LOW),
+        },
+    )
+
+
+def attention_backward(ident, beside, grad_middle, entering, gains, segments, w_qkv, w_out, kept):
+    levels, blocks = sizes()
+    rows, width = entering.shape
+    tokens, size = (blocks * rows, 4 * rows)
+    scaling = HD ** (-0.5)
+
+    def kernel(refs, plane, greeting, sends, copies):
+        loads = [copies.start(refs.w_out, refs.own_out)]
+        late = [copies.start(refs.w_qkv, refs.own_qkv), copies.start(refs.rows_a, refs.own_rows_a)]
+        low = refs.grad_middle[...].astype(LOW)
+        refs.rows[span(plane.block, rows)] = low
+        refs.out_bias[...] = jnp.sum(low.astype(WIDE), axis=0, keepdims=True)
+        refs.grad_keys[...] = jnp.zeros_like(refs.grad_keys)
+        refs.grad_values[...] = jnp.zeros_like(refs.grad_values)
+        greeting.wait()
+        gather = Gather(plane, sends, refs.rows, refs.gather_sems)
+        gather.open()
+        beside.begin(plane, refs, sends, copies)
+        for number in loads:
+            copies.wait(number)
+
+        def attend_group(step, zz):
+            group = span(zz, size)
+            live = (refs.query_segment[group] >= 0).astype(WIDE)
+            grad_mixed = (dot_back(refs.rows[group], refs.own_out[...]).astype(LOW) * live).astype(LOW)
+            allowed = visible(refs, group, size, tokens)
+            queries = refs.queries[group]
+            scores = dot_back(queries, refs.keys[...]) * scaling
+            scores = jnp.where(allowed, scores, NEG_FILL)
+            probs = jnp.exp(scores - refs.log_total[group])
+            grad_probs = dot_back(grad_mixed, refs.values[...])
+            delta = jnp.sum(probs * grad_probs, axis=-1, keepdims=True)
+            grad_scores = jnp.where(allowed, probs * (grad_probs - delta), 0.0).astype(LOW)
+            refs.grad_proj[group, :HD] = (dot(grad_scores, refs.keys[...]) * scaling).astype(LOW)
+            refs.grad_keys[...] += dot_rows(grad_scores, queries)
+            refs.grad_values[...] += dot_rows(probs.astype(LOW), grad_mixed)
+
+        gather.run(attend_group, beside.tick)
+        refs.grad_proj[:, HD : 2 * HD] = (refs.grad_keys[...] * scaling).astype(LOW)
+        refs.grad_proj[:, 2 * HD :] = refs.grad_values[...].astype(LOW)
+        for number in late:
+            copies.wait(number)
+
+        def make(step, zz):
+            group = span(zz, size)
+            for cut in range(0, width, 512):
+                refs.part[group, cut : cut + 512] = dot_back(
+                    refs.grad_proj[group], refs.own_qkv[cut : cut + 512]
+                ).astype(LOW)
+
+        def qkv_product(at, carry):
+            cut = span(at, 256)
+            refs.qkv_grad[cut] = dot_rows(refs.own_rows_a[:, cut], refs.grad_proj[...]).astype(LOW)
+            return carry
+
+        def fill(at):
+            if at == 0:
+                proj_sums = jnp.sum(refs.grad_proj[...].astype(WIDE), axis=0, keepdims=True)
+                refs.qv_grad[0:1] = proj_sums[:, :HD]
+                refs.qv_grad[1:2] = proj_sums[:, 2 * HD :]
+            if at == 1:
+                refs.out_grad[...] = dot_rows(refs.mixed[...], refs.rows[...]).astype(LOW)
+            if at == 2:
+                lax.fori_loop(0, width // 512, qkv_product, 0)
+            if at == 3:
+                lax.fori_loop(width // 512, width // 256, qkv_product, 0)
+
+        Scatter(plane, sends, refs, refs.sum).run(make, beside.tick, fill)
+        hidden = refs.entering[...].astype(WIDE)
+        _, unit, inverse = layer_norm(hidden, refs.gains[0:1], refs.gains[0:1])
+        refs.gain_grad[...] = jnp.sum(refs.sum[...] * unit, axis=0, keepdims=True)
+        refs.shift_grad[...] = jnp.sum(refs.sum[...], axis=0, keepdims=True)
+        refs.grad_in[...] = refs.grad_middle[...] + norm_back(
+            refs.sum[...], unit, inverse, refs.gains[0:1]
+        )
+
+    line = ((1, width), WIDE, VMEM)
+    return launch(
+        f"attention_backward{ident}",
+        ident,
+        kernel,
+        beside,
+        (Gather.count(levels, CHUNKS) + Scatter.count(levels), 3),
+        {
+            "grad_middle": (grad_middle, VMEM),
+            "entering": (entering, VMEM),
+            "gains": (gains, VMEM),
+            "query_segment": (segments[0], VMEM),
+            "key_segment": (segments[1], VMEM),
+            "w_qkv": (w_qkv, HBM),
+            "w_out": (w_out, HBM),
+            "rows_a": (kept.rows_a, HBM),
+            "queries": (kept.queries, VMEM),
+            "keys": (kept.keys, VMEM),
+            "values": (kept.values, VMEM),
+            "mixed": (kept.mixed, VMEM),
+            "log_total": (kept.log_total, VMEM),
+        },
+        {
+            "grad_in": ((rows, width), WIDE, VMEM),
+            "qkv_grad": (w_qkv.shape, LOW, VMEM),
+            "out_grad": (w_out.shape, LOW, VMEM),
+            "qv_grad": ((2, HD), WIDE, VMEM),
+            "gain_grad": line,
+            "shift_grad": line,
+            "out_bias": line,
+        },
+        gather_scratch(rows, width, levels, CHUNKS)
+        | scatter_scratch(rows, width, levels)
+        | {
+            "own_qkv": pltpu.VMEM(w_qkv.shape, LOW),
+            "own_out": pltpu.VMEM(w_out.shape, LOW),
+            "own_rows_a": pltpu.VMEM((tokens, width), LOW),
+            "grad_proj": pltpu.VMEM((tokens, 3 * HD), LOW),
+            "grad_keys": pltpu.VMEM((tokens, HD), WIDE),
+            "grad_values": pltpu.VMEM((tokens, HD), WIDE),
+        },
+    )
+
+
+VECTOR_LINES = 8
+
+
+def closing(ident, beside, vectors):
+    levels, blocks = sizes()
+    members = 2 * levels
+    lines = (2 + members) * VECTOR_LINES
+    inputs = {}
+    for layer, (norms, heads, units) in enumerate(vectors):
+        for at, line in enumerate(norms):
+            inputs[f"norm{layer}{at}"] = (line, VMEM)
+        inputs[f"heads{layer}"] = (heads, VMEM)
+        inputs[f"units{layer}"] = (units, VMEM)
+    count, unit_lines = (len(vectors[0][0]), vectors[0][2].shape[1] // HD)
+
+    def kernel(refs, plane, greeting, sends, copies):
+        refs.part[...] = jnp.zeros_like(refs.part)
+        for layer in (0, 1):
+            for z in range(levels):
+                for y in (0, 1):
+                    base = (z * 4 + layer * 2 + y) * lines
+                    for x in (0, 1):
+                        cut = (z * 4 + x * 2 + y) * HD
+                        for at in range(count):
+                            line = base + x * VECTOR_LINES + at
+                            refs.part[line : line + 1] = getattr(refs, f"norm{layer}{at}")[
+                                :, cut : cut + HD
+                            ]
+            own = [getattr(refs, f"heads{layer}")[...]]
+            for at in range(unit_lines):
+                own.append(getattr(refs, f"units{layer}")[:, at * HD : (at + 1) * HD])
+            own.append(jnp.zeros((VECTOR_LINES - 2 - unit_lines, HD), WIDE))
+            refs.own[layer] = jnp.concatenate(own, axis=0)
+            for z in range(levels):
+                start = (z * 4 + layer * 2 + plane.y) * lines + (2 + plane.member) * VECTOR_LINES
+                refs.part[pl.ds(pl.multiple_of(start, VECTOR_LINES), VECTOR_LINES)] = refs.own[layer]
+        greeting.wait()
+        beside.begin(plane, refs, sends, copies)
+        Scatter(plane, sends, refs, refs.sum).run(lambda step, zz: None, beside.tick)
+        beside.drain()
+        sends.start(True, refs.sum, refs.other, refs.pair_sem.at[0], plane.over)
+        await_block(refs.other, refs.pair_sem.at[0], plane.over)
+        refs.vectors[...] = refs.sum[...] + refs.other[...]
+
+    return launch(
+        "closing",
+        ident,
+        kernel,
+        beside,
+        (Scatter.count(levels) + 1, 0),
+        inputs,
+        {"vectors": ((lines, HD), WIDE, VMEM)},
+        scatter_scratch(lines, HD, levels, WIDE)
+        | {
+            "own": pltpu.VMEM((2, VECTOR_LINES, HD), WIDE),
+            "other": pltpu.VMEM((lines, HD), WIDE),
+            "pair_sem": pltpu.SemaphoreType.DMA((1,)),
+        },
+    )
+
+
+def plane_body(
+    boundary,
+    doc_lengths,
+    qkv_weight,
+    qv_bias,
+    out_weight,
+    up_weight,
+    up_bias,
+    down_weight,
+    norm_gains,
+    norm_biases,
+):
+    plane = Plane()
+    levels, y, member = (plane.levels, plane.y, plane.member)
+    members = 2 * levels
+    width = boundary.shape[3]
+    heads_shard = qv_bias.shape[2]
+    head_cut = qv_bias.shape[3]
+    block_shard = up_bias.shape[1]
+    own_blocks = block_shard // members
+
+    pieces = (qv_bias[0], up_bias[0], norm_gains[0], norm_biases[0])
+    packed = jnp.concatenate([piece.reshape(-1) for piece in pieces])
+    lines = 16 * -(-packed.size // (16 * HD))
+    packed = jnp.pad(packed, (0, lines * HD - packed.size)).reshape(lines, HD)
+    depth = qkv_weight.shape[1]
+    by_head = (
+        qkv_weight[0]
+        .reshape(depth, 3, members, HD)
+        .transpose(0, 2, 1, 3)
+        .reshape(depth, members * 3 * HD)
+    )
+    attention_shards = {0: by_head, 1: out_weight[0]}
+    feed_shards = {2: up_weight[0], 3: down_weight[0]}
+    start = opening(1, boundary[0], packed, Fetch(0, attention_shards, together=2, lag=3))
+    planes = start.planes
+    shared = start.vectors.reshape(levels, 2, 2, 2, -1).transpose(1, 0, 3, 2, 4)
+    shared = shared.reshape(2, members, 2, -1)
+    cuts = [0]
+    for piece in pieces:
+        cuts.append(cuts[-1] + piece.size)
+    plane_part = lax.dynamic_index_in_dim(shared, y, 2, keepdims=False)
+    qv = plane_part[:, :, cuts[0] : cuts[1]].reshape(2, members, 2, heads_shard, head_cut)
+    qv = lax.dynamic_index_in_dim(qv, member, 3, keepdims=False)
+    b_qv = qv.transpose(0, 2, 1, 3).reshape(2, 2, HD).astype(WIDE)
+    ub = plane_part[:, :, cuts[1] : cuts[2]].reshape(2, members, block_shard, head_cut)
+    ub = lax.dynamic_slice_in_dim(ub, member * own_blocks, own_blocks, axis=2)
+    b_up = ub.transpose(0, 2, 1, 3).reshape(2, 1, own_blocks * HD).astype(WIDE)
+    gains = (
+        shared[..., cuts[2] : cuts[3]].reshape(2, members * 2, 2, -1).transpose(0, 2, 1, 3)
+    ).reshape(2, 2, width).astype(WIDE)
+    biases = (
+        shared[..., cuts[3] : cuts[4]].reshape(2, members * 2, 4, -1).transpose(0, 2, 1, 3)
+    ).reshape(2, 4, width).astype(WIDE)
+
+    lengths = lax.dynamic_index_in_dim(doc_lengths, plane.x, 0, keepdims=False)
+    tokens = boundary.shape[2] * 4 * levels
+    _, segment, live, _, _, _ = visibility(lengths, 0, tokens, tokens)
+    segments = (jnp.where(live, segment, -1)[:, None], segment[None, :])
+
+    entering = planes[0]
+    att0 = attention_forward(
+        2, Fetch(0, feed_shards), entering, gains[0], biases[0], b_qv[0], segments, start.slice0, start.slice1
+    )
+    ffn0 = feed_forward(
+        3, Fetch(1, attention_shards), att0.middle, gains[0], biases[0], b_up[0], att0.slice2, att0.slice3
+    )
+    att1 = attention_forward(
+        4, Fetch(1, feed_shards), ffn0.leaving, gains[1], biases[1], b_qv[1], segments, ffn0.slice0, ffn0.slice1
+    )
+    ffn1 = feed_forward(
+        5, Nothing(), att1.middle, gains[1], biases[1], b_up[1], att1.slice2, att1.slice3
+    )
+    back1 = feed_backward(
+        6, Outward({0: ffn0.leaving, 1: ffn1.leaving}), planes[1], start.gathered, att1.middle, gains[1],
+        att1.slice2, att1.slice3, ffn1.rows_b, ffn1.preact, ffn1.activated,
+    )
+    wards1 = attention_backward(
+        7, Return(1, {2: back1.up_grad, 3: back1.down_grad}), back1.grad_middle, ffn0.leaving, gains[1],
+        segments, ffn0.slice0, ffn0.slice1, att1,
+    )
+    back0 = feed_backward(
+        8,
+        Together(
+            Outward({1: wards1.grad_in}),
+            Return(1, {0: wards1.qkv_grad, 1: wards1.out_grad}),
+        ),
+        wards1.grad_in.astype(LOW), None, att0.middle,
+        gains[0], att0.slice2, att0.slice3, ffn0.rows_b, ffn0.preact, ffn0.activated,
+    )
+    wards0 = attention_backward(
+        9, Return(0, {2: back0.up_grad, 3: back0.down_grad}), back0.grad_middle, entering, gains[0],
+        segments, start.slice0, start.slice1, att0,
+    )
+    vectors = [
+        (
+            (
+                attend.gain_grad,
+                feed.gain_grad,
+                attend.shift_grad,
+                attend.out_bias,
+                feed.shift_grad,
+                feed.down_bias,
+            ),
+            attend.qv_grad,
+            feed.up_bias,
+        )
+        for attend, feed in ((wards0, back0), (wards1, back1))
+    ]
+    end = closing(
+        10,
+        Together(
+            Return(0, {0: wards0.qkv_grad, 1: wards0.out_grad}, lag=0), Outward({0: wards0.grad_in})
+        ),
+        vectors,
+    )
+    summed = end.vectors.reshape(2 + members, VECTOR_LINES, HD)
+    norms = lax.dynamic_index_in_dim(summed, plane.x, 0, keepdims=False)
+    by_member = lax.dynamic_slice_in_dim(
+        summed[2:], (plane.z * 2 + plane.x) * head_cut, head_cut, axis=2
+    )
+    own_lines = 2 + own_blocks
+
+    def owned(first, second):
+        return jnp.where(plane.core == 0, first, second).astype(WIDE)
+
+    qkv_shard = (
+        owned(end.shard0, back0.shard0)
+        .reshape(depth, members, 3, HD)
+        .transpose(0, 2, 1, 3)
+        .reshape(depth, 3, members * HD)
+    )
+    return (
+        back1.owned_rows[None],
+        owned(end.owned_rows, back0.owned_rows)[None],
+        qkv_shard[None],
+        by_member[:, :2].transpose(1, 0, 2)[None],
+        owned(end.shard1, back0.shard1)[None],
+        owned(wards0.shard2, wards1.shard2)[None],
+        by_member[:, 2:own_lines].reshape(1, block_shard, head_cut),
+        owned(wards0.shard3, wards1.shard3)[None],
+        norms[None, :2],
+        norms[None, 2:6],
+    )
+
+
+def fits_plane(mesh):
+    return mesh.shape["dp"] == 8 and mesh.shape["tensor"] == 2 and mesh.shape["section"] == 2
+
+
 def solution(mesh):
     placed = (
         P("section", None, ("dp", "tensor"), None),
@@ -467,7 +1824,7 @@
         P("section", None, ("dp", "tensor")),
     )
     return jax.shard_map(
-        body,
+        plane_body if fits_plane(mesh) else body,
         mesh=mesh,
         in_specs=placed,
         out_specs=(

time: 3180 us -> 841 us (0.26)
  waiting for transfers between devices: 2330 us -> 0 us
  Pallas kernels: 0 us -> 790 us
  matrix products: 314 us -> 0 us
  blocking collectives: 246 us -> 0 us
  local copies, waits for them, and re-layouts: 157 us -> 23.7 us
  other arithmetic: 96 us -> 16.9 us
    reduce_scatter x22 -> x0, waiting for transfers between devices: 1320 us -> none  [the longest x1 283 us: reduce_grads(): lax.psum_scatter(up_grad[None].astype(jnp.bfloat16), 'dp', scatter_dimens...]
    all_gather x10 -> x0, waiting for transfers between devices: 791 us -> none  [the longest x1 217 us: fetch_weights(): lax.all_gather(down_weight[0], 'dp', axis=1, tiled=True)]
    pallas_call x0 -> x10, Pallas kernels: none -> 790 us  [launch(): pl.pallas_call(body, out_shape=[jax.ShapeDtypeStruct(shape, dtype) for sh...]
    dot_general x70 -> x0, matrix products: 314 us -> none  [the longest x3 43.4 us: backward(): jnp.einsum('rd,fd->rf', wide_branch, w_down, preferred_element_type=jnp.f...]
    all_gather x16 -> x0, blocking collectives: 246 us -> none  [the longest x12 105 us: widen(): return lax.all_gather(rows_low, 'tensor', axis=0, tiled=True)]
    unnamed x40 -> x0, waiting for transfers between devices: 221 us -> none
    unnamed x451 -> x25, local copies, waits for them, and re-layouts: 86.9 us -> 7.62 us
    reduce_sum x32 -> x0, other arithmetic: 35.9 us -> none  [the longest x3 6.51 us: backward(): out_bias_grad = jnp.sum(grad_attn.astype(jnp.float32), axis=0)]
  transfers between devices with their start and end apart: 40 -> 0, of which waited for: 33 -> 0; matrix products, arithmetic and copies ran while one was open for 8% -> 0% of each run, Pallas kernels for 0% -> 0%
where the time goes in v2:
time: 841 us; the launch traced here: 832 us
  Pallas kernels  790 us (94%)
  local copies, waits for them, and re-layouts  23.7 us (3%)
  other arithmetic  16.9 us (2%)
    pallas_call x10, Pallas kernels, launch(): pl.pallas_call(body, out_shape=[jax.ShapeDtypeStruct(shape, dtype) for sh...  790 us

profile of v2, /device:TPU:0, one launch (start us, length us, event | category | flops | bytes accessed | tf_op | source)
XLA Modules:
  0.0 831.8 jit_solution(16074483687511067218)
XLA Ops:
  3.2 1.3 fusion.23.refs_1_
  5.8 1.0 fusion.5.refs_4_.refs_3_
  6.8 1.7 copy.38
  8.7 1.7 copy.40.refs_2_.refs_6_
  10.4 74.7 %opening.1 = (bf16[2,64,2048]{2,1,0:T(8,128)(2,1)}, bf16[1024,2048]{1,0:T(8,128)(2,1)}, bf16[512,128]{1,0:T(8,128)(2,1)}, bf16[2048,384]{1,0:T(8,128)(2,1)}, bf16[128,2048]{1,0:T(8,128)(2,1)}) custom-call(bf16[2,64,2048]{2,1,0:T(8,128)(2,1)} %bitcast.90, bf16[16,128]{1,0:T(8,128)(2,1)} %fusion.23.refs_1_, bf16[256,3072]{1,0:T(8,128)(2,1)} %copy.40.refs_2_.refs_6_, ...), custom_call_target="tpu_custom_call" | custom-call | tf_op jit(solution)/shard_map/opening/pallas_call | solution.py:1110
  85.1 1.9 slice_bitcast_fusion
  92.6 97.4 %attention_forward2.1 = (f32[64,2048]{1,0:T(8,128)}, bf16[1024,2048]{1,0:T(8,128)(2,1)}, bf16[1024,128]{1,0:T(8,128)(2,1)}, bf16[1024,128]{1,0:T(8,128)(2,1)}, b...) custom-call(bf16[64,2048]{1,0:T(8,128)(2,1)} %get-tuple-element.176., ...), custom_call_target="tpu_custom_call" | custom-call | tf_op jit(solution)/shard_map/attention_forward2/pallas_call | solution.py:1110
  190.1 86.5 %feed_forward3.1 = (bf16[64,2048]{1,0:T(8,128)(2,1)}, bf16[1024,2048]{1,0:T(8,128)(2,1)}, f32[1024,512]{1,0:T(8,128)}, bf16[1024,512]{1,0:T(8,128)(2,1)}, bf16[2...) custom-call(f32[64,2048]{1,0:T(8,128)} %get-tuple-element.87.refs_0_.refs_1_, ...), custom_call_target="tpu_custom_call" | custom-call | tf_op jit(solution)/shard_map/feed_forward3/pallas_call | solution.py:1110
  276.6 97.3 %attention_forward4.1 = (f32[64,2048]{1,0:T(8,128)}, bf16[1024,2048]{1,0:T(8,128)(2,1)}, bf16[1024,128]{1,0:T(8,128)(2,1)}, bf16[1024,128]{1,0:T(8,128)(2,1)}, b...) custom-call(bf16[64,2048]{1,0:T(8,128)(2,1)} %get-tuple-element.90.r, ...), custom_call_target="tpu_custom_call" | custom-call | tf_op jit(solution)/shard_map/attention_forward4/pallas_call | solution.py:1110
  373.9 66.5 %feed_forward5.1 = (bf16[64,2048]{1,0:T(8,128)(2,1)}, bf16[1024,2048]{1,0:T(8,128)(2,1)}, f32[1024,512]{1,0:T(8,128)}, bf16[1024,512]{1,0:T(8,128)(2,1)}) custom-call(f32[64,2048]{1,0:T(8,128)} %get-tuple-element.93.refs_0_.refs_1_, f32[2,2048]{1,0:T(2,128)} %get-tuple-element.182.refs_1_.refs_2_, f32[4,2048]{1,0:T(4,128)} %get-tuple-element.178.refs_2_, ...), custom_call_target="tpu_custom_call" | custom-call | tf_op jit(solution)/shard_map/feed_forward5/pallas_call | solution.py:1110
  440.4 41.4 %feed_backward6.1 = (f32[64,2048]{1,0:T(8,128)}, bf16[2048,512]{1,0:T(8,128)(2,1)}, bf16[512,2048]{1,0:T(8,128)(2,1)}, f32[1,512]{1,0:T(1,128)}, f32[1,2048]{1,0...) custom-call(bf16[64,2048]{1,0:T(8,128)(2,1)} %get-tuple-element.177.refs_0_, ...), custom_call_target="tpu_custom_call" | custom-call | tf_op jit(solution)/shard_map/feed_backward6/pallas_call | solution.py:1110
  481.8 95.3 %attention_backward7.1 = (f32[64,2048]{1,0:T(8,128)}, bf16[2048,384]{1,0:T(8,128)(2,1)}, bf16[128,2048]{1,0:T(8,128)(2,1)}, f32[2,128]{1,0:T(2,128)}, f32[1,2048...) custom-call(f32[64,2048]{1,0:T(8,128)} %get-tuple-element.102.refs_0, ...), custom_call_target="tpu_custom_call" | custom-call | tf_op jit(solution)/shard_map/attention_backward7/pallas_call | solution.py:1110
  577.1 1.8 convert_element_type.69.refs_0_
  578.9 89.7 %feed_backward8.1 = (f32[64,2048]{1,0:T(8,128)}, bf16[2048,512]{1,0:T(8,128)(2,1)}, bf16[512,2048]{1,0:T(8,128)(2,1)}, f32[1,512]{1,0:T(1,128)}, f32[1,2048]{1,0...) custom-call(bf16[64,2048]{1,0:T(8,128)(2,1)} %convert_element_type.6, ...), custom_call_target="tpu_custom_call" | custom-call | tf_op jit(solution)/shard_map/feed_backward8/pallas_call | solution.py:1110
  668.6 98.1 %attention_backward9.1 = (f32[64,2048]{1,0:T(8,128)}, bf16[2048,384]{1,0:T(8,128)(2,1)}, bf16[128,2048]{1,0:T(8,128)(2,1)}, f32[2,128]{1,0:T(2,128)}, f32[1,2048...) custom-call(f32[64,2048]{1,0:T(8,128)} %get-tuple-element.117.refs_0, ...), custom_call_target="tpu_custom_call" | custom-call | tf_op jit(solution)/shard_map/attention_backward9/pallas_call | solution.py:1110
  766.7 42.8 %closing.1 = (f32[80,128]{1,0:T(8,128)}, bf16[256,3072]{1,0:T(8,128)(2,1)}, bf16[1024,256]{1,0:T(8,128)(2,1)}, f32[2,64,2048]{2,1,0:T(8,128)}) custom-call(f32[1,2048]{1,0:T(1,128)} %get-tuple-element.126.refs_0_, f32[1,2048]{1,0:T(1,128)} %get-tuple-element.127.refs_1_, f32[1,2048]{1,0:T(1,128)} %get-tuple-element.128.refs_2_, ...), custom_call_target="tpu_custom_call" | custom-call | tf_op jit(solution)/shard_map/closing/pallas_call | solution.py:1110
  809.5 2.5 select_bitcast_fusion
  814.6 1.0 bitcast_convert_fusion.2
  815.7 1.6 select_convert_fusion
  817.3 2.4 copy.48
  819.6 2.2 copy.49
  821.8 2.4 copy.52
  824.2 4.0 bitcast_convert_fusion.1
  828.2 2.3 bitcast_convert_fusion
  (64 shorter events, 12.9 us)
Async XLA Ops:
  0.6 0.7 copy-start
  766.7 42.8 %copy-start.4 = (f32[2,64,2048]{2,1,0:T(8,128)S(1)}, f32[2,64,2048]{2,1,0:T(8,128)}, u32[]{:S(2)}) copy-start(f32[2,64,2048]{2,1,0:T(8,128)} %get-tuple-element.146) | copy-start | bytes 3145732
  809.5 2.5 copy-start.8
  809.5 5.1 copy-start.5
  809.5 5.1 copy-start.6
  824.2 4.0 copy-start.2
  824.2 4.0 copy-start.3
  828.2 2.3 copy-start.7
  828.2 3.1 copy-start.1

commit v3 on v0

--- a/solution.py
+++ b/solution.py
@@ -1,9 +1,12 @@
 from functools import partial
 import math
+from types import SimpleNamespace
 
 import jax
 import jax.numpy as jnp
 from jax import lax
+from jax.experimental import pallas as pl
+from jax.experimental.pallas import tpu as pltpu
 from jax.sharding import PartitionSpec as P
 
 HD = 128
@@ -11,6 +14,7 @@
 
 EPSILON = 1e-05
 NEG_FILL = -1e30
+MESH = pl.DeviceIdType.MESH
 
 
 def from_behind(value, axis, steps):
@@ -453,6 +457,1269 @@
     return (acts, input_grads) + tuple(summed)
 
 
+LOW, WIDE = (jnp.bfloat16, jnp.float32)
+HBM, VMEM, DMAS = (pl.ANY, pltpu.VMEM, pltpu.SemaphoreType.DMA)
+
+
+def dot(left, right):
+    return jnp.dot(left, right, preferred_element_type=WIDE)
+
+
+def dot_back(left, right):
+    return lax.dot_general(left, right, (((1,), (1,)), ((), ())), preferred_element_type=WIDE)
+
+
+def dot_rows(left, right):
+    return lax.dot_general(left, right, (((0,), (0,)), ((), ())), preferred_element_type=WIDE)
+
+
+def device(core, z, x, y):
+    return (core, z * 2 + x, y)
+
+
+class Plane:
+    def __init__(self):
+        dp = lax.axis_index("dp")
+        self.levels = lax.axis_size("dp") // 2
+        self.core, self.y = (lax.axis_index("section"), lax.axis_index("tensor"))
+        self.z, self.x = (dp // 2, lax.rem(dp, 2))
+        self.sibling = device(1 - self.core, self.z, self.x, self.y)
+        self.across = device(self.core, self.z, self.x, 1 - self.y)
+        self.over = device(self.core, self.z, 1 - self.x, self.y)
+        self.corner = device(1 - self.core, self.z, 1 - self.x, self.y)
+        self.member = self.z * 2 + self.core
+        self.block = self.z * 4 + self.core * 2 + self.y
+
+    def along(self, z):
+        return device(self.core, jnp.clip(z, 0, self.levels - 1), self.x, self.y)
+
+    def partners(self):
+        partners = [self.across, self.over, self.corner]
+        for step in range(self.levels):
+            zz = lax.rem(self.z + step, self.levels)
+            for other in (0, 1):
+                if step or other:
+                    core = 1 - self.core if other else self.core
+                    partners.append(device(core, zz, self.x, self.y))
+        return partners
+
+    def nearest(self):
+        tables = []
+        for z in range(self.levels):
+            tables.append(sorted(range(self.levels), key=lambda zz: (abs(zz - z), zz)))
+        found = []
+        for place in range(self.levels):
+            number = jnp.int32(tables[0][place])
+            for z in range(1, self.levels):
+                number = jnp.where(self.z == z, tables[z][place], number)
+            found.append(number)
+        return found
+
+
+def guarded(present, act):
+    if present is True:
+        act()
+    else:
+        pl.when(present)(act)
+
+
+class Sends:
+    def __init__(self, sems):
+        self.sems = sems
+        self.pending = []
+
+    def start(self, present, source, target, arrived, partner):
+        copy = pltpu.make_async_remote_copy(
+            src_ref=source,
+            dst_ref=target,
+            send_sem=self.sems.at[len(self.pending)],
+            recv_sem=arrived,
+            device_id=partner,
+            device_id_type=MESH,
+        )
+        guarded(present, copy.start)
+        self.pending.append([present, copy, False])
+        return len(self.pending) - 1
+
+    def wait(self, *numbers):
+        for number in numbers:
+            present, copy, done = self.pending[number]
+            if not done:
+                guarded(present, copy.wait_send)
+                self.pending[number][2] = True
+
+    def finish(self):
+        self.wait(*range(len(self.pending)))
+
+
+class Copies:
+    def __init__(self, sems):
+        self.sems = sems
+        self.pending = []
+
+    def start(self, source, target, present=True):
+        copy = pltpu.make_async_copy(source, target, self.sems.at[len(self.pending)])
+        guarded(present, copy.start)
+        self.pending.append([present, copy, False])
+        return len(self.pending) - 1
+
+    def wait(self, *numbers):
+        for number in numbers:
+            present, copy, done = self.pending[number]
+            if not done:
+                guarded(present, copy.wait)
+                self.pending[number][2] = True
+
+    def finish(self):
+        for number in range(len(self.pending)):
+            self.wait(number)
+
+
+def await_block(block, arrived, partner):
+    pltpu.make_async_remote_copy(
+        src_ref=block,
+        dst_ref=block,
+        send_sem=arrived,
+        recv_sem=arrived,
+        device_id=partner,
+        device_id_type=MESH,
+    ).wait_recv()
+
+
+def span(start, size):
+    return pl.ds(pl.multiple_of(start * size, size), size)
+
+
+class Gather:
+    def __init__(self, plane, sends, rows, sems):
+        self.plane, self.sends, self.rows, self.sems = (plane, sends, rows, sems)
+        self.chunks = sems.shape[1]
+        self.size = rows.shape[0] // (sems.shape[0] * self.chunks)
+
+    def spot(self, zz, core, y, chunk):
+        number = zz * 4 + core * 2 + y
+        return (
+            self.rows.at[span(number * self.chunks + chunk, self.size)],
+            self.sems.at[number, chunk],
+        )
+
+    def open(self):
+        plane = self.plane
+        for chunk in range(self.chunks):
+            held, arrived = self.spot(plane.z, plane.core, plane.y, chunk)
+            for present, partner in (
+                (True, plane.across),
+                (plane.z > 0, plane.along(plane.z - 1)),
+                (plane.z < plane.levels - 1, plane.along(plane.z + 1)),
+                (True, plane.sibling),
+            ):
+                self.sends.start(present, held, held, arrived, partner)
+
+    def run(self, on_group, tick):
+        plane = self.plane
+        order = plane.nearest()
+
+        def complete(step):
+            zz = order[step]
+            for chunk in range(self.chunks):
+                held, arrived = self.spot(zz, plane.core, 1 - plane.y, chunk)
+                await_block(held, arrived, plane.across)
+                self.sends.start(True, held, held, arrived, plane.sibling)
+            for yy in (plane.y, 1 - plane.y):
+                for chunk in range(self.chunks):
+                    held, arrived = self.spot(zz, 1 - plane.core, yy, chunk)
+                    await_block(held, arrived, plane.sibling)
+            on_group(step, zz)
+
+        for step in range(1, plane.levels):
+            zz = order[step]
+            onward = jnp.where(zz < plane.z, plane.z + 1, plane.z - 1)
+            can_go = (onward >= 0) & (onward < plane.levels)
+            for chunk in range(self.chunks):
+                held, arrived = self.spot(zz, plane.core, plane.y, chunk)
+                await_block(held, arrived, plane.across)
+                self.sends.start(can_go, held, held, arrived, plane.along(onward))
+                self.sends.start(True, held, held, arrived, plane.across)
+                self.sends.start(True, held, held, arrived, plane.sibling)
+            complete(step - 1)
+            tick()
+        complete(plane.levels - 1)
+        tick()
+
+    @staticmethod
+    def count(levels, chunks):
+        return chunks * (4 + 3 * (levels - 1) + levels)
+
+
+class Scatter:
+    def __init__(self, plane, sends, refs, result):
+        self.plane, self.sends, self.refs, self.result = (plane, sends, refs, result)
+        self.chunks = refs.across_sems.shape[1]
+        self.size = result.shape[0] // self.chunks
+
+    @staticmethod
+    def count(levels, chunks):
+        return chunks * (4 * levels - 1)
+
+    def part(self, zz, core, y, chunk):
+        number = (zz * 4 + core * 2 + y) * self.chunks + chunk
+        return self.refs.part.at[span(number, self.size)]
+
+    def spot(self, buffer, sems, slot, chunk):
+        return buffer.at[slot, span(chunk, self.size)], sems.at[slot, chunk]
+
+    def take(self, buffer, sems, slot, chunk):
+        came, arrived = self.spot(buffer, sems, slot, chunk)
+        await_block(came, arrived, self.plane.across)
+        return came[...].astype(WIDE)
+
+    def pair(self, zz, y, chunk):
+        refs = self.refs
+        own = self.part(zz, self.plane.core, y, chunk)[...].astype(WIDE)
+        return own + self.take(refs.from_sibling, refs.sibling_sems, zz * 2 + y, chunk)
+
+    def give_sibling(self, zz):
+        plane, refs = (self.plane, self.refs)
+        for yy in (1 - plane.y, plane.y):
+            for chunk in range(self.chunks):
+                landing, arrived = self.spot(
+                    refs.from_sibling, refs.sibling_sems, zz * 2 + yy, chunk
+                )
+                self.sends.start(
+                    True, self.part(zz, 1 - plane.core, yy, chunk), landing, arrived, plane.sibling
+                )
+
+    def give_across(self, zz):
+        plane, refs = (self.plane, self.refs)
+        for chunk in range(self.chunks):
+            staged = refs.from_sibling.at[zz * 2 + 1 - plane.y, span(chunk, self.size)]
+            staged[...] = self.pair(zz, 1 - plane.y, chunk).astype(staged.dtype)
+            landing, arrived = self.spot(refs.from_across, refs.across_sems, zz, chunk)
+            self.sends.start(True, staged, landing, arrived, plane.across)
+
+    def plane_sum(self, zz, chunk):
+        refs = self.refs
+        total = self.pair(zz, self.plane.y, chunk)
+        return total + self.take(refs.from_across, refs.across_sems, zz, chunk)
+
+    def come(self, slot, chunk):
+        return self.take(self.refs.from_behind, self.refs.behind_sems, slot, chunk)
+
+    def give_onward(self, zz):
+        plane, refs = (self.plane, self.refs)
+        onward = jnp.where(zz > plane.z, plane.z + 1, plane.z - 1)
+        behind = plane.z * 2 - onward
+        slot = jnp.where((onward == zz) & (zz < plane.z), plane.levels, zz)
+        for chunk in range(self.chunks):
+            refs.total[...] = self.plane_sum(zz, chunk)
+
+            @pl.when((behind >= 0) & (behind < plane.levels))
+            def _(chunk=chunk):
+                refs.total[...] += self.come(zz, chunk)
+
+            staged = refs.from_sibling.at[zz * 2 + plane.y, span(chunk, self.size)]
+            staged[...] = refs.total[...].astype(staged.dtype)
+            landing, arrived = self.spot(refs.from_behind, refs.behind_sems, slot, chunk)
+            self.sends.start(True, staged, landing, arrived, plane.along(onward))
+
+    def conclude(self):
+        plane = self.plane
+        for chunk in range(self.chunks):
+            own = self.result.at[span(chunk, self.size)]
+            own[...] = self.plane_sum(plane.z, chunk)
+
+            @pl.when(plane.z > 0)
+            def _(own=own, chunk=chunk):
+                own[...] += self.come(plane.z, chunk)
+
+            @pl.when(plane.z < plane.levels - 1)
+            def _(own=own, chunk=chunk):
+                own[...] += self.come(plane.levels, chunk)
+
+    def run(self, make, tick, fill=None):
+        levels = self.plane.levels
+        order = self.plane.nearest()[::-1]
+        for step in range(levels + 3):
+            if step < levels:
+                make(step, order[step])
+                self.give_sibling(order[step])
+            if 0 < step <= levels:
+                self.give_across(order[step - 1])
+            if step >= levels - 1:
+                tick()
+                if fill is not None:
+                    fill(step - levels + 1)
+            if 3 <= step < levels + 2:
+                self.give_onward(order[step - 3])
+        self.conclude()
+
+
+def scatter_scratch(rows, width, levels, chunks, dtype=LOW):
+    def held(count):
+        return VMEM((count, rows, width), dtype)
+
+    return dict(
+        part=VMEM((rows * 4 * levels, width), dtype),
+        from_sibling=held(2 * levels),
+        from_across=held(levels),
+        from_behind=held(levels + 1),
+        total=VMEM((rows // chunks, width), WIDE),
+        sum=VMEM((rows, width), WIDE),
+        sibling_sems=DMAS((2 * levels, chunks)),
+        across_sems=DMAS((levels, chunks)),
+        behind_sems=DMAS((levels + 1, chunks)),
+    )
+
+
+def by_rows(which):
+    return which in (1, 3)
+
+
+def piece_of_shard(which, ref, member, members):
+    if by_rows(which):
+        return ref.at[span(member, ref.shape[0] // members)]
+    return ref.at[:, span(member, ref.shape[1] // members)]
+
+
+def piece_of_slice(which, ref, shard, shards):
+    if by_rows(which):
+        return ref.at[:, span(shard, ref.shape[1] // shards)]
+    return ref.at[span(shard, ref.shape[0] // shards)]
+
+
+def slice_shape(which, shape, shards):
+    rows, columns = shape
+    if by_rows(which):
+        return (rows // shards, columns * shards)
+    return (rows * shards, columns // shards)
+
+
+def shard_shape(which, shape, shards):
+    rows, columns = shape
+    if by_rows(which):
+        return (rows * shards, columns // shards)
+    return (rows // shards, columns * shards)
+
+
+class Fetch:
+    UNITS = ((0, (0, 1)), (0, (2,)), (0, (3,)), (1, (0, 1)), (1, (2,)), (1, (3,)))
+    LAG = 4
+
+    def __init__(self, plane, shards, slices, refs, sends, copies):
+        self.plane, self.shards, self.slices = (plane, shards, slices)
+        self.refs, self.sends, self.copies = (refs, sends, copies)
+        acts = []
+        for unit in range(len(self.UNITS)):
+            for step in range(plane.levels - 1, -1, -1):
+                acts.append((unit, step))
+        self.moments = []
+        for at in range(len(acts) + self.LAG):
+            moment = []
+            if at < len(acts):
+                moment.append((self.spread,) + acts[at])
+            if at >= self.LAG:
+                moment.append((self.hand_over,) + acts[at - self.LAG])
+            self.moments.append(moment)
+        self.left = [plane.levels] * len(self.UNITS)
+        self.kept = [[] for _ in self.UNITS]
+
+    @staticmethod
+    def count(levels):
+        return 4 * 2 * (3 * levels), 4 * 2 + 8
+
+    def tick(self, times=1):
+        for _ in range(times):
+            if self.moments:
+                for act, unit, step in self.moments.pop(0):
+                    for which in self.UNITS[unit][1]:
+                        act(unit, which, step)
+                    if act == self.hand_over:
+                        self.left[unit] -= 1
+
+    def require(self, unit):
+        while self.left[unit]:
+            self.tick()
+        plane, refs = (self.plane, self.refs)
+        layer, weights = self.UNITS[unit]
+        for which in weights:
+            part = self.slices[which].at[layer]
+            for zz in range(plane.levels):
+                held = piece_of_slice(which, part, zz * 2 + 1 - plane.x, 2 * plane.levels)
+                await_block(held, refs.cross_sems.at[which, layer, zz], plane.over)
+        self.copies.wait(*self.kept[unit])
+        for which in weights:
+            self.copies.start(self.slices[which].at[layer], refs.slices_out[which].at[layer])
+
+    def spread(self, unit, which, step):
+        plane, refs, layer = (self.plane, self.refs, self.UNITS[unit][0])
+        members = 2 * plane.levels
+        shard, part = (self.shards[which], self.slices[which].at[layer])
+        owner = plane.core == layer
+        target = piece_of_slice(which, part, plane.z * 2 + plane.x, members)
+        zz = lax.rem(plane.z + step, plane.levels)
+        for other in (0, 1):
+            core = 1 - plane.core if other else plane.core
+            source = piece_of_shard(which, shard, zz * 2 + core, members)
+            if step or other:
+                self.sends.start(
+                    owner,
+                    source,
+                    target,
+                    refs.column_sems.at[which, layer, plane.z],
+                    device(core, zz, plane.x, plane.y),
+                )
+            else:
+                self.kept[unit].append(self.copies.start(source, target, owner))
+
+    def hand_over(self, unit, which, step):
+        plane, refs, layer = (self.plane, self.refs, self.UNITS[unit][0])
+        members = 2 * plane.levels
+        shard, part = (self.shards[which], self.slices[which].at[layer])
+        zz = lax.rem(plane.z - step + plane.levels, plane.levels)
+        held = piece_of_slice(which, part, zz * 2 + plane.x, members)
+        arrived = refs.column_sems.at[which, layer, zz]
+        cross = refs.cross_sems.at[which, layer, zz]
+        if step:
+            await_block(held, arrived, plane.over)
+            self.sends.start(True, held, held, cross, plane.over)
+        else:
+            owner = plane.core == layer
+            source = piece_of_shard(which, shard, plane.member, members)
+            guarded(jnp.logical_not(owner), partial(await_block, held, arrived, plane.over))
+            self.sends.start(jnp.logical_not(owner), held, held, cross, plane.over)
+            self.sends.start(owner, source, held, cross, plane.over)
+
+
+class Return:
+    def __init__(self, plane, slices, landed, shards, refs, sends, copies):
+        self.plane, self.slices, self.landed, self.shards = (plane, slices, landed, shards)
+        self.refs, self.sends, self.copies = (refs, sends, copies)
+        self.moments, self.left, self.given = ([], {}, {})
+
+    @staticmethod
+    def count(levels):
+        return 4 * 2 * (2 * levels), 4 * 2
+
+    def give(self, layer, which, lag=0):
+        plane = self.plane
+        self.moments.extend([None] * lag)
+        self.left[layer, which], self.given[layer, which] = (plane.levels, [])
+        for step in range(plane.levels - 1, -1, -1):
+            zz = lax.rem(plane.z + step, plane.levels)
+            number = self.sends.start(
+                True,
+                piece_of_slice(which, self.slices[which], zz * 2 + 1 - plane.x, 2 * plane.levels),
+                self.landed[which].at[layer, zz],
+                self.refs.cross_sems.at[which, layer, zz],
+                plane.over,
+            )
+            self.given[layer, which].append(number)
+            self.moments.append((layer, which, step))
+
+    def tick(self, times=1):
+        for _ in range(times):
+            if self.moments:
+                moment = self.moments.pop(0)
+                if moment is not None:
+                    self.add(*moment)
+                    self.left[moment[:2]] -= 1
+
+    def require(self, layer, which):
+        while self.left[layer, which]:
+            self.tick()
+        self.sends.wait(*self.given[layer, which])
+
+    def add(self, layer, which, step):
+        plane, refs = (self.plane, self.refs)
+        members = 2 * plane.levels
+        here = plane.core == layer
+        target = piece_of_shard(which, self.shards[which], plane.member, members)
+        zz = lax.rem(plane.z + step, plane.levels)
+        held = self.landed[which].at[layer, zz]
+        await_block(held, refs.cross_sems.at[which, layer, zz], plane.over)
+        own = piece_of_slice(which, self.slices[which], zz * 2 + plane.x, members)
+        held[...] = (held[...].astype(WIDE) + own[...].astype(WIDE)).astype(LOW)
+        self.sends.start(
+            True if step else jnp.logical_not(here),
+            held,
+            target,
+            refs.column_sems.at[which, plane.core, plane.z],
+            device(layer, zz, plane.x, plane.y),
+        )
+        if step == 0:
+            self.copies.start(held, target, here)
+
+    def finish(self):
+        while self.moments:
+            self.tick()
+        plane, refs = (self.plane, self.refs)
+        members = 2 * plane.levels
+        for which in range(4):
+            for core in (0, 1):
+                for step in range(plane.levels):
+                    zz = lax.rem(plane.z + step, plane.levels)
+                    held = piece_of_shard(which, self.shards[which], zz * 2 + core, members)
+                    guarded(
+                        True if step else plane.core != core,
+                        partial(
+                            await_block, held, refs.column_sems.at[which, core, zz], plane.over
+                        ),
+                    )
+
+
+class Outward:
+    @staticmethod
+    def count():
+        return 6, 2
+
+    def __init__(self, plane, target, sems):
+        self.plane, self.target, self.sems = (plane, target, sems)
+
+    def give(self, layer, source, sends, copies):
+        plane, target = (self.plane, self.target.at[self.plane.x])
+        same_core, same_x = (plane.core == layer, plane.core == plane.x)
+        other_core, other_x = (plane.core != layer, plane.core != plane.x)
+        for present, partner in (
+            (same_core & other_x, plane.over),
+            (other_core & same_x, plane.sibling),
+            (other_core & other_x, plane.corner),
+        ):
+            sends.start(present, source, target, self.sems.at[plane.x], partner)
+        copies.start(source, target, same_core & same_x)
+
+    def finish(self):
+        plane = self.plane
+        for slot in (0, 1):
+            away = jnp.logical_not((plane.core == plane.x) & (plane.x == slot))
+            guarded(away, partial(await_block, self.target.at[slot], self.sems.at[slot], plane.over))
+
+
+def launch(name, ident, kernel, counts, inputs, outputs, scratch):
+    scratch = dict(
+        scratch,
+        send_sems=DMAS((counts[0],)),
+        phase_sems=DMAS((counts[1],)),
+        copy_sems=DMAS((counts[2],)),
+    )
+    names = list(inputs) + list(outputs) + list(scratch)
+
+    def body(*refs):
+        held = SimpleNamespace(**dict(zip(names, refs)))
+        plane = Plane()
+        barrier = pltpu.get_barrier_semaphore()
+        partners = plane.partners()
+        for partner in partners:
+            pl.semaphore_signal(barrier, inc=1, device_id=partner, device_id_type=MESH)
+        sends, copies = (Sends(held.send_sems), Copies(held.copy_sems))
+        kernel(held, plane, lambda: pl.semaphore_wait(barrier, len(partners)), sends, copies)
+        copies.finish()
+        sends.finish()
+        assert len(sends.pending) == counts[0], len(sends.pending)
+        assert len(copies.pending) == counts[2], len(copies.pending)
+
+    results = pl.pallas_call(
+        body,
+        out_shape=[jax.ShapeDtypeStruct(shape, dtype) for shape, dtype, _ in outputs.values()],
+        in_specs=[pl.BlockSpec(memory_space=space) for _, space in inputs.values()],
+        out_specs=[pl.BlockSpec(memory_space=space) for _, _, space in outputs.values()],
+        scratch_shapes=list(scratch.values()),
+        compiler_params=pltpu.CompilerParams(
+            collective_id=ident, has_side_effects=True, vmem_limit_bytes=60 << 20
+        ),
+        name=name,
+    )(*[array for array, _ in inputs.values()])
+    return SimpleNamespace(**dict(zip(outputs, results)))
+
+
+CHUNKS, SUM_CHUNKS, CUT = (2, 2, 512)
+NORM_LINES, HEAD_LINES, LINES = (6, 8, 16)
+
+
+def unpack_vectors(refs, plane, levels):
+    members, blocks = (2 * levels, 4 * levels)
+    for layer in (0, 1):
+        for z in range(levels):
+            for x in (0, 1):
+                for y in (0, 1):
+                    start = ((z * 4 + layer * 2 + y) * 2 + x) * LINES
+                    cut = (z * 4 + x * 2 + y) * HD
+                    refs.norms[layer, :, cut : cut + HD] = refs.small[
+                        start : start + LINES
+                    ].astype(WIDE)[:HEAD_LINES]
+    lines = []
+    for layer in (0, 1):
+        pieces = []
+        for z in range(levels):
+            for x in (0, 1):
+                number = (z * 4 + layer * 2 + plane.y) * 2 + x
+                pieces.append(refs.small[span(number, LINES)].astype(WIDE)[HEAD_LINES:])
+        lines.append(jnp.concatenate(pieces, axis=1))
+    lines = jnp.concatenate(lines, axis=0).astype(LOW)
+    width = HD // members
+    place = lax.broadcasted_iota(jnp.int32, (members * HD, HD), 0)
+    lane = lax.broadcasted_iota(jnp.int32, (members * HD, HD), 1)
+
+    def pick(first):
+        chosen = (place // HD == lane // width) & (place % HD == lane % width + first)
+        return dot(lines, chosen.astype(WIDE).astype(LOW))
+
+    heads = pick(plane.member * width)
+    units = refs.b_up.shape[2] // HD
+    per_line = HD // (units * width)
+    row = lax.broadcasted_iota(jnp.int32, (HEAD_LINES, HD), 0)
+    for layer in (0, 1):
+        refs.b_qv[layer] = heads[layer * HEAD_LINES : layer * HEAD_LINES + 2]
+    for unit in range(units):
+        found = pick((lax.rem(plane.member, per_line) * units + unit) * width)
+        for layer in (0, 1):
+            own = found[layer * HEAD_LINES : (layer + 1) * HEAD_LINES]
+            own = jnp.where(row == 2 + plane.member // per_line, own, 0.0)
+            refs.b_up[layer, :, unit * HD : (unit + 1) * HD] = jnp.sum(own, axis=0, keepdims=True)
+
+
+def visible(refs, group, size, tokens):
+    segment = refs.query_segment[group]
+    place = group.start + lax.broadcasted_iota(jnp.int32, (size, tokens), 0)
+    keys = lax.broadcasted_iota(jnp.int32, (size, tokens), 1)
+    return (segment == refs.key_segment[...]) & (keys <= place)
+
+
+def forward_planes(ident, boundary, packed, segments, shards):
+    levels = lax.axis_size("dp") // 2
+    blocks, members = (4 * levels, 2 * levels)
+    rows, width = boundary.shape[1:]
+    tokens, size = (blocks * rows, 4 * rows)
+    slice_shapes = [
+        slice_shape(which, shard.shape, members) for which, shard in enumerate(shards)
+    ]
+    units = slice_shapes[2][1]
+    scaling = HD ** (-0.5)
+
+    def kernel(refs, plane, greet, sends, copies):
+        core, x = (plane.core, plane.x)
+        own_block = span(plane.block, rows)
+        refs.slices_out = [refs.out0, refs.out1, refs.out2, refs.out3]
+        slices = [refs.w0, refs.w1, refs.w2, refs.w3]
+        fetch = Fetch(
+            plane, [refs.shard0, refs.shard1, refs.shard2, refs.shard3], slices, refs, sends, copies
+        )
+        small_block = span(plane.block * 2 + x, LINES)
+        refs.small[small_block] = refs.packed[...]
+        greet()
+        phase = Sends(refs.phase_sems)
+        own_small = refs.small.at[small_block]
+        phase.start(True, own_small, own_small, refs.pair_sem.at[0], plane.over)
+        inward = []
+        for slot in (0, 1):
+            source, target = (refs.boundary.at[slot], refs.landed_planes.at[core])
+            arrived = refs.inward_sems.at[core]
+            for present, partner in (
+                ((x == core) & (slot != x), plane.over),
+                ((x != core) & (slot == x), plane.sibling),
+                ((x != core) & (slot != x), plane.corner),
+            ):
+                phase.start(present, source, target, arrived, partner)
+            inward.append(copies.start(source, target, (x == core) & (slot == x)))
+        fetch.tick(levels)
+        other_small = refs.small.at[span(plane.block * 2 + 1 - x, LINES)]
+        await_block(other_small, refs.pair_sem.at[0], plane.over)
+        small = Gather(plane, phase, refs.small, refs.small_sems)
+        small.open()
+        small.run(lambda step, zz: None, lambda: None)
+        for slot in (0, 1):
+            here = (core == x) & (core == slot)
+            guarded(
+                jnp.logical_not(here),
+                partial(await_block, refs.landed_planes.at[slot], refs.inward_sems.at[slot], plane.over),
+            )
+        copies.wait(*inward)
+        refs.planes[...] = refs.landed_planes[...]
+        refs.rows[0, own_block] = refs.landed_planes[1]
+        gather = Gather(plane, phase, refs.rows.at[0], refs.gather_sems.at[0])
+        gather.open()
+        unpack_vectors(refs, plane, levels)
+        kept = []
+
+        def keep(step, zz):
+            group = span(zz, size)
+            kept.append(copies.start(refs.rows.at[0, group], refs.gathered.at[group]))
+
+        gather.run(keep, fetch.tick)
+        copies.wait(*kept)
+        phase.finish()
+
+        for layer in (0, 1):
+            number = 1 + 2 * layer
+            norms = refs.norms.at[layer]
+            held, sems = (refs.rows.at[number % 2], refs.gather_sems.at[number % 2])
+            entering = refs.planes[0] if layer == 0 else refs.leaving[0]
+            hidden = entering.astype(WIDE)
+            normed, _, _ = layer_norm(hidden, norms[0:1], norms[2:3])
+            held[own_block] = normed.astype(LOW)
+            phase = Sends(refs.phase_sems)
+            gather = Gather(plane, phase, held, sems)
+            gather.open()
+            fetch.require(3 * layer)
+            kept = []
+
+            def project(step, zz):
+                group = span(zz, size)
+                projected = dot(held[group], refs.w0[layer])
+                refs.queries[layer, group] = (projected[:, :HD] + refs.b_qv[layer, 0:1]).astype(LOW)
+                refs.keys[layer, group] = projected[:, HD : 2 * HD].astype(LOW)
+                refs.values[layer, group] = (
+                    projected[:, 2 * HD :] + refs.b_qv[layer, 1:2]
+                ).astype(LOW)
+                kept.append(copies.start(held.at[group], refs.rows_a.at[layer, group]))
+
+            gather.run(project, fetch.tick)
+
+            def attend(step, zz):
+                group = span(zz, size)
+                allowed = visible(refs, group, size, tokens)
+                scores = dot_back(refs.queries[layer, group], refs.keys[layer]) * scaling
+                scores = jnp.where(allowed, scores, NEG_FILL)
+                top = jnp.max(scores, axis=-1, keepdims=True)
+                raised = jnp.exp(scores - top)
+                total = jnp.sum(raised, axis=-1, keepdims=True)
+                refs.log_total[layer, group] = top + jnp.log(total)
+                probs = (raised / total).astype(LOW)
+                live = (refs.query_segment[group] >= 0).astype(WIDE)
+                mixed = (dot(probs, refs.values[layer]) * live).astype(LOW)
+                refs.mixed[layer, group] = mixed
+                for cut in range(0, width, CUT):
+                    refs.part[group, cut : cut + CUT] = dot(
+                        mixed, refs.w1[layer, :, cut : cut + CUT]
+                    ).astype(LOW)
+
+            Scatter(plane, phase, refs, refs.sum).run(attend, fetch.tick)
+            middle = hidden + refs.sum[...] + norms[3:4]
+            refs.middle[layer] = middle
+            copies.wait(*kept)
+            phase.finish()
+
+            number = number + 1
+            held, sems = (refs.rows.at[number % 2], refs.gather_sems.at[number % 2])
+            normed, _, _ = layer_norm(middle, norms[1:2], norms[4:5])
+            held[own_block] = normed.astype(LOW)
+            phase = Sends(refs.phase_sems)
+            gather = Gather(plane, phase, held, sems)
+            gather.open()
+            fetch.require(3 * layer + 1)
+            kept = []
+
+            def expand(step, zz):
+                group = span(zz, size)
+                preact = dot(held[group], refs.w2[layer]) + refs.b_up[layer]
+                refs.own_preact[layer, group] = preact
+                refs.own_activated[layer, group] = (
+                    0.5 * preact * (1.0 + lax.erf(preact * math.sqrt(0.5)))
+                ).astype(LOW)
+                for own, out in (
+                    (held.at[group], refs.rows_b),
+                    (refs.own_preact.at[layer, group], refs.preact),
+                    (refs.own_activated.at[layer, group], refs.activated),
+                ):
+                    kept.append(copies.start(own, out.at[layer, group]))
+
+            gather.run(expand, fetch.tick)
+            fetch.require(3 * layer + 2)
+
+            def shrink(step, zz):
+                group = span(zz, size)
+                for cut in range(0, width, CUT):
+                    refs.part[group, cut : cut + CUT] = dot(
+                        refs.own_activated[layer, group], refs.w3[layer, :, cut : cut + CUT]
+                    ).astype(LOW)
+
+            Scatter(plane, phase, refs, refs.sum).run(shrink, fetch.tick)
+            refs.leaving[layer] = (refs.middle[layer] + refs.sum[...] + norms[5:6]).astype(LOW)
+            copies.wait(*kept)
+            phase.finish()
+
+    head = ((2, tokens, HD), LOW, VMEM)
+    gathers = Gather.count(levels, CHUNKS)
+    lasting = Fetch.count(levels)
+    return launch(
+        "forward_planes",
+        ident,
+        kernel,
+        (
+            lasting[0],
+            max(gathers + Scatter.count(levels, SUM_CHUNKS), 7 + Gather.count(levels, 1) + gathers),
+            lasting[1] + 2 + levels + 2 * 4 * levels,
+        ),
+        dict(
+            boundary=(boundary, HBM),
+            packed=(packed, VMEM),
+            query_segment=(segments[0], VMEM),
+            key_segment=(segments[1], VMEM),
+            shard0=(shards[0], HBM),
+            shard1=(shards[1], HBM),
+            shard2=(shards[2], HBM),
+            shard3=(shards[3], HBM),
+        ),
+        dict(
+            planes=((2, rows, width), LOW, VMEM),
+            leaving=((2, rows, width), LOW, VMEM),
+            middle=((2, rows, width), WIDE, VMEM),
+            norms=((2, HEAD_LINES, width), WIDE, VMEM),
+            queries=head,
+            keys=head,
+            values=head,
+            mixed=head,
+            log_total=((2, tokens, 1), WIDE, VMEM),
+            gathered=((tokens, width), LOW, HBM),
+            rows_a=((2, tokens, width), LOW, HBM),
+            rows_b=((2, tokens, width), LOW, HBM),
+            preact=((2, tokens, units), WIDE, HBM),
+            activated=((2, tokens, units), LOW, HBM),
+            out0=((2,) + slice_shapes[0], LOW, HBM),
+            out1=((2,) + slice_shapes[1], LOW, HBM),
+            out2=((2,) + slice_shapes[2], LOW, HBM),
+            out3=((2,) + slice_shapes[3], LOW, HBM),
+        ),
+        dict(
+            scatter_scratch(rows, width, levels, SUM_CHUNKS),
+            rows=VMEM((2, tokens, width), LOW),
+            gather_sems=DMAS((2, blocks, CHUNKS)),
+            small=VMEM((2 * blocks * LINES, HD), LOW),
+            small_sems=DMAS((blocks, 1)),
+            pair_sem=DMAS((1,)),
+            inward_sems=DMAS((2,)),
+            landed_planes=VMEM((2, rows, width), LOW),
+            b_qv=VMEM((2, 2, HD), WIDE),
+            b_up=VMEM((2, 1, units), WIDE),
+            w0=VMEM((2,) + slice_shapes[0], LOW),
+            w1=VMEM((2,) + slice_shapes[1], LOW),
+            w2=VMEM((2,) + slice_shapes[2], LOW),
+            w3=VMEM((2,) + slice_shapes[3], LOW),
+            own_preact=VMEM((2, tokens, units), WIDE),
+            own_activated=VMEM((2, tokens, units), LOW),
+            column_sems=DMAS((4, 2, levels)),
+            cross_sems=DMAS((4, 2, levels)),
+        ),
+    )
+
+
+def backward_planes(ident, kept, segments):
+    levels = lax.axis_size("dp") // 2
+    blocks, members = (4 * levels, 2 * levels)
+    rows, width = kept.planes.shape[1:]
+    tokens, size = (blocks * rows, 4 * rows)
+    slice_shapes = [array.shape[1:] for array in (kept.out0, kept.out1, kept.out2, kept.out3)]
+    shard_shapes = [shard_shape(which, shape, members) for which, shape in enumerate(slice_shapes)]
+    units = slice_shapes[2][1]
+    unit_lines = units // HD
+    scaling = HD ** (-0.5)
+    vector_lines = (2 + members) * HEAD_LINES
+
+    def landing(which):
+        shape = slice_shapes[which]
+        if by_rows(which):
+            return VMEM((2, levels, shape[0], shape[1] // members), LOW)
+        return VMEM((2, levels, shape[0] // members, shape[1]), LOW)
+
+    def kernel(refs, plane, greet, sends, copies):
+        own_block = span(plane.block, rows)
+        back = Return(
+            plane,
+            [refs.grad0, refs.grad1, refs.grad2, refs.grad3],
+            [refs.landed0, refs.landed1, refs.landed2, refs.landed3],
+            [refs.shard0, refs.shard1, refs.shard2, refs.shard3],
+            refs,
+            sends,
+            copies,
+        )
+        acts = Outward(plane, refs.acts, refs.acts_sems)
+        ends = Outward(plane, refs.input_grads, refs.ends_sems)
+
+        def load(layer):
+            return [
+                copies.start(refs.out3.at[layer], refs.w3),
+                copies.start(refs.preact.at[layer], refs.own_preact),
+                copies.start(refs.out2.at[layer], refs.w2),
+                copies.start(refs.activated.at[layer], refs.own_activated),
+                copies.start(refs.rows_b.at[layer], refs.own_rows),
+                copies.start(refs.out1.at[layer], refs.w1),
+                copies.start(refs.out0.at[layer], refs.w0),
+                copies.start(refs.all_queries.at[layer], refs.queries),
+                copies.start(refs.all_keys.at[layer], refs.keys),
+                copies.start(refs.all_values.at[layer], refs.values),
+                copies.start(refs.all_mixed.at[layer], refs.mixed),
+                copies.start(refs.all_totals.at[layer], refs.log_total),
+            ]
+
+        loads = load(1)
+        first = copies.start(refs.gathered, refs.rows.at[0])
+        greet()
+        acts.give(0, refs.leaving.at[0], sends, copies)
+        acts.give(1, refs.leaving.at[1], sends, copies)
+
+        for layer in (1, 0):
+            number = 2 * (1 - layer)
+            norms = refs.norms.at[layer]
+            vectors = refs.vectors.at[layer]
+            held, sems = (refs.rows.at[number % 2], refs.gather_sems.at[number % 2])
+            phase = Sends(refs.phase_sems)
+            low = refs.planes[1] if layer == 1 else refs.leaving_grads[1].astype(LOW)
+            vectors[5:6] = jnp.sum(low.astype(WIDE), axis=0, keepdims=True)
+            refs.unit_sums[layer] = jnp.zeros((1, units), WIDE)
+            if layer == 0:
+                held[own_block] = low
+                gather = Gather(plane, phase, held, sems)
+                gather.open()
+            else:
+                copies.wait(first)
+            copies.wait(loads[0], loads[1])
+
+            def slope(step, zz):
+                group = span(zz, size)
+                grad_act = dot_back(held[group], refs.w3[...])
+                value = refs.own_preact[group]
+                rise = 0.5 * (1.0 + lax.erf(value * math.sqrt(0.5))) + value * jnp.exp(
+                    -0.5 * value * value
+                ) * (1.0 / math.sqrt(2.0 * math.pi))
+                grad_pre = (grad_act * rise).astype(LOW)
+                refs.grad_pre[group] = grad_pre
+                refs.unit_sums[layer] += jnp.sum(grad_pre.astype(WIDE), axis=0, keepdims=True)
+
+            if layer == 0:
+                gather.run(slope, back.tick)
+            copies.wait(loads[2])
+
+            def widen_units(step, zz):
+                group = span(zz, size)
+                if layer == 1:
+                    slope(step, zz)
+                for cut in range(0, width, CUT):
+                    refs.part[group, cut : cut + CUT] = dot_back(
+                        refs.grad_pre[group], refs.w2[cut : cut + CUT]
+                    ).astype(LOW)
+
+            def down_product(at, carry):
+                cut = span(at, 128)
+                refs.grad3[cut] = dot_rows(refs.own_activated[:, cut], held[...]).astype(LOW)
+                return carry
+
+            def up_product(at, carry):
+                cut = span(at, 256)
+                refs.grad2[cut] = dot_rows(refs.own_rows[:, cut], refs.grad_pre[...]).astype(LOW)
+                return carry
+
+            def products(at):
+                if at == 0:
+                    copies.wait(loads[3], loads[4])
+                    if layer == 0:
+                        back.require(1, 3)
+                        back.require(1, 2)
+                if at == 1:
+                    lax.fori_loop(0, units // 128, down_product, 0)
+                    back.give(layer, 3, lag=1)
+                if at == 2:
+                    lax.fori_loop(0, width // 512, up_product, 0)
+                if at == 3:
+                    lax.fori_loop(width // 512, width // 256, up_product, 0)
+                    back.give(layer, 2)
+
+            Scatter(plane, phase, refs, refs.sum).run(widen_units, back.tick, products)
+            loads.append(copies.start(refs.rows_a.at[layer], refs.own_rows))
+            _, unit, inverse = layer_norm(refs.middle[layer], norms[1:2], norms[1:2])
+            vectors[1:2] = jnp.sum(refs.sum[...] * unit, axis=0, keepdims=True)
+            vectors[4:5] = jnp.sum(refs.sum[...], axis=0, keepdims=True)
+            grad_out = refs.planes[1].astype(WIDE) if layer == 1 else refs.leaving_grads[1].astype(LOW).astype(WIDE)
+            grad_middle = grad_out + norm_back(refs.sum[...], unit, inverse, norms[1:2])
+            phase.finish()
+
+            number = number + 1
+            held, sems = (refs.rows.at[number % 2], refs.gather_sems.at[number % 2])
+            phase = Sends(refs.phase_sems)
+            refs.grad_middle[...] = grad_middle
+            low = grad_middle.astype(LOW)
+            held[own_block] = low
+            gather = Gather(plane, phase, held, sems)
+            gather.open()
+            vectors[3:4] = jnp.sum(low.astype(WIDE), axis=0, keepdims=True)
+            refs.grad_keys[...] = jnp.zeros_like(refs.grad_keys)
+            refs.grad_values[...] = jnp.zeros_like(refs.grad_values)
+            copies.wait(loads[5], *loads[7:12])
+
+            def attend(step, zz):
+                group = span(zz, size)
+                live = (refs.query_segment[group] >= 0).astype(WIDE)
+                grad_mixed = (
+                    dot_back(held[group], refs.w1[...]).astype(LOW) * live
+                ).astype(LOW)
+                allowed = visible(refs, group, size, tokens)
+                queries = refs.queries[group]
+                scores = dot_back(queries, refs.keys[...]) * scaling
+                scores = jnp.where(allowed, scores, NEG_FILL)
+                probs = jnp.exp(scores - refs.log_total[group])
+                grad_probs = dot_back(grad_mixed, refs.values[...])
+                delta = jnp.sum(probs * grad_probs, axis=-1, keepdims=True)
+                grad_scores = jnp.where(allowed, probs * (grad_probs - delta), 0.0).astype(LOW)
+                refs.grad_proj[group, :HD] = (dot(grad_scores, refs.keys[...]) * scaling).astype(LOW)
+                refs.grad_keys[...] += dot_rows(grad_scores, queries)
+                refs.grad_values[...] += dot_rows(probs.astype(LOW), grad_mixed)
+
+            gather.run(attend, back.tick)
+            refs.grad_proj[:, HD : 2 * HD] = (refs.grad_keys[...] * scaling).astype(LOW)
+            refs.grad_proj[:, 2 * HD :] = refs.grad_values[...].astype(LOW)
+            copies.wait(loads[6])
+
+            def widen_heads(step, zz):
+                group = span(zz, size)
+                for cut in range(0, width, CUT):
+                    refs.part[group, cut : cut + CUT] = dot_back(
+                        refs.grad_proj[group], refs.w0[cut : cut + CUT]
+                    ).astype(LOW)
+
+            def qkv_product(at, carry):
+                cut = span(at, 256)
+                refs.grad0[cut] = dot_rows(refs.own_rows[:, cut], refs.grad_proj[...]).astype(LOW)
+                return carry
+
+            def more_products(at):
+                if at == 0:
+                    sums = jnp.sum(refs.grad_proj[...].astype(WIDE), axis=0, keepdims=True)
+                    refs.head_sums[layer, 0:1] = sums[:, :HD]
+                    refs.head_sums[layer, 1:2] = sums[:, 2 * HD :]
+                    copies.wait(loads[12])
+                    if layer == 0:
+                        back.require(1, 1)
+                        back.require(1, 0)
+                if at == 1:
+                    refs.grad1[...] = dot_rows(refs.mixed[...], held[...]).astype(LOW)
+                    back.give(layer, 1, lag=layer)
+                    lax.fori_loop(0, width // 1024, qkv_product, 0)
+                if at == 2:
+                    lax.fori_loop(width // 1024, width // 512, qkv_product, 0)
+                if at == 3:
+                    lax.fori_loop(width // 512, width // 256, qkv_product, 0)
+                    back.give(layer, 0)
+
+            Scatter(plane, phase, refs, refs.sum).run(widen_heads, back.tick, more_products)
+            if layer == 1:
+                loads = load(0)
+            entering = refs.planes[0] if layer == 0 else refs.leaving[0]
+            _, unit, inverse = layer_norm(entering.astype(WIDE), norms[0:1], norms[0:1])
+            vectors[0:1] = jnp.sum(refs.sum[...] * unit, axis=0, keepdims=True)
+            vectors[2:3] = jnp.sum(refs.sum[...], axis=0, keepdims=True)
+            refs.leaving_grads[layer] = refs.grad_middle[...] + norm_back(
+                refs.sum[...], unit, inverse, norms[0:1]
+            )
+            ends.give(layer, refs.leaving_grads.at[layer], sends, copies)
+            phase.finish()
+
+        tail = SimpleNamespace(
+            part=refs.vector_part,
+            from_sibling=refs.vector_from_sibling,
+            from_across=refs.vector_from_across,
+            from_behind=refs.vector_from_behind,
+            total=refs.vector_total,
+            sibling_sems=refs.vector_sibling_sems,
+            across_sems=refs.vector_across_sems,
+            behind_sems=refs.vector_behind_sems,
+        )
+        tail.part[...] = jnp.zeros_like(tail.part)
+        for layer in (0, 1):
+            own = [refs.head_sums[layer]]
+            for at in range(unit_lines):
+                own.append(refs.unit_sums[layer, :, at * HD : (at + 1) * HD])
+            own.append(jnp.zeros((HEAD_LINES - 2 - unit_lines, HD), WIDE))
+            own = jnp.concatenate(own, axis=0)
+            for z in range(levels):
+                for y in (0, 1):
+                    base = (z * 4 + layer * 2 + y) * vector_lines
+                    for x in (0, 1):
+                        cut = (z * 4 + x * 2 + y) * HD
+                        line = base + x * HEAD_LINES
+                        tail.part[line : line + HEAD_LINES] = refs.vectors[layer, :, cut : cut + HD]
+                start = (z * 4 + layer * 2 + plane.y) * vector_lines
+                start = start + (2 + plane.member) * HEAD_LINES
+                tail.part[pl.ds(pl.multiple_of(start, HEAD_LINES), HEAD_LINES)] = own
+        phase = Sends(refs.phase_sems)
+        Scatter(plane, phase, tail, refs.vector_sum).run(lambda step, zz: None, back.tick)
+        phase.start(True, refs.vector_sum, refs.vector_other, refs.pair_sem.at[0], plane.over)
+        await_block(refs.vector_other, refs.pair_sem.at[0], plane.over)
+        refs.vector_out[...] = refs.vector_sum[...] + refs.vector_other[...]
+        acts.finish()
+        back.finish()
+        ends.finish()
+        phase.finish()
+
+    lasting = Return.count(levels)
+    outward = Outward.count()
+    vector = scatter_scratch(vector_lines, HD, levels, 1, WIDE)
+    return launch(
+        "backward_planes",
+        ident,
+        kernel,
+        (
+            lasting[0] + 2 * outward[0],
+            Gather.count(levels, CHUNKS) + Scatter.count(levels, SUM_CHUNKS),
+            lasting[1] + 2 * outward[1] + 2 * 13 + 1,
+        ),
+        dict(
+            planes=(kept.planes, VMEM),
+            leaving=(kept.leaving, VMEM),
+            middle=(kept.middle, VMEM),
+            norms=(kept.norms, VMEM),
+            query_segment=(segments[0], VMEM),
+            key_segment=(segments[1], VMEM),
+            all_queries=(kept.queries, HBM),
+            all_keys=(kept.keys, HBM),
+            all_values=(kept.values, HBM),
+            all_mixed=(kept.mixed, HBM),
+            all_totals=(kept.log_total, HBM),
+            gathered=(kept.gathered, HBM),
+            rows_a=(kept.rows_a, HBM),
+            rows_b=(kept.rows_b, HBM),
+            preact=(kept.preact, HBM),
+            activated=(kept.activated, HBM),
+            out0=(kept.out0, HBM),
+            out1=(kept.out1, HBM),
+            out2=(kept.out2, HBM),
+            out3=(kept.out3, HBM),
+        ),
+        dict(
+            acts=((2, rows, width), LOW, HBM),
+            input_grads=((2, rows, width), WIDE, HBM),
+            shard0=(shard_shapes[0], LOW, HBM),
+            shard1=(shard_shapes[1], LOW, HBM),
+            shard2=(shard_shapes[2], LOW, HBM),
+            shard3=(shard_shapes[3], LOW, HBM),
+            vector_out=((vector_lines, HD), WIDE, VMEM),
+        ),
+        dict(
+            scatter_scratch(rows, width, levels, SUM_CHUNKS),
+            rows=VMEM((2, tokens, width), LOW),
+            gather_sems=DMAS((2, blocks, CHUNKS)),
+            w0=VMEM(slice_shapes[0], LOW),
+            w1=VMEM(slice_shapes[1], LOW),
+            w2=VMEM(slice_shapes[2], LOW),
+            w3=VMEM(slice_shapes[3], LOW),
+            own_preact=VMEM((tokens, units), WIDE),
+            own_activated=VMEM((tokens, units), LOW),
+            own_rows=VMEM((tokens, width), LOW),
+            grad_pre=VMEM((tokens, units), LOW),
+            grad_proj=VMEM((tokens, 3 * HD), LOW),
+            queries=VMEM((tokens, HD), LOW),
+            keys=VMEM((tokens, HD), LOW),
+            values=VMEM((tokens, HD), LOW),
+            mixed=VMEM((tokens, HD), LOW),
+            log_total=VMEM((tokens, 1), WIDE),
+            grad_keys=VMEM((tokens, HD), WIDE),
+            grad_values=VMEM((tokens, HD), WIDE),
+            grad_middle=VMEM((rows, width), WIDE),
+            leaving_grads=VMEM((2, rows, width), WIDE),
+            grad0=VMEM(slice_shapes[0], LOW),
+            grad1=VMEM(slice_shapes[1], LOW),
+            grad2=VMEM(slice_shapes[2], LOW),
+            grad3=VMEM(slice_shapes[3], LOW),
+            landed0=landing(0),
+            landed1=landing(1),
+            landed2=landing(2),
+            landed3=landing(3),
+            column_sems=DMAS((4, 2, levels)),
+            cross_sems=DMAS((4, 2, levels)),
+            acts_sems=DMAS((2,)),
+            ends_sems=DMAS((2,)),
+            pair_sem=DMAS((1,)),
+            vectors=VMEM((2, HEAD_LINES, width), WIDE),
+            head_sums=VMEM((2, 2, HD), WIDE),
+            unit_sums=VMEM((2, 1, units), WIDE),
+            vector_part=vector["part"],
+            vector_from_sibling=vector["from_sibling"],
+            vector_from_across=vector["from_across"],
+            vector_from_behind=vector["from_behind"],
+            vector_total=vector["total"],
+            vector_sum=vector["sum"],
+            vector_other=VMEM((vector_lines, HD), WIDE),
+            vector_sibling_sems=vector["sibling_sems"],
+            vector_across_sems=vector["across_sems"],
+            vector_behind_sems=vector["behind_sems"],
+        ),
+    )
+
+
+def plane_body(
+    boundary,
+    doc_lengths,
+    qkv_weight,
+    qv_bias,
+    out_weight,
+    up_weight,
+    up_bias,
+    down_weight,
+    norm_gains,
+    norm_biases,
+):
+    plane = Plane()
+    levels = plane.levels
+    members = 2 * levels
+    head_cut = qv_bias.shape[3]
+    block_shard = up_bias.shape[1]
+    own_blocks = block_shard // members
+
+    def lines(piece):
+        return piece.reshape(-1, HD)
+
+    packed = jnp.concatenate(
+        (
+            lines(norm_gains[0]),
+            lines(norm_biases[0]),
+            jnp.zeros((HEAD_LINES - NORM_LINES, HD), LOW),
+            lines(qv_bias[0]),
+            lines(up_bias[0]),
+            jnp.zeros((LINES - HEAD_LINES - 2 - up_bias[0].size // HD, HD), LOW),
+        )
+    )
+    depth = qkv_weight.shape[1]
+    by_head = (
+        qkv_weight[0]
+        .reshape(depth, 3, members, HD)
+        .transpose(0, 2, 1, 3)
+        .reshape(depth, members * 3 * HD)
+    )
+    lengths = lax.dynamic_index_in_dim(doc_lengths, plane.x, 0, keepdims=False)
+    tokens = boundary.shape[2] * 4 * levels
+    _, segment, live, _, _, _ = visibility(lengths, 0, tokens, tokens)
+    segments = (jnp.where(live, segment, -1)[:, None], segment[None, :])
+
+    kept = forward_planes(
+        0, boundary[0], packed, segments, (by_head, out_weight[0], up_weight[0], down_weight[0])
+    )
+    end = backward_planes(1, kept, segments)
+
+    summed = end.vector_out.reshape(2 + members, HEAD_LINES, HD)
+    norms = lax.dynamic_index_in_dim(summed, plane.x, 0, keepdims=False)
+    by_member = lax.dynamic_slice_in_dim(
+        summed[2:], (plane.z * 2 + plane.x) * head_cut, head_cut, axis=2
+    )
+    qkv_shard = (
+        end.shard0.reshape(depth, members, 3, HD)
+        .transpose(0, 2, 1, 3)
+        .reshape(depth, 3, members * HD)
+    )
+    return (
+        end.acts[None],
+        end.input_grads[None],
+        qkv_shard.astype(WIDE)[None],
+        by_member[:, :2].transpose(1, 0, 2)[None],
+        end.shard1.astype(WIDE)[None],
+        end.shard2.astype(WIDE)[None],
+        by_member[:, 2 : 2 + own_blocks].reshape(1, block_shard, head_cut),
+        end.shard3.astype(WIDE)[None],
+        norms[None, :2],
+        norms[None, 2:NORM_LINES],
+    )
+
+
+def fits_plane(mesh):
+    return mesh.shape["dp"] == 8 and mesh.shape["tensor"] == 2 and mesh.shape["section"] == 2
+
+
 def solution(mesh):
     placed = (
         P("section", None, ("dp", "tensor"), None),
@@ -467,7 +1734,7 @@
         P("section", None, ("dp", "tensor")),
     )
     return jax.shard_map(
-        body,
+        plane_body if fits_plane(mesh) else body,
         mesh=mesh,
         in_specs=placed,
         out_specs=(

time: 3180 us -> 755 us (0.24)
  waiting for transfers between devices: 2330 us -> 0 us
  Pallas kernels: 0 us -> 715 us
  matrix products: 314 us -> 0 us
  blocking collectives: 246 us -> 0 us
  local copies, waits for them, and re-layouts: 157 us -> 21.1 us
  other arithmetic: 96 us -> 9.23 us
    reduce_scatter x22 -> x0, waiting for transfers between devices: 1320 us -> none  [the longest x1 283 us: reduce_grads(): lax.psum_scatter(up_grad[None].astype(jnp.bfloat16), 'dp', scatter_dimens...]
    all_gather x10 -> x0, waiting for transfers between devices: 791 us -> none  [the longest x1 217 us: fetch_weights(): lax.all_gather(down_weight[0], 'dp', axis=1, tiled=True)]
    pallas_call x0 -> x2, Pallas kernels: none -> 715 us  [launch(): pl.pallas_call(body, out_shape=[jax.ShapeDtypeStruct(shape, dtype) for sh...]
    dot_general x70 -> x0, matrix products: 314 us -> none  [the longest x3 43.4 us: backward(): jnp.einsum('rd,fd->rf', wide_branch, w_down, preferred_element_type=jnp.f...]
    all_gather x16 -> x0, blocking collectives: 246 us -> none  [the longest x12 105 us: widen(): return lax.all_gather(rows_low, 'tensor', axis=0, tiled=True)]
    unnamed x40 -> x0, waiting for transfers between devices: 221 us -> none
    unnamed x451 -> x19, local copies, waits for them, and re-layouts: 86.9 us -> 9.87 us
    reduce_sum x32 -> x0, other arithmetic: 35.9 us -> none  [the longest x3 6.51 us: backward(): out_bias_grad = jnp.sum(grad_attn.astype(jnp.float32), axis=0)]
  transfers between devices with their start and end apart: 40 -> 0, of which waited for: 33 -> 0; matrix products, arithmetic and copies ran while one was open for 8% -> 0% of each run, Pallas kernels for 0% -> 0%
where the time goes in v3:
time: 755 us; the launch traced here: 746 us
  Pallas kernels  715 us (95%)
  local copies, waits for them, and re-layouts  21.1 us (3%)
  other arithmetic  9.23 us (1%)
    pallas_call x2, Pallas kernels, launch(): pl.pallas_call(body, out_shape=[jax.ShapeDtypeStruct(shape, dtype) for sh...  715 us

profile of v3, /device:TPU:0, one launch (start us, length us, event | category | flops | bytes accessed | tf_op | source)
XLA Modules:
  0.0 745.8 jit_solution(281148108182270210)
XLA Ops:
  0.7 0.6 copy-done
  1.5 0.8 reshape_squeeze.9
  2.3 0.8 copy.32
  3.2 1.9 concatenate.3.refs_1_
  5.6 0.6 fusion.15.refs_3_.refs_5_
  6.4 1.0 fusion.5.refs_2_.refs_4_
  7.4 1.7 copy.34
  9.3 1.7 copy.36.refs_4_
  11.0 396.7 %forward_planes.1 = (bf16[2,64,2048]{2,1,0:T(8,128)(2,1)}, bf16[2,64,2048]{2,1,0:T(8,128)(2,1)}, f32[2,64,2048]{2,1,0:T(8,128)}, f32[2,8,2048]{2,1,0:T(8,128)}, ...) custom-call(bf16[2,64,2048]{2,1,0:T(8,128)(2,1)} %bitcast.48, ...), custom_call_target="tpu_custom_call" | custom-call | tf_op jit(solution)/shard_map/forward_planes/pallas_call | solution.py:1020
  407.7 317.8 %backward_planes.1 = (bf16[2,64,2048]{2,1,0:T(8,128)(2,1)}, f32[2,64,2048]{2,1,0:T(8,128)}, bf16[256,3072]{1,0:T(8,128)(2,1)}, bf16[1024,256]{1,0:T(8,128)(2,1)}...) custom-call(bf16[2,64,2048]{2,1,0:T(8,128)(2,1)} %get-tuple-element.35.refs_0_, ...), custom_call_target="tpu_custom_call" | custom-call | tf_op jit(solution)/shard_map/backward_planes/pallas_call | solution.py:1020
  725.5 0.7 constant_dynamic-slice_fusion.1
  726.2 0.6 slice.28
  726.8 0.6 slice.29
  727.4 0.8 slice_bitcast_fusion
  728.3 0.7 copy.42
  729.0 0.6 copy.47
  729.5 2.1 bitcast_convert_fusion.2
  731.6 1.7 copy.37
  733.3 1.9 copy.38
  735.3 3.7 copy.41
  739.0 2.5 bitcast_convert_fusion.1
  741.5 2.3 bitcast_convert_fusion
  743.8 0.8 copy.50
  744.6 1.0 copy.51
  (22 shorter events, 1.3 us)
Async XLA Ops:
  0.6 0.7 copy-start
  735.3 3.7 copy-start.3
  739.0 2.5 copy-start.2
  741.5 2.4 copy-start.5
  741.5 3.1 copy-start.4
  741.5 4.1 copy-start.1

commit v4 on v3

--- a/solution.py
+++ b/solution.py
@@ -641,8 +641,8 @@
                 self.sends.start(can_go, held, held, arrived, plane.along(onward))
                 self.sends.start(True, held, held, arrived, plane.across)
                 self.sends.start(True, held, held, arrived, plane.sibling)
+            tick()
             complete(step - 1)
-            tick()
         complete(plane.levels - 1)
         tick()
 
@@ -801,44 +801,60 @@
     return (rows // shards, columns * shards)
 
 
+FETCHES = (
+    ((0, 0), (0, 2), (0, 2), (0, 0)),
+    ((0, 1), (0, 1), (2, 1), (2, 1), (0, 0), (0, 0), (0, 1), (0, 1)),
+    ((0, 1), (0, 1), (2, 0), (2, 0), (0, 0), (0, 1), (2, 1), (2, 2)),
+    ((0, 1), (0, 1), (2, 1), (2, 1), (0, 0), (0, 0), (0, 2), (0, 1)),
+    ((0, 1), (0, 0), (0, 0), (0, 0), (0, 0), (0, 0), (0, 0), (0, 0)),
+)
+ADDS = (
+    (0, 0, 1, 2),
+    (0, 0, 2, 3, 0, 0, 0, 0),
+    (2, 2, 2, 2, 0, 0, 1, 1),
+    (0, 1, 2, 3, 0, 0, 0, 2),
+    (2, 1, 1, 1),
+)
+
+
 class Fetch:
     UNITS = ((0, (0, 1)), (0, (2,)), (0, (3,)), (1, (0, 1)), (1, (2,)), (1, (3,)))
-    LAG = 4
 
     def __init__(self, plane, shards, slices, refs, sends, copies):
         self.plane, self.shards, self.slices = (plane, shards, slices)
         self.refs, self.sends, self.copies = (refs, sends, copies)
-        acts = []
+        self.spreads = []
         for unit in range(len(self.UNITS)):
             for step in range(plane.levels - 1, -1, -1):
-                acts.append((unit, step))
-        self.moments = []
-        for at in range(len(acts) + self.LAG):
-            moment = []
-            if at < len(acts):
-                moment.append((self.spread,) + acts[at])
-            if at >= self.LAG:
-                moment.append((self.hand_over,) + acts[at - self.LAG])
-            self.moments.append(moment)
+                self.spreads.append((unit, step))
+        self.hands = list(self.spreads)
         self.left = [plane.levels] * len(self.UNITS)
         self.kept = [[] for _ in self.UNITS]
+        self.plan = [moment for stage in FETCHES for moment in stage]
 
     @staticmethod
     def count(levels):
         return 4 * 2 * (3 * levels), 4 * 2 + 8
 
-    def tick(self, times=1):
-        for _ in range(times):
-            if self.moments:
-                for act, unit, step in self.moments.pop(0):
-                    for which in self.UNITS[unit][1]:
-                        act(unit, which, step)
-                    if act == self.hand_over:
-                        self.left[unit] -= 1
+    def tick(self):
+        self.start(*self.plan.pop(0))
+
+    def start(self, spreads, hands):
+        for _ in range(spreads):
+            if self.spreads:
+                unit, step = self.spreads.pop(0)
+                for which in self.UNITS[unit][1]:
+                    self.spread(unit, which, step)
+        for _ in range(hands):
+            if len(self.hands) > len(self.spreads):
+                unit, step = self.hands.pop(0)
+                for which in self.UNITS[unit][1]:
+                    self.hand_over(unit, which, step)
+                self.left[unit] -= 1
 
     def require(self, unit):
         while self.left[unit]:
-            self.tick()
+            self.start(0, 1) if len(self.hands) > len(self.spreads) else self.start(1, 0)
         plane, refs = (self.plane, self.refs)
         layer, weights = self.UNITS[unit]
         for which in weights:
@@ -895,14 +911,14 @@
         self.plane, self.slices, self.landed, self.shards = (plane, slices, landed, shards)
         self.refs, self.sends, self.copies = (refs, sends, copies)
         self.moments, self.left, self.given = ([], {}, {})
+        self.plan = [count for stage in ADDS for count in stage]
 
     @staticmethod
     def count(levels):
         return 4 * 2 * (2 * levels), 4 * 2
 
-    def give(self, layer, which, lag=0):
+    def give(self, layer, which):
         plane = self.plane
-        self.moments.extend([None] * lag)
         self.left[layer, which], self.given[layer, which] = (plane.levels, [])
         for step in range(plane.levels - 1, -1, -1):
             zz = lax.rem(plane.z + step, plane.levels)
@@ -916,17 +932,19 @@
             self.given[layer, which].append(number)
             self.moments.append((layer, which, step))
 
-    def tick(self, times=1):
-        for _ in range(times):
+    def tick(self):
+        self.start(self.plan.pop(0))
+
+    def start(self, adds):
+        for _ in range(adds):
             if self.moments:
                 moment = self.moments.pop(0)
-                if moment is not None:
-                    self.add(*moment)
-                    self.left[moment[:2]] -= 1
+                self.add(*moment)
+                self.left[moment[:2]] -= 1
 
     def require(self, layer, which):
         while self.left[layer, which]:
-            self.tick()
+            self.start(1)
         self.sends.wait(*self.given[layer, which])
 
     def add(self, layer, which, step):
@@ -950,8 +968,7 @@
             self.copies.start(held, target, here)
 
     def finish(self):
-        while self.moments:
-            self.tick()
+        self.start(len(self.moments))
         plane, refs = (self.plane, self.refs)
         members = 2 * plane.levels
         for which in range(4):
@@ -1120,12 +1137,13 @@
             ):
                 phase.start(present, source, target, arrived, partner)
             inward.append(copies.start(source, target, (x == core) & (slot == x)))
-        fetch.tick(levels)
+        fetch.start(levels, 0)
         other_small = refs.small.at[span(plane.block * 2 + 1 - x, LINES)]
         await_block(other_small, refs.pair_sem.at[0], plane.over)
         small = Gather(plane, phase, refs.small, refs.small_sems)
         small.open()
         small.run(lambda step, zz: None, lambda: None)
+        fetch.start(levels, 0)
         for slot in (0, 1):
             here = (core == x) & (core == slot)
             guarded(
@@ -1413,12 +1431,11 @@
                     if layer == 0:
                         back.require(1, 3)
                         back.require(1, 2)
+                    lax.fori_loop(0, units // 128, down_product, 0)
+                    back.give(layer, 3)
                 if at == 1:
-                    lax.fori_loop(0, units // 128, down_product, 0)
-                    back.give(layer, 3, lag=1)
+                    lax.fori_loop(0, width // 512, up_product, 0)
                 if at == 2:
-                    lax.fori_loop(0, width // 512, up_product, 0)
-                if at == 3:
                     lax.fori_loop(width // 512, width // 256, up_product, 0)
                     back.give(layer, 2)
 
@@ -1490,7 +1507,7 @@
                         back.require(1, 0)
                 if at == 1:
                     refs.grad1[...] = dot_rows(refs.mixed[...], held[...]).astype(LOW)
-                    back.give(layer, 1, lag=layer)
+                    back.give(layer, 1)
                     lax.fori_loop(0, width // 1024, qkv_product, 0)
                 if at == 2:
                     lax.fori_loop(width // 1024, width // 512, qkv_product, 0)

time: 755 us -> 715 us (0.947)
  Pallas kernels: 715 us -> 675 us
    pallas_call x2, Pallas kernels: 715 us -> 675 us  [launch(): pl.pallas_call(body, out_shape=[jax.ShapeDtypeStruct(shape, dtype) for sh...]
where the time goes in v4:
time: 715 us; the launch traced here: 706 us
  Pallas kernels  675 us (94%)
  local copies, waits for them, and re-layouts  21.1 us (3%)
  other arithmetic  9.23 us (1%)
    pallas_call x2, Pallas kernels, launch(): pl.pallas_call(body, out_shape=[jax.ShapeDtypeStruct(shape, dtype) for sh...  675 us

profile of v4, /device:TPU:0, one launch (start us, length us, event | category | flops | bytes accessed | tf_op | source)
XLA Modules:
  0.0 706.5 jit_solution(5793048691257380604)
XLA Ops:
  0.7 0.6 copy-done
  1.5 0.8 reshape_squeeze.9
  2.3 0.8 copy.32
  3.2 1.9 concatenate.3.refs_1_
  5.6 0.6 fusion.15.refs_3_.refs_5_
  6.4 1.0 fusion.5.refs_2_.refs_4_
  7.4 1.7 copy.34
  9.3 1.7 copy.36.refs_4_
  11.0 378.7 %forward_planes.1 = (bf16[2,64,2048]{2,1,0:T(8,128)(2,1)}, bf16[2,64,2048]{2,1,0:T(8,128)(2,1)}, f32[2,64,2048]{2,1,0:T(8,128)}, f32[2,8,2048]{2,1,0:T(8,128)}, ...) custom-call(bf16[2,64,2048]{2,1,0:T(8,128)(2,1)} %bitcast.48, ...), custom_call_target="tpu_custom_call" | custom-call | tf_op jit(solution)/shard_map/forward_planes/pallas_call | solution.py:1037
  389.7 296.4 %backward_planes.1 = (bf16[2,64,2048]{2,1,0:T(8,128)(2,1)}, f32[2,64,2048]{2,1,0:T(8,128)}, bf16[256,3072]{1,0:T(8,128)(2,1)}, bf16[1024,256]{1,0:T(8,128)(2,1)}...) custom-call(bf16[2,64,2048]{2,1,0:T(8,128)(2,1)} %get-tuple-element.35.refs_0_, ...), custom_call_target="tpu_custom_call" | custom-call | tf_op jit(solution)/shard_map/backward_planes/pallas_call | solution.py:1037
  686.2 0.7 constant_dynamic-slice_fusion.1
  686.9 0.6 slice.28
  687.4 0.6 slice.29
  688.0 0.8 slice_bitcast_fusion
  688.9 0.7 copy.42
  689.6 0.6 copy.47
  690.2 2.1 bitcast_convert_fusion.2
  692.3 1.7 copy.37
  694.0 1.9 copy.38
  695.9 3.7 copy.41
  699.6 2.5 bitcast_convert_fusion.1
  702.1 2.3 bitcast_convert_fusion
  704.5 0.8 copy.50
  705.3 1.0 copy.51
  (22 shorter events, 1.3 us)
Async XLA Ops:
  0.6 0.7 copy-start
  695.9 3.7 copy-start.3
  699.6 2.5 copy-start.2
  702.1 2.4 copy-start.5
  702.1 3.1 copy-start.4
  702.1 4.1 copy-start.1

commit v5 on v4

--- a/solution.py
+++ b/solution.py
@@ -802,8 +802,8 @@
 
 
 FETCHES = (
-    ((0, 0), (0, 2), (0, 2), (0, 0)),
-    ((0, 1), (0, 1), (2, 1), (2, 1), (0, 0), (0, 0), (0, 1), (0, 1)),
+    ((0, 0), (2, 0), (2, 2), (0, 2)),
+    ((0, 0), (0, 1), (2, 1), (2, 1), (0, 0), (0, 1), (0, 1), (0, 1)),
     ((0, 1), (0, 1), (2, 0), (2, 0), (0, 0), (0, 1), (2, 1), (2, 2)),
     ((0, 1), (0, 1), (2, 1), (2, 1), (0, 0), (0, 0), (0, 2), (0, 1)),
     ((0, 1), (0, 0), (0, 0), (0, 0), (0, 0), (0, 0), (0, 0), (0, 0)),
@@ -812,8 +812,8 @@
     (0, 0, 1, 2),
     (0, 0, 2, 3, 0, 0, 0, 0),
     (2, 2, 2, 2, 0, 0, 1, 1),
-    (0, 1, 2, 3, 0, 0, 0, 2),
-    (2, 1, 1, 1),
+    (0, 1, 2, 3, 0, 2, 2, 2),
+    (1, 1, 0, 0),
 )
 
 
@@ -1137,7 +1137,6 @@
             ):
                 phase.start(present, source, target, arrived, partner)
             inward.append(copies.start(source, target, (x == core) & (slot == x)))
-        fetch.start(levels, 0)
         other_small = refs.small.at[span(plane.block * 2 + 1 - x, LINES)]
         await_block(other_small, refs.pair_sem.at[0], plane.over)
         small = Gather(plane, phase, refs.small, refs.small_sems)
@@ -1505,13 +1504,12 @@
                     if layer == 0:
                         back.require(1, 1)
                         back.require(1, 0)
-                if at == 1:
+                if at == (1 if layer else 0):
                     refs.grad1[...] = dot_rows(refs.mixed[...], held[...]).astype(LOW)
                     back.give(layer, 1)
-                    lax.fori_loop(0, width // 1024, qkv_product, 0)
-                if at == 2:
-                    lax.fori_loop(width // 1024, width // 512, qkv_product, 0)
-                if at == 3:
+                if at == (2 if layer else 0):
+                    lax.fori_loop(0, width // 512, qkv_product, 0)
+                if at == (3 if layer else 0):
                     lax.fori_loop(width // 512, width // 256, qkv_product, 0)
                     back.give(layer, 0)
 

time: 715 us -> 698 us (0.976)
  Pallas kernels: 675 us -> 658 us
    pallas_call x2, Pallas kernels: 675 us -> 658 us  [launch(): pl.pallas_call(body, out_shape=[jax.ShapeDtypeStruct(shape, dtype) for sh...]
where the time goes in v5:
time: 698 us; the launch traced here: 689 us
  Pallas kernels  658 us (94%)
  local copies, waits for them, and re-layouts  21.1 us (3%)
  other arithmetic  9.23 us (1%)
    pallas_call x2, Pallas kernels, launch(): pl.pallas_call(body, out_shape=[jax.ShapeDtypeStruct(shape, dtype) for sh...  658 us

profile of v5, /device:TPU:0, one launch (start us, length us, event | category | flops | bytes accessed | tf_op | source)
XLA Modules:
  0.0 689.0 jit_solution(17011781037364223784)
XLA Ops:
  0.7 0.6 copy-done
  1.5 0.8 reshape_squeeze.9
  2.3 0.8 copy.32
  3.2 1.9 concatenate.3.refs_1_
  5.6 0.6 fusion.15.refs_3_.refs_5_
  6.4 1.0 fusion.5.refs_2_.refs_4_
  7.4 1.7 copy.34
  9.3 1.7 copy.36.refs_4_
  11.0 361.6 %forward_planes.1 = (bf16[2,64,2048]{2,1,0:T(8,128)(2,1)}, bf16[2,64,2048]{2,1,0:T(8,128)(2,1)}, f32[2,64,2048]{2,1,0:T(8,128)}, f32[2,8,2048]{2,1,0:T(8,128)}, ...) custom-call(bf16[2,64,2048]{2,1,0:T(8,128)(2,1)} %bitcast.48, ...), custom_call_target="tpu_custom_call" | custom-call | tf_op jit(solution)/shard_map/forward_planes/pallas_call | solution.py:1037
  372.6 296.1 %backward_planes.1 = (bf16[2,64,2048]{2,1,0:T(8,128)(2,1)}, f32[2,64,2048]{2,1,0:T(8,128)}, bf16[256,3072]{1,0:T(8,128)(2,1)}, bf16[1024,256]{1,0:T(8,128)(2,1)}...) custom-call(bf16[2,64,2048]{2,1,0:T(8,128)(2,1)} %get-tuple-element.35.refs_0_, ...), custom_call_target="tpu_custom_call" | custom-call | tf_op jit(solution)/shard_map/backward_planes/pallas_call | solution.py:1037
  668.7 0.7 constant_dynamic-slice_fusion.1
  669.4 0.6 slice.28
  670.0 0.6 slice.29
  670.5 0.8 slice_bitcast_fusion
  671.4 0.7 copy.42
  672.1 0.6 copy.47
  672.7 2.1 bitcast_convert_fusion.2
  674.8 1.7 copy.37
  676.5 1.9 copy.38
  678.5 3.7 copy.41
  682.2 2.5 bitcast_convert_fusion.1
  684.7 2.3 bitcast_convert_fusion
  687.0 0.8 copy.50
  687.8 1.0 copy.51
  (22 shorter events, 1.3 us)
Async XLA Ops:
  0.6 0.7 copy-start
  678.5 3.7 copy-start.3
  682.2 2.5 copy-start.2
  684.7 2.4 copy-start.5
  684.7 3.1 copy-start.4
  684.7 4.1 copy-start.1

commit v6 on v5

--- a/solution.py
+++ b/solution.py
@@ -776,6 +776,8 @@
 
 
 def piece_of_shard(which, ref, member, members):
+    if which == 0:
+        return ref.at[:, :, span(member, ref.shape[2] // members)]
     if by_rows(which):
         return ref.at[span(member, ref.shape[0] // members)]
     return ref.at[:, span(member, ref.shape[1] // members)]
@@ -787,7 +789,18 @@
     return ref.at[span(shard, ref.shape[0] // shards)]
 
 
+def matched(which, of_shard, of_slice):
+    if which:
+        return [(of_shard, of_slice)]
+    kinds, _, depth = of_shard.shape
+    return [
+        (of_shard.at[kind], of_slice.at[:, pl.ds(kind * depth, depth)]) for kind in range(kinds)
+    ]
+
+
 def slice_shape(which, shape, shards):
+    if which == 0:
+        return (shape[1] * shards, shape[0] * shape[2] // shards)
     rows, columns = shape
     if by_rows(which):
         return (rows // shards, columns * shards)
@@ -796,6 +809,8 @@
 
 def shard_shape(which, shape, shards):
     rows, columns = shape
+    if which == 0:
+        return (3, rows // shards, columns * shards // 3)
     if by_rows(which):
         return (rows * shards, columns // shards)
     return (rows // shards, columns * shards)
@@ -834,7 +849,7 @@
 
     @staticmethod
     def count(levels):
-        return 4 * 2 * (3 * levels), 4 * 2 + 8
+        return 4 * 2 * (3 * levels) + 8 * levels, 4 * 2 + 8 + 4
 
     def tick(self):
         self.start(*self.plan.pop(0))
@@ -875,17 +890,18 @@
         zz = lax.rem(plane.z + step, plane.levels)
         for other in (0, 1):
             core = 1 - plane.core if other else plane.core
-            source = piece_of_shard(which, shard, zz * 2 + core, members)
-            if step or other:
-                self.sends.start(
-                    owner,
-                    source,
-                    target,
-                    refs.column_sems.at[which, layer, plane.z],
-                    device(core, zz, plane.x, plane.y),
-                )
-            else:
-                self.kept[unit].append(self.copies.start(source, target, owner))
+            piece = piece_of_shard(which, shard, zz * 2 + core, members)
+            for source, landing in matched(which, piece, target):
+                if step or other:
+                    self.sends.start(
+                        owner,
+                        source,
+                        landing,
+                        refs.column_sems.at[which, layer, plane.z],
+                        device(core, zz, plane.x, plane.y),
+                    )
+                else:
+                    self.kept[unit].append(self.copies.start(source, landing, owner))
 
     def hand_over(self, unit, which, step):
         plane, refs, layer = (self.plane, self.refs, self.UNITS[unit][0])
@@ -903,7 +919,8 @@
             source = piece_of_shard(which, shard, plane.member, members)
             guarded(jnp.logical_not(owner), partial(await_block, held, arrived, plane.over))
             self.sends.start(jnp.logical_not(owner), held, held, cross, plane.over)
-            self.sends.start(owner, source, held, cross, plane.over)
+            for end, landing in matched(which, source, held):
+                self.sends.start(owner, end, landing, cross, plane.over)
 
 
 class Return:
@@ -915,7 +932,7 @@
 
     @staticmethod
     def count(levels):
-        return 4 * 2 * (2 * levels), 4 * 2
+        return 4 * 2 * (2 * levels) + 4 * levels, 4 * 2 + 4
 
     def give(self, layer, which):
         plane = self.plane
@@ -957,15 +974,16 @@
         await_block(held, refs.cross_sems.at[which, layer, zz], plane.over)
         own = piece_of_slice(which, self.slices[which], zz * 2 + plane.x, members)
         held[...] = (held[...].astype(WIDE) + own[...].astype(WIDE)).astype(LOW)
-        self.sends.start(
-            True if step else jnp.logical_not(here),
-            held,
-            target,
-            refs.column_sems.at[which, plane.core, plane.z],
-            device(layer, zz, plane.x, plane.y),
-        )
-        if step == 0:
-            self.copies.start(held, target, here)
+        for landing, source in matched(which, target, held):
+            self.sends.start(
+                True if step else jnp.logical_not(here),
+                source,
+                landing,
+                refs.column_sems.at[which, plane.core, plane.z],
+                device(layer, zz, plane.x, plane.y),
+            )
+            if step == 0:
+                self.copies.start(source, landing, here)
 
     def finish(self):
         self.start(len(self.moments))
@@ -1690,20 +1708,13 @@
             jnp.zeros((LINES - HEAD_LINES - 2 - up_bias[0].size // HD, HD), LOW),
         )
     )
-    depth = qkv_weight.shape[1]
-    by_head = (
-        qkv_weight[0]
-        .reshape(depth, 3, members, HD)
-        .transpose(0, 2, 1, 3)
-        .reshape(depth, members * 3 * HD)
-    )
     lengths = lax.dynamic_index_in_dim(doc_lengths, plane.x, 0, keepdims=False)
     tokens = boundary.shape[2] * 4 * levels
     _, segment, live, _, _, _ = visibility(lengths, 0, tokens, tokens)
     segments = (jnp.where(live, segment, -1)[:, None], segment[None, :])
 
     kept = forward_planes(
-        0, boundary[0], packed, segments, (by_head, out_weight[0], up_weight[0], down_weight[0])
+        0, boundary[0], packed, segments, (qkv_weight[0].transpose(1, 0, 2), out_weight[0], up_weight[0], down_weight[0])
     )
     end = backward_planes(1, kept, segments)
 
@@ -1712,15 +1723,10 @@
     by_member = lax.dynamic_slice_in_dim(
         summed[2:], (plane.z * 2 + plane.x) * head_cut, head_cut, axis=2
     )
-    qkv_shard = (
-        end.shard0.reshape(depth, members, 3, HD)
-        .transpose(0, 2, 1, 3)
-        .reshape(depth, 3, members * HD)
-    )
     return (
         end.acts[None],
         end.input_grads[None],
-        qkv_shard.astype(WIDE)[None],
+        end.shard0.transpose(1, 0, 2).astype(WIDE)[None],
         by_member[:, :2].transpose(1, 0, 2)[None],
         end.shard1.astype(WIDE)[None],
         end.shard2.astype(WIDE)[None],

time: 698 us -> 690 us (0.989)
  local copies, waits for them, and re-layouts: 21.1 us -> 10.2 us
where the time goes in v6:
time: 690 us; the launch traced here: 679 us
  Pallas kernels  655 us (95%)
  other arithmetic  12.8 us (2%)
  local copies, waits for them, and re-layouts  10.2 us (1%)
    pallas_call x2, Pallas kernels, launch(): pl.pallas_call(body, out_shape=[jax.ShapeDtypeStruct(shape, dtype) for sh...  655 us

profile of v6, /device:TPU:0, one launch (start us, length us, event | category | flops | bytes accessed | tf_op | source)
XLA Modules:
  0.0 678.6 jit_solution(1992246716904346524)
XLA Ops:
  0.7 0.6 copy-done
  1.3 0.2 reduce_window_sum.11
  1.5 0.8 reshape_squeeze.6
  2.3 0.8 copy.23
  3.1 0.1 reshape_squeeze.7
  3.2 1.9 concatenate.3.refs_1_
  5.1 0.5 broadcast_select_fusion
  5.6 0.6 fusion.15.refs_3_.refs_5_
  6.2 0.2 copy.24
  6.4 1.0 fusion.5.refs_2_.refs_4_
  7.4 362.5 %forward_planes.1 = (bf16[2,64,2048]{2,1,0:T(8,128)(2,1)}, bf16[2,64,2048]{2,1,0:T(8,128)(2,1)}, f32[2,64,2048]{2,1,0:T(8,128)}, f32[2,8,2048]{2,1,0:T(8,128)}, ...) custom-call(bf16[2,64,2048]{2,1,0:T(8,128)(2,1)} %bitcast.44, ...), custom_call_target="tpu_custom_call" | custom-call | tf_op jit(solution)/shard_map/forward_planes/pallas_call | solution.py:1055
  369.9 292.1 %backward_planes.1 = (bf16[2,64,2048]{2,1,0:T(8,128)(2,1)}, f32[2,64,2048]{2,1,0:T(8,128)}, bf16[3,256,1024]{2,1,0:T(8,128)(2,1)}, bf16[1024,256]{1,0:T(8,128)(2...) custom-call(bf16[2,64,2048]{2,1,0:T(8,128)(2,1)} %get-tuple-element.35.refs_0_, ...), custom_call_target="tpu_custom_call" | custom-call | tf_op jit(solution)/shard_map/backward_planes/pallas_call | solution.py:1055
  662.0 0.7 constant_dynamic-slice_fusion.1
  662.7 0.6 slice.28
  663.2 0.6 slice.29
  663.8 0.8 slice_bitcast_fusion
  664.7 0.7 copy.27
  665.4 0.6 copy.32
  666.0 2.2 bitcast_convert_fusion.2
  668.2 3.5 convert_bitcast_fusion
  671.7 2.5 bitcast_convert_fusion.1
  674.2 2.3 bitcast_convert_fusion
  676.6 0.8 copy.35
  677.4 1.0 copy.36
  (17 shorter events, 0.2 us)
Async XLA Ops:
  0.6 0.7 copy-start
  666.0 5.7 copy-start.3
  671.7 2.5 copy-start.2
  674.2 2.4 copy-start.5
  674.2 3.1 copy-start.4
  674.2 4.1 copy-start.1
